TPU v7x, 32 devices: a whole 2x2x4 slice. The times are simulated.
32 devices in a mesh: dp: 8 (over z, x), mp: 4 (over y, core).
Axes of the slice: x: 2, y: 2, z: 4, core: 2. Of those that a mesh axis runs over, the one named last changes fastest.
Arguments:
- inputs: bfloat16 [2, 1024, 1024], P(None, 'dp'), may hold values from -6 to 6
- segment: int32 [2, 1024], P(None, 'dp'), may hold values from 0 to 15, never falling along the last dimension, each value on 1 to 128 neighbouring positions
- norm_gain: bfloat16 [1024], P(('dp', 'mp')), may hold values from 0.5 to 1.5
- w_query: bfloat16 [1024, 512], P('dp', 'mp'), may hold values from -0.1875 to 0.1875
- w_key: bfloat16 [1024, 512], P('dp', 'mp'), may hold values from -0.1875 to 0.1875
- w_value: bfloat16 [1024, 1024], P('dp', 'mp'), may hold values from -0.1875 to 0.1875
- w_gate_out: bfloat16 [1024, 1024], P('dp', 'mp'), may hold values from -0.1875 to 0.1875
- w_rank_in: bfloat16 [1024, 16], P(('dp', 'mp')), may hold values from -0.1875 to 0.1875
- w_rank_out: bfloat16 [512, 16], P(('dp', 'mp')), may hold values from -1.5 to 1.5
- rank_bias: bfloat16 [512], P(('dp', 'mp')), may hold values from -2 to 5
- head_gain: bfloat16 [256], P(('dp', 'mp')), may hold values from 0.5 to 1.5
- w_output: bfloat16 [1024, 1024], P('dp', 'mp'), may hold values from -0.375 to 0.375
- ffn_gain: bfloat16 [1024], P(('dp', 'mp')), may hold values from 0.5 to 1.5
- w_ffn_gate: bfloat16 [1024, 2816], P('dp', 'mp'), may hold values from -0.1875 to 0.1875
- w_ffn_up: bfloat16 [1024, 2816], P('dp', 'mp'), may hold values from -0.1875 to 0.1875
- w_ffn_down: bfloat16 [1024, 2816], P('dp', 'mp'), may hold values from -0.21875 to 0.21875
- cotangent: bfloat16 [2, 1024, 1024], P(None, 'dp'), may hold values from -6 to 6
Outputs:
- output: bfloat16 [2, 1024, 1024], P(None, 'dp')
- input_grad: float32 [2, 1024, 1024], P(None, 'dp')
- grad_norm_gain: float32 [1024], P(('dp', 'mp'))
- grad_w_query: float32 [1024, 512], P('dp', 'mp')
- grad_w_key: float32 [1024, 512], P('dp', 'mp')
- grad_w_value: float32 [1024, 1024], P('dp', 'mp')
- grad_w_gate_out: float32 [1024, 1024], P('dp', 'mp')
- grad_w_rank_in: float32 [1024, 16], P(('dp', 'mp'))
- grad_w_rank_out: float32 [512, 16], P(('dp', 'mp'))
- grad_rank_bias: float32 [512], P(('dp', 'mp'))
- grad_head_gain: float32 [256], P(('dp', 'mp'))
- grad_w_output: float32 [1024, 1024], P('dp', 'mp')
- grad_ffn_gain: float32 [1024], P(('dp', 'mp'))
- grad_w_ffn_gate: float32 [1024, 2816], P('dp', 'mp')
- grad_w_ffn_up: float32 [1024, 2816], P('dp', 'mp')
- grad_w_ffn_down: float32 [1024, 2816], P('dp', 'mp')
Inputs may be any that keep to these rules, and one draw needn't show every extreme that they name: `segment`: along each micro-batch's 1024 tokens the document numbers never fall; every document has 1 to 128 tokens, and some document has exactly 128.
All inputs are finite; a program needn't handle non-finite values.
Results may differ from a plain program's by a relative error of at most 0.02.
Values may be sent and summed in bfloat16 or wider, within the bound.
A program may use at most 128 MiB of HBM per device.

v0:
```python
import jax
import jax.numpy as jnp
from jax import lax
from jax.sharding import PartitionSpec as P

H = 4
SPAN = 64


norm_eps = 1e-06
head_eps = 0.1
gate_divisor = 16.0


def product(left, right):
    return jnp.dot(left, right, precision=lax.Precision.HIGHEST, preferred_element_type=jnp.float32)


def low_dot(left, right):
    return jnp.dot(left, right, preferred_element_type=jnp.float32)


def low_dot_t(left, right):
    return lax.dot_general(
        left, right, (((0,), (0,)), ((), ())), preferred_element_type=jnp.float32
    )


def dot_right_t(left, right):
    return lax.dot_general(
        left, right, (((1,), (1,)), ((), ())), preferred_element_type=jnp.float32
    )


def rms_gain(values, gain):
    return values * lax.rsqrt(jnp.mean(values * values, axis=-1, keepdims=True) + norm_eps) * gain


def gla_core(queries, key_in, values, decays, segment):
    length, width = queries.shape
    value_width = values.shape[1]
    blocks = length // SPAN
    scaling = width ** (-0.5)
    previous = jnp.concatenate([jnp.full((1,), -1, jnp.int32), segment[:-1]])
    prev_block = previous.reshape(blocks, SPAN)[:, 0]
    positions = jnp.arange(SPAN)
    causal_base = positions[:, None] >= positions[None, :]

    def block_step(carry_state, block_items):
        query_blk, key_blk, value_blk, decay_blk, seg_blk, prev_seg = block_items
        cumulative = jnp.cumsum(decay_blk, axis=0)
        causal = causal_base & (seg_blk[:, None] == seg_blk[None, :])
        query_up = query_blk * jnp.exp(cumulative)
        key_down = key_blk * jnp.exp(-cumulative)
        scores = jnp.where(causal, product(query_up, key_down.T), 0.0)
        inner_sum = product(scores, value_blk)
        carried = (seg_blk == prev_seg)[:, None]
        outer_sum = jnp.where(carried, product(query_up, carry_state), 0.0)
        final_log = cumulative[-1]
        weighted = jnp.where(
            (seg_blk == seg_blk[-1])[:, None], key_down * jnp.exp(final_log)[None, :], 0.0
        )
        kept_state = jnp.where(
            seg_blk[-1] == prev_seg, jnp.exp(final_log)[:, None] * carry_state, 0.0
        )
        new_state = kept_state + product(weighted.T, value_blk)
        return (new_state, scaling * (inner_sum + outer_sum))

    start_state = jnp.zeros((width, value_width), jnp.float32)
    block_items = (
        queries.reshape(blocks, SPAN, width),
        key_in.reshape(blocks, SPAN, width),
        values.reshape(blocks, SPAN, value_width),
        decays.reshape(blocks, SPAN, width),
        segment.reshape(blocks, SPAN),
        prev_block,
    )
    final_state, results = lax.scan(jax.checkpoint(block_step), start_state, block_items)
    return results.reshape(length, value_width)


def head_gate(core_out, gate_lin, head_gain):
    normed = (
        core_out
        * lax.rsqrt(jnp.mean(core_out * core_out, axis=-1, keepdims=True) + head_eps)
        * head_gain
    )
    gate_three = gate_lin.reshape(core_out.shape)
    return (normed * gate_three * jax.nn.sigmoid(gate_three)).reshape(gate_lin.shape)


def core_heads(queries, key_in, values, decay_in, doc_ids):
    mapped = jax.vmap(gla_core, in_axes=(1, 1, 1, 1, None), out_axes=1)
    return mapped(queries, key_in, values, decay_in, doc_ids)


def on_device(
    inputs,
    segment,
    norm_gain,
    w_query,
    w_key,
    w_value,
    w_gate_out,
    w_rank_in,
    w_rank_out,
    rank_bias,
    head_gain,
    w_output,
    ffn_gain,
    w_ffn_gate,
    w_ffn_up,
    w_ffn_down,
    cotangent,
):
    mp_index = lax.axis_index("mp")
    mp_count = lax.axis_size("mp")
    shared = (
        lax.all_gather(norm_gain, ("dp", "mp"), axis=0, tiled=True),
        lax.all_gather(ffn_gain, ("dp", "mp"), axis=0, tiled=True),
        lax.all_gather(head_gain, ("dp", "mp"), axis=0, tiled=True),
        lax.all_gather(w_rank_in, ("dp", "mp"), axis=0, tiled=True),
        lax.all_gather(w_rank_out, ("dp", "mp"), axis=0, tiled=True),
        lax.all_gather(rank_bias, ("dp", "mp"), axis=0, tiled=True),
    )
    gain_in = shared[0].astype(jnp.float32)
    gain_mid = shared[1].astype(jnp.float32)
    gain_head = shared[2].astype(jnp.float32)
    rank_in = shared[3]
    local_keys = w_query.shape[1]
    head_start = mp_index * local_keys
    rank_out = lax.dynamic_slice_in_dim(shared[4], head_start, local_keys, 0)
    bias_local = lax.dynamic_slice_in_dim(shared[5], head_start, local_keys, 0).astype(jnp.float32)
    lead_copy = (mp_index == 0).astype(jnp.float32)
    heads_local = H // mp_count
    dp_count = lax.axis_size("dp")
    locals_list = (w_query, w_key, w_value, w_gate_out, w_output, w_ffn_gate, w_ffn_up, w_ffn_down)
    grad_mats = [
        jnp.zeros((matrix.shape[0] * dp_count, matrix.shape[1]), jnp.float32)
        for matrix in locals_list
    ]
    grad_gain_in = jnp.zeros(gain_in.shape, jnp.float32)
    grad_gain_mid = jnp.zeros(gain_mid.shape, jnp.float32)
    grad_head = jnp.zeros(gain_head.shape, jnp.float32)
    grad_rank_in = jnp.zeros(rank_in.shape, jnp.float32)
    grad_rank_out = jnp.zeros(rank_out.shape, jnp.float32)
    grad_bias = jnp.zeros((local_keys,), jnp.float32)
    outputs_all = []
    input_grads = []
    for micro_step in range(inputs.shape[0]):
        forward_mats = (
            lax.all_gather(w_query, "dp", axis=0, tiled=True),
            lax.all_gather(w_key, "dp", axis=0, tiled=True),
            lax.all_gather(w_value, "dp", axis=0, tiled=True),
            lax.all_gather(w_gate_out, "dp", axis=0, tiled=True),
            lax.all_gather(w_output, "dp", axis=0, tiled=True),
            lax.all_gather(w_ffn_gate, "dp", axis=0, tiled=True),
            lax.all_gather(w_ffn_up, "dp", axis=0, tiled=True),
            lax.all_gather(w_ffn_down, "dp", axis=0, tiled=True),
        )
        (
            full_query,
            full_key,
            full_value,
            full_gate,
            full_output,
            full_ffn_gate,
            full_ffn_up,
            full_ffn_down,
        ) = forward_mats
        tokens = inputs[micro_step].astype(jnp.float32)
        doc_ids = segment[micro_step]
        length = tokens.shape[0]
        normed_in, norm_in_back = jax.vjp(rms_gain, tokens, gain_in)
        normed_low = normed_in.astype(jnp.bfloat16)
        query_low = low_dot(normed_low, full_query).astype(jnp.bfloat16)
        key_low = low_dot(normed_low, full_key).astype(jnp.bfloat16)
        value_low = low_dot(normed_low, full_value).astype(jnp.bfloat16)
        gate_lin = low_dot(normed_low, full_gate)
        rank_low = low_dot(normed_low, rank_in).astype(jnp.bfloat16)
        logits = dot_right_t(rank_low, rank_out) + bias_local
        decays = jax.nn.log_sigmoid(logits) / gate_divisor

        def core_local(queries, key_in, values, decay_in):
            return core_heads(queries, key_in, values, decay_in, doc_ids)

        core_out, core_back = jax.vjp(
            core_local,
            query_low.astype(jnp.float32).reshape(length, heads_local, -1),
            key_low.astype(jnp.float32).reshape(length, heads_local, -1),
            value_low.astype(jnp.float32).reshape(length, heads_local, -1),
            decays.reshape(length, heads_local, -1),
        )
        gated, gate_back = jax.vjp(head_gate, core_out, gate_lin, gain_head)
        gated_low = gated.astype(jnp.bfloat16)
        attended_part = dot_right_t(gated_low, full_output)
        attended = lax.psum(attended_part.astype(jnp.bfloat16), "mp").astype(jnp.float32)
        middle = tokens + attended
        normed_mid, norm_mid_back = jax.vjp(rms_gain, middle, gain_mid)
        mid_low = normed_mid.astype(jnp.bfloat16)
        gate_act = low_dot(mid_low, full_ffn_gate)
        up_act = low_dot(mid_low, full_ffn_up)
        hidden_low = (jax.nn.silu(gate_act) * up_act).astype(jnp.bfloat16)
        ffn_part = dot_right_t(hidden_low, full_ffn_down)
        ffn_out = lax.psum(ffn_part.astype(jnp.bfloat16), "mp").astype(jnp.float32)
        outputs_all.append((middle + ffn_out).astype(jnp.bfloat16))
        back_mats = (
            lax.all_gather(w_query, "dp", axis=0, tiled=True),
            lax.all_gather(w_key, "dp", axis=0, tiled=True),
            lax.all_gather(w_value, "dp", axis=0, tiled=True),
            lax.all_gather(w_gate_out, "dp", axis=0, tiled=True),
            lax.all_gather(w_output, "dp", axis=0, tiled=True),
            lax.all_gather(w_ffn_gate, "dp", axis=0, tiled=True),
            lax.all_gather(w_ffn_up, "dp", axis=0, tiled=True),
            lax.all_gather(w_ffn_down, "dp", axis=0, tiled=True),
        )
        (
            back_query,
            back_key,
            back_value,
            back_gate,
            back_output,
            back_ffn_gate,
            back_ffn_up,
            back_ffn_down,
        ) = back_mats
        grad_low = cotangent[micro_step]
        grad_out = grad_low.astype(jnp.float32)
        grad_mats[7] = grad_mats[7] + low_dot_t(grad_low, hidden_low)
        d_hidden = low_dot(grad_low, back_ffn_down)
        sigma = jax.nn.sigmoid(gate_act)
        d_gate_low = (d_hidden * up_act * sigma * (1.0 + gate_act * (1.0 - sigma))).astype(
            jnp.bfloat16
        )
        d_up_low = (d_hidden * gate_act * sigma).astype(jnp.bfloat16)
        grad_mats[5] = grad_mats[5] + low_dot_t(mid_low, d_gate_low)
        grad_mats[6] = grad_mats[6] + low_dot_t(mid_low, d_up_low)
        d_mid_part = dot_right_t(d_gate_low, back_ffn_gate) + dot_right_t(d_up_low, back_ffn_up)
        d_normed_mid = lax.psum(d_mid_part.astype(jnp.bfloat16), "mp").astype(jnp.float32)
        d_middle_norm, d_gain_mid = norm_mid_back(d_normed_mid)
        grad_gain_mid = grad_gain_mid + lead_copy * d_gain_mid
        d_middle = grad_out + d_middle_norm
        d_att_low = d_middle.astype(jnp.bfloat16)
        grad_mats[4] = grad_mats[4] + low_dot_t(d_att_low, gated_low)
        d_gated = low_dot(d_att_low, back_output)
        d_core, d_gate_lin, d_gain_head = gate_back(d_gated)
        grad_head = grad_head + d_gain_head
        d_lin_low = d_gate_lin.astype(jnp.bfloat16)
        d_queries, d_keys, d_values, d_decays = core_back(d_core)
        d_query_low = d_queries.reshape(length, -1).astype(jnp.bfloat16)
        d_key_low = d_keys.reshape(length, -1).astype(jnp.bfloat16)
        d_value_low = d_values.reshape(length, -1).astype(jnp.bfloat16)
        d_logit_low = (
            d_decays.reshape(length, -1) * jax.nn.sigmoid(-logits) / gate_divisor
        ).astype(jnp.bfloat16)
        grad_rank_out = grad_rank_out + low_dot_t(d_logit_low, rank_low)
        grad_bias = grad_bias + jnp.sum(d_logit_low.astype(jnp.float32), axis=0)
        d_rank_low = low_dot(d_logit_low, rank_out).astype(jnp.bfloat16)
        grad_rank_in = grad_rank_in + low_dot_t(normed_low, d_rank_low)
        grad_mats[0] = grad_mats[0] + low_dot_t(normed_low, d_query_low)
        grad_mats[1] = grad_mats[1] + low_dot_t(normed_low, d_key_low)
        grad_mats[2] = grad_mats[2] + low_dot_t(normed_low, d_value_low)
        grad_mats[3] = grad_mats[3] + low_dot_t(normed_low, d_lin_low)
        d_in_part = (
            dot_right_t(d_query_low, back_query)
            + dot_right_t(d_key_low, back_key)
            + dot_right_t(d_value_low, back_value)
            + dot_right_t(d_lin_low, back_gate)
            + dot_right_t(d_rank_low, rank_in)
        )
        d_normed_in = lax.psum(d_in_part.astype(jnp.bfloat16), "mp").astype(jnp.float32)
        d_tokens_norm, d_gain_in = norm_in_back(d_normed_in)
        grad_gain_in = grad_gain_in + lead_copy * d_gain_in
        input_grads.append(d_middle + d_tokens_norm)
    weight_grads = (
        lax.psum_scatter(grad_mats[0], "dp", scatter_dimension=0, tiled=True),
        lax.psum_scatter(grad_mats[1], "dp", scatter_dimension=0, tiled=True),
        lax.psum_scatter(grad_mats[2], "dp", scatter_dimension=0, tiled=True),
        lax.psum_scatter(grad_mats[3], "dp", scatter_dimension=0, tiled=True),
        lax.psum_scatter(grad_mats[4], "dp", scatter_dimension=0, tiled=True),
        lax.psum_scatter(grad_mats[5], "dp", scatter_dimension=0, tiled=True),
        lax.psum_scatter(grad_mats[6], "dp", scatter_dimension=0, tiled=True),
        lax.psum_scatter(grad_mats[7], "dp", scatter_dimension=0, tiled=True),
    )
    rank_out_full = lax.dynamic_update_slice_in_dim(
        jnp.zeros(shared[4].shape, jnp.float32), grad_rank_out, head_start, 0
    )
    bias_full = lax.dynamic_update_slice_in_dim(
        jnp.zeros(shared[5].shape, jnp.float32), grad_bias, head_start, 0
    )
    small_grads = (
        lax.psum_scatter(grad_gain_in, ("dp", "mp"), scatter_dimension=0, tiled=True),
        lax.psum_scatter(grad_gain_mid, ("dp", "mp"), scatter_dimension=0, tiled=True),
        lax.psum_scatter(grad_head, ("dp", "mp"), scatter_dimension=0, tiled=True),
        lax.psum_scatter(grad_rank_in, ("dp", "mp"), scatter_dimension=0, tiled=True),
        lax.psum_scatter(rank_out_full, ("dp", "mp"), scatter_dimension=0, tiled=True),
        lax.psum_scatter(bias_full, ("dp", "mp"), scatter_dimension=0, tiled=True),
    )
    return (
        jnp.stack(outputs_all),
        jnp.stack(input_grads),
        small_grads[0],
        weight_grads[0],
        weight_grads[1],
        weight_grads[2],
        weight_grads[3],
        small_grads[3],
        small_grads[4],
        small_grads[5],
        small_grads[2],
        weight_grads[4],
        small_grads[1],
        weight_grads[5],
        weight_grads[6],
        weight_grads[7],
    )


def solution(mesh):
    in_specs = (
        P(None, "dp", None),
        P(None, "dp"),
        P(("dp", "mp")),
        P("dp", "mp"),
        P("dp", "mp"),
        P("dp", "mp"),
        P("dp", "mp"),
        P(("dp", "mp"), None),
        P(("dp", "mp"), None),
        P(("dp", "mp")),
        P(("dp", "mp")),
        P("dp", "mp"),
        P(("dp", "mp")),
        P("dp", "mp"),
        P("dp", "mp"),
        P("dp", "mp"),
        P(None, "dp", None),
    )
    out_specs = (
        P(None, "dp", None),
        P(None, "dp", None),
        P(("dp", "mp")),
        P("dp", "mp"),
        P("dp", "mp"),
        P("dp", "mp"),
        P("dp", "mp"),
        P(("dp", "mp"), None),
        P(("dp", "mp"), None),
        P(("dp", "mp")),
        P(("dp", "mp")),
        P("dp", "mp"),
        P(("dp", "mp")),
        P("dp", "mp"),
        P("dp", "mp"),
        P("dp", "mp"),
    )
    return jax.shard_map(
        on_device, mesh=mesh, in_specs=in_specs, out_specs=out_specs, check_vma=False
    )
```

profile of v0, /device:TPU:13, one launch (start us, length us, event | category | flops | bytes accessed | tf_op | source)
XLA Modules:
  0.0 1425.0 jit_solution(3262202542450994889)
XLA Ops:
  9.6 31.8 %all-gather = bf16[32,32,16]{1,2,0:T(8,128)(2,1)S(1)} all-gather(bf16[1,32,16]{1,2,0:T(8,128)(2,1)} %bitcast.941), channel_id=1, replica_groups=mesh['dp'=8,'mp'=4] {'dp','mp'}, dimensions={0}, use_global_device_ids=true | all-gather | bytes 33792 | tf_op jit(solution)/shard_map/all_gather | solution.py:122
  45.0 47.6 %all-reduce.11 = (bf16[1024]{0:T(1024)(128)(2,1)S(1)}, bf16[512]{0:T(512)(128)(2,1)S(1)}, bf16[256]{0:T(256)(128)(2,1)S(1)}, bf16[1024]{0:T(1024)(128)(2,1)S(1)}) all-reduce(bf16[1024]{0:T(1024)(128)(2,1)S(1)} %dynamic-update-slice, bf16[512]{0:T(512)(128)(2,1)S(1)} %dynamic-update-slice.1, ...), channel_id=1, replica_groups=mesh['dp'=8,'mp'=4] {'dp','mp'}, use_global_device_ids=true, to_apply=%add.2 | all-reduce | flops 2816 | bytes 11264
  92.6 1.2 fusion.218
  93.9 20.7 %all_gather.32 = bf16[1024,128]{1,0:T(8,128)(2,1)S(1)} all-gather(bf16[128,128]{1,0:T(8,128)(2,1)} %param.29), channel_id=1, replica_groups=mesh['dp'=8,'mp'=4] {'dp'}, dimensions={0}, use_global_device_ids=true | all-gather | bytes 294912 | tf_op jit(solution)/shard_map/all_gather | solution.py:153
  115.8 25.6 %all_gather.33 = bf16[1024,256]{1,0:T(8,128)(2,1)S(1)} all-gather(bf16[128,256]{1,0:T(8,128)(2,1)S(1)} %copy-done.85), channel_id=1, replica_groups=mesh['dp'=8,'mp'=4] {'dp'}, dimensions={0}, use_global_device_ids=true | all-gather | bytes 589824 | tf_op jit(solution)/shard_map/all_gather | solution.py:154
  142.0 25.1 %all_gather.34 = bf16[1024,128]{1,0:T(8,128)(2,1)S(1)} all-gather(bf16[128,128]{1,0:T(8,128)(2,1)S(1)} %copy-done.88), channel_id=1, replica_groups=mesh['dp'=8,'mp'=4] {'dp'}, dimensions={0}, use_global_device_ids=true | all-gather | bytes 294912 | tf_op jit(solution)/shard_map/all_gather | solution.py:152
  168.2 53.0 %all_gather.30 = bf16[512,16]{1,0:T(8,128)(2,1)S(1)} all-gather(bf16[16,16]{1,0:T(8,128)(2,1)S(1)} %copy-done.98), channel_id=1, replica_groups=mesh['dp'=8,'mp'=4] {'dp','mp'}, dimensions={0}, use_global_device_ids=true | all-gather | bytes 16896 | tf_op jit(solution)/shard_map/all_gather | solution.py:123
  222.2 10.0 while.78
  233.4 29.3 %all_gather.36 = bf16[1024,256]{1,0:T(8,128)(2,1)S(1)} all-gather(bf16[128,256]{1,0:T(8,128)(2,1)S(1)} %copy-done.86), channel_id=1, replica_groups=mesh['dp'=8,'mp'=4] {'dp'}, dimensions={0}, use_global_device_ids=true | all-gather | bytes 589824 | tf_op jit(solution)/shard_map/all_gather | solution.py:155
  264.7 12.8 while.79
  265.6 1.2 dynamic_slice.371
  272.0 1.2 dynamic_slice.371
  278.3 26.6 %all_gather.37 = bf16[1024,256]{1,0:T(8,128)(2,1)S(1)} all-gather(bf16[128,256]{1,0:T(8,128)(2,1)S(1)} %copy-done.87), channel_id=1, replica_groups=mesh['dp'=8,'mp'=4] {'dp'}, dimensions={0}, use_global_device_ids=true | all-gather | bytes 589824 | tf_op jit(solution)/shard_map/all_gather | solution.py:156
  312.4 39.7 %all-reduce.23.cloned.1.call-done = (bf16[128,1024]{1,0:T(8,128)(2,1)}, bf16[128,1024]{1,0:T(8,128)(2,1)}) async-done(((bf16[128,1024]{1,0:T(8,128)(2,1)}, bf16[128,1024]{1,0:T(8,128)(2,1)}), (bf16[128,1024]{1,0:T(8,128)(2,1)}, bf16[128,1024]{1,0:T(8,128)(2,1)})) %all-reduce.23.cloned.1.call-update) | async-done | bytes 524304 | tf_op jit(solution)/shard_map/psum | solution.py:197
  352.1 1.3 multiply_reduce_fusion.5
  353.9 1.9 multiply_convert_fusion.1
  355.8 7.8 all-gather.5.cloned.1.call-done
  363.6 2.6 fusion.325
  366.3 40.7 %all-gather.7.cloned.1.call-done = bf16[1024,704]{0,1:T(8,128)(2,1)} async-done(((bf16[128,704]{0,1:T(8,128)(2,1)}), bf16[1024,704]{0,1:T(8,128)(2,1)}) %all-gather.7.cloned.1.call-update) | async-done | bytes 1441808 | tf_op jit(solution)/shard_map/all_gather | solution.py:158
  407.0 2.7 fusion.326
  409.7 1.3 fusion.323
  411.0 1.3 fusion.324
  412.3 37.9 %all-gather.9.cloned.1.call-done = bf16[1024,704]{0,1:T(8,128)(2,1)} async-done(((bf16[128,704]{0,1:T(8,128)(2,1)}), bf16[1024,704]{0,1:T(8,128)(2,1)}) %all-gather.9.cloned.1.call-update) | async-done | bytes 1441808 | tf_op jit(solution)/shard_map/all_gather | solution.py:159
  450.3 2.9 multiply_convert_fusion.2
  454.8 1.2 multiply_convert_fusion.4
  458.9 2.1 convolution_convert_fusion
  462.1 28.8 %all-reduce.21.cloned.1.call-done = (bf16[128,1024]{1,0:T(8,128)(2,1)}, bf16[128,1024]{1,0:T(8,128)(2,1)}) async-done(((bf16[128,1024]{1,0:T(8,128)(2,1)}, bf16[128,1024]{1,0:T(8,128)(2,1)}), (bf16[128,1024]{1,0:T(8,128)(2,1)}, bf16[128,1024]{1,0:T(8,128)(2,1)})) %all-reduce.21.cloned.1.call-update) | async-done | bytes 524304 | tf_op jit(solution)/shard_map/psum | solution.py:239
  491.0 2.2 fusion.214
  494.6 1.6 multiply_reduce_fusion.7
  497.7 25.9 %while.81 = (s32[]{:T(128)}, f32[1,128,256]{1,2,0:T(8,128)}, bf16[2,1,64,128]{3,2,1,0:T(8,128)(2,1)}, bf16[2,1,64,128]{3,2,1,0:T(8,128)(2,1)}, bf16[2,1,64,256]{...) while((s32[]{:T(128)}, f32[1,128,256]{1,2,0:T(8,128)}, ...), condition=%wide.region_35.36_spmd.clone, body=%wide.region_30.35_spmd.clone.sunk | while | flops 146305152 | bytes 3984778 | solution.py:78
  500.5 1.2 dynamic_slice.383
  503.8 1.3 broadcast_compare_fusion.19
  512.9 1.2 dynamic_slice.383
  517.1 1.3 broadcast_compare_fusion.19
  523.6 2.0 fusion.330
  525.6 1.4 convert_reduce_fusion
  528.6 19.5 %while.80 = (s32[]{:T(128)}, f32[1,128,256]{1,2,0:T(8,128)S(1)}, bf16[2,1,64,128]{3,2,1,0:T(8,128)(2,1)}, bf16[2,1,64,128]{3,2,1,0:T(8,128)(2,1)}, bf16[2,1,64,2...) while((s32[]{:T(128)}, f32[1,128,256]{1,2,0:T(8,128)S(1)}, ...), condition=%wide.region_24.25_spmd.clone, body=%wide.region_19.24_spmd.clone.sunk | while | flops 146305152 | bytes 5049906 | solution.py:78
  530.4 1.2 dynamic_slice.377
  533.6 1.3 broadcast_compare_fusion.18
  540.1 1.2 dynamic_slice.377
  543.4 1.3 broadcast_compare_fusion.18
  548.1 1.3 fusion.328
  559.0 1.2 convolution_add_fusion.12
  562.1 1.4 convolution_add_fusion.8
  564.0 1.4 convolution_add_fusion.7
  566.3 1.3 convolution_add_fusion.6
  568.6 2.1 convolution_add_fusion.5
  572.1 2.1 convolution_add_fusion.4
  575.9 2.2 add_bitcast_fusion
  578.9 85.1 %reduce-scatter.31.cloned.1.call-done = f32[32,16]{1,0:T(8,128)} async-done(((f32[1024,16]{1,0:T(8,128)}), f32[32,16]{1,0:T(8,128)}) %reduce-scatter.31.cloned.1.call-update) | async-done | bytes 2064
  663.9 1.4 copy.99
  665.3 62.6 %all-reduce.19.cloned.1.call-done = (bf16[128,1024]{1,0:T(8,128)(2,1)}, bf16[128,1024]{1,0:T(8,128)(2,1)}, bf16[128,1024]{1,0:T(8,128)(2,1)}, bf16[128,1024]{1,0:T(8,128)(2,1)}) async-done(((bf16[128,1024]{1,0:T(8,128)(2,1)}, bf16[128,1024]{1,0:T(8,128)(2,1)}, bf16[128,1024]{1,0:T(8,128)(2,1)}, bf16[128,1024]{1,0:T(8,128)(2,1)}), (bf16[128,1024]{1,0:T(8,128)(2,1)}, bf16[128,1024]{1,0:T(8,128)(2,1)}, ...) | async-done | bytes 1048592 | tf_op jit(solution)/shard_map/psum | solution.py:205
  727.9 1.5 fusion.215
  729.4 40.3 %all-reduce.10 = (f32[1024]{0:T(1024)S(1)}, f32[512]{0:T(512)S(1)}, f32[256]{0:T(256)S(1)}, f32[1024]{0:T(1024)S(1)}) all-reduce(f32[1024]{0:T(1024)S(1)} %add_multiply_fusion.1, f32[512]{0:T(512)S(1)} %add_dynamic-update-slice_fusion, f32[256]{0:T(256)S(1)} %add.384, ...), channel_id=2, replica_groups=mesh['dp'=8,'mp'=4] {'dp','mp'}, use_global_device_ids=true, to_apply=%region_40.41.clone | all-reduce | flops 2816 | bytes 22528
  772.1 1.6 fusion.228
  775.6 60.4 %reduce-scatter.21.cloned.1.call-done = f32[16,16]{1,0:T(8,128)} async-done(((f32[512,16]{1,0:T(8,128)}), f32[16,16]{1,0:T(8,128)}) %reduce-scatter.21.cloned.1.call-update) | async-done | bytes 1040 | tf_op jit(solution)/shard_map/reduce_scatter | solution.py:296
  836.0 89.2 %reduce-scatter.13.cloned.1.call-done = f32[128,128]{1,0:T(8,128)} async-done(((f32[1024,128]{1,0:T(8,128)}), f32[128,128]{1,0:T(8,128)}) %reduce-scatter.13.cloned.1.call-update) | async-done | bytes 65552 | tf_op jit(solution)/shard_map/reduce_scatter | solution.py:276
  925.2 64.8 %reduce-scatter.15.cloned.1.call-done = f32[128,128]{1,0:T(8,128)} async-done(((f32[1024,128]{1,0:T(8,128)}), f32[128,128]{1,0:T(8,128)}) %reduce-scatter.15.cloned.1.call-update) | async-done | bytes 65552 | tf_op jit(solution)/shard_map/reduce_scatter | solution.py:277
  990.0 66.8 %reduce-scatter.17.cloned.1.call-done = f32[128,256]{1,0:T(8,128)} async-done(((f32[1024,256]{1,0:T(8,128)}), f32[128,256]{1,0:T(8,128)}) %reduce-scatter.17.cloned.1.call-update) | async-done | bytes 131088 | tf_op jit(solution)/shard_map/reduce_scatter | solution.py:278
  1056.8 66.6 %reduce-scatter.19.cloned.1.call-done = f32[128,256]{1,0:T(8,128)} async-done(((f32[1024,256]{1,0:T(8,128)}), f32[128,256]{1,0:T(8,128)}) %reduce-scatter.19.cloned.1.call-update) | async-done | bytes 131088 | tf_op jit(solution)/shard_map/reduce_scatter | solution.py:279
  1123.3 66.7 %reduce-scatter.23.cloned.1.call-done = f32[128,256]{1,0:T(8,128)} async-done(((f32[1024,256]{1,0:T(8,128)}), f32[128,256]{1,0:T(8,128)}) %reduce-scatter.23.cloned.1.call-update) | async-done | bytes 131088 | tf_op jit(solution)/shard_map/reduce_scatter | solution.py:280
  1190.1 76.6 %reduce-scatter.25.cloned.1.call-done = f32[128,704]{0,1:T(8,128)} async-done(((f32[1024,704]{0,1:T(8,128)}), f32[128,704]{0,1:T(8,128)}) %reduce-scatter.25.cloned.1.call-update) | async-done | bytes 360464 | tf_op jit(solution)/shard_map/reduce_scatter | solution.py:281
  1266.7 75.4 %reduce-scatter.27.cloned.1.call-done = f32[128,704]{0,1:T(8,128)} async-done(((f32[1024,704]{0,1:T(8,128)}), f32[128,704]{0,1:T(8,128)}) %reduce-scatter.27.cloned.1.call-update) | async-done | bytes 360464 | tf_op jit(solution)/shard_map/reduce_scatter | solution.py:282
  1342.1 75.6 %reduce-scatter.29.cloned.1.call-done = f32[128,704]{0,1:T(8,128)} async-done(((f32[1024,704]{0,1:T(8,128)}), f32[128,704]{0,1:T(8,128)}) %reduce-scatter.29.cloned.1.call-update) | async-done | bytes 360464 | tf_op jit(solution)/shard_map/reduce_scatter | solution.py:283
  (559 shorter events, 96.5 us)
Async XLA Ops:
  8.0 106.6 %copy-start = (bf16[2,128,1024]{2,1,0:T(8,128)(2,1)S(1)}, bf16[2,128,1024]{2,1,0:T(8,128)(2,1)}, u32[]{:S(2)}) copy-start(bf16[2,128,1024]{2,1,0:T(8,128)(2,1)} %param.25) | copy-start | bytes 1572868
  8.0 344.1 %all-reduce.23.cloned.1.call-start = ((), (), s32[]{:S(2)}) async-start(), calls=%async_computation.25 | async-start | bytes 1048576 | tf_op jit(solution)/shard_map/psum | solution.py:197
  41.6 73.8 %copy-start.66 = (bf16[1024,16]{0,1:T(8,128)(2,1)}, bf16[1024,16]{0,1:T(8,128)(2,1)S(1)}, u32[]{:S(2)}) copy-start(bf16[1024,16]{0,1:T(8,128)(2,1)S(1)} %reshape.1385) | copy-start | bytes 98308
  93.9 21.6 %copy-start.106 = (f32[128]{0:T(128)}, f32[128]{0:T(128)S(1)}, u32[]{:S(2)}) copy-start(f32[128]{0:T(128)S(1)} %get-tuple-element.1198) | copy-start | bytes 1540
  93.9 21.9 %copy-start.104 = (f32[128]{0:T(128)}, f32[128]{0:T(128)S(1)}, u32[]{:S(2)}) copy-start(f32[128]{0:T(128)S(1)} %get-tuple-element.1199) | copy-start | bytes 1540
  114.9 106.4 %copy-start.101 = (bf16[128,16]{0,1:T(8,128)(2,1)}, bf16[128,16]{0,1:T(8,128)(2,1)S(1)}, u32[]{:S(2)}) copy-start(bf16[128,16]{0,1:T(8,128)(2,1)S(1)} %convolution_convert_fusion.13) | copy-start | bytes 12292
  115.5 148.2 %copy-start.99 = (bf16[128,16]{0,1:T(8,128)(2,1)}, bf16[128,16]{0,1:T(8,128)(2,1)S(1)}, u32[]{:S(2)}) copy-start(bf16[128,16]{0,1:T(8,128)(2,1)S(1)} %convolution_convert_fusion.12) | copy-start | bytes 12292
  115.8 26.2 %copy-start.88 = (bf16[128,128]{1,0:T(8,128)(2,1)S(1)}, bf16[128,128]{1,0:T(8,128)(2,1)}, u32[]{:S(2)}) copy-start(bf16[128,128]{1,0:T(8,128)(2,1)} %param.28) | copy-start | bytes 98308
  141.4 26.0 %copy-start.23 = (bf16[1024,256]{1,0:T(8,128)(2,1)}, bf16[1024,256]{1,0:T(8,128)(2,1)S(1)}, u32[]{:S(2)}) copy-start(bf16[1024,256]{1,0:T(8,128)(2,1)S(1)} %all_gather.33) | copy-start | bytes 1572868
  141.7 26.5 %copy-start.98 = (bf16[16,16]{1,0:T(8,128)(2,1)S(1)}, bf16[16,16]{1,0:T(8,128)(2,1)}, u32[]{:S(2)}) copy-start(bf16[16,16]{1,0:T(8,128)(2,1)} %param.33) | copy-start | bytes 1540
  221.1 42.6 %copy-start.71 = (bf16[512,16]{1,0:T(8,128)(2,1)}, bf16[512,16]{1,0:T(8,128)(2,1)S(1)}, u32[]{:S(2)}) copy-start(bf16[512,16]{1,0:T(8,128)(2,1)S(1)} %all_gather.30) | copy-start | bytes 49156
  222.1 11.2 copy-start.86
  232.7 31.8 %copy-start.28 = (f32[2,1,128,256]{3,2,1,0:T(8,128)}, f32[2,1,128,256]{3,2,1,0:T(8,128)S(1)}, u32[]{:S(2)}) copy-start(f32[2,1,128,256]{3,2,1,0:T(8,128)S(1)} %get-tuple-element.1926) | copy-start | bytes 786436
  232.7 31.9 %copy-start.19 = (f32[2,1,64,128]{3,2,1,0:T(8,128)}, f32[2,1,64,128]{3,2,1,0:T(8,128)S(1)}, u32[]{:S(2)}) copy-start(f32[2,1,64,128]{3,2,1,0:T(8,128)S(1)} %get-tuple-element.2016) | copy-start | bytes 196612
  232.7 32.0 %copy-start.15 = (f32[2,1,64,128]{3,2,1,0:T(8,128)}, f32[2,1,64,128]{3,2,1,0:T(8,128)S(1)}, u32[]{:S(2)}) copy-start(f32[2,1,64,128]{3,2,1,0:T(8,128)S(1)} %get-tuple-element.2014) | copy-start | bytes 196612
  232.7 72.1 %copy-start.39 = (f32[2,1,64,256]{3,2,1,0:T(8,128)}, f32[2,1,64,256]{3,2,1,0:T(8,128)S(1)}, u32[]{:S(2)}) copy-start(f32[2,1,64,256]{3,2,1,0:T(8,128)S(1)} %get-tuple-element.844) | copy-start | bytes 393220
  232.8 72.1 %copy-start.108 = (f32[256]{0:T(256)}, f32[256]{0:T(256)S(1)}, u32[]{:S(2)}) copy-start(f32[256]{0:T(256)S(1)} %convert_element_type.266) | copy-start | bytes 3076
  233.3 29.7 %copy-start.121 = (f32[128]{0:T(128)}, f32[128]{0:T(128)S(1)}, u32[]{:S(2)}) copy-start(f32[128]{0:T(128)S(1)} %add.342) | copy-start | bytes 1540
  233.3 71.5 %copy-start.112 = (f32[128]{0:T(128)}, f32[128]{0:T(128)S(1)}, u32[]{:S(2)}) copy-start(f32[128]{0:T(128)S(1)} %rsqrt.63) | copy-start | bytes 1540
  262.6 42.3 %copy-start.25 = (bf16[1024,256]{1,0:T(8,128)(2,1)}, bf16[1024,256]{1,0:T(8,128)(2,1)S(1)}, u32[]{:S(2)}) copy-start(bf16[1024,256]{1,0:T(8,128)(2,1)S(1)} %all_gather.36) | copy-start | bytes 1572868
  262.9 42.0 %copy-start.82 = (f32[128,256]{1,0:T(8,128)}, f32[128,256]{1,0:T(8,128)S(1)}, u32[]{:S(2)}) copy-start(f32[128,256]{1,0:T(8,128)S(1)} %fusion.303) | copy-start | bytes 393220
  264.7 13.6 copy-start.87
  277.6 28.3 %copy-start.3 = (f32[2,1,64,256]{3,2,1,0:T(8,128)}, f32[2,1,64,256]{3,2,1,0:T(8,128)S(1)}, u32[]{:S(2)}) copy-start(f32[2,1,64,256]{3,2,1,0:T(8,128)S(1)} %get-tuple-element.2009) | copy-start | bytes 393220
  277.6 28.3 %copy-start.41 = (f32[2,1,64,256]{3,2,1,0:T(8,128)}, f32[2,1,64,256]{3,2,1,0:T(8,128)S(1)}, u32[]{:S(2)}) copy-start(f32[2,1,64,256]{3,2,1,0:T(8,128)S(1)} %get-tuple-element.845) | copy-start | bytes 393220
  277.6 28.3 %copy-start.92 = (s32[2,64]{1,0:T(2,128)}, s32[2,64]{1,0:T(2,128)S(1)}, u32[]{:S(2)}) copy-start(s32[2,64]{1,0:T(2,128)S(1)} %get-tuple-element.2060) | copy-start | bytes 1540
  278.3 27.6 %copy-start.123 = (f32[128]{0:T(128)}, f32[128]{0:T(128)S(1)}, u32[]{:S(2)}) copy-start(f32[128]{0:T(128)S(1)} %add.352) | copy-start | bytes 1540
  278.3 27.6 %copy-start.114 = (f32[128]{0:T(128)}, f32[128]{0:T(128)S(1)}, u32[]{:S(2)}) copy-start(f32[128]{0:T(128)S(1)} %rsqrt.66) | copy-start | bytes 1540
  307.9 55.7 %all-gather.5.cloned.1.call-start = ((), (), s32[]{:S(2)}) async-start(), calls=%async_computation.10 | async-start | bytes 1622016 | tf_op jit(solution)/shard_map/all_gather | solution.py:157
  308.5 98.5 %all-gather.7.cloned.1.call-start = ((), (), s32[]{:S(2)}) async-start(), calls=%async_computation.11 | async-start | bytes 1622016 | tf_op jit(solution)/shard_map/all_gather | solution.py:158
  309.1 141.2 %all-gather.9.cloned.1.call-start = ((), (), s32[]{:S(2)}) async-start(), calls=%async_computation.12 | async-start | bytes 1622016 | tf_op jit(solution)/shard_map/all_gather | solution.py:159
  309.7 181.3 %all-reduce.21.cloned.1.call-start = ((), (), s32[]{:S(2)}) async-start(), calls=%async_computation.24 | async-start | bytes 1048576 | tf_op jit(solution)/shard_map/psum | solution.py:239
  309.9 45.9 %copy-start.43 = (bf16[2,1,64,128]{3,2,1,0:T(8,128)(2,1)}, bf16[2,1,64,128]{3,2,1,0:T(8,128)(2,1)S(1)}, u32[]{:S(2)}) copy-start(bf16[2,1,64,128]{3,2,1,0:T(8,128)(2,1)S(1)} %fusion.322) | copy-start | bytes 98308
  311.8 51.8 %copy-start.45 = (bf16[2,1,64,256]{3,2,1,0:T(8,128)(2,1)}, bf16[2,1,64,256]{3,2,1,0:T(8,128)(2,1)S(1)}, u32[]{:S(2)}) copy-start(bf16[2,1,64,256]{3,2,1,0:T(8,128)(2,1)S(1)} %fusion.321) | copy-start | bytes 196612
  353.4 12.9 copy-start.116
  353.9 12.4 copy-start.94
  353.9 12.4 copy-start.96
  355.8 51.2 %copy-start.9 = (bf16[128,1024]{1,0:T(8,128)(2,1)}, bf16[128,1024]{1,0:T(8,128)(2,1)S(1)}, u32[]{:S(2)}) copy-start(bf16[128,1024]{1,0:T(8,128)(2,1)S(1)} %get-tuple-element.1365) | copy-start | bytes 786436
  366.3 43.4 %copy-start.1 = (bf16[1024,704]{0,1:T(8,128)(2,1)S(1)}, bf16[1024,704]{0,1:T(8,128)(2,1)}, u32[]{:S(2)}) copy-start(bf16[1024,704]{0,1:T(8,128)(2,1)} %all-gather.5.cloned.1.call-done) | copy-start | bytes 4325380
  458.7 205.2 %reduce-scatter.31.cloned.1.call-start = ((), (), s32[]{:S(2)}) async-start(), calls=%async_computation.22 | async-start | bytes 540672
  458.9 32.0 %copy-start.7 = (bf16[128,1024]{1,0:T(8,128)(2,1)S(1)}, bf16[128,1024]{1,0:T(8,128)(2,1)}, u32[]{:S(2)}) copy-start(bf16[128,1024]{1,0:T(8,128)(2,1)} %get-tuple-element.1316) | copy-start | bytes 786436
  458.9 32.0 %copy-start.8 = (bf16[128,1024]{1,0:T(8,128)(2,1)S(1)}, bf16[128,1024]{1,0:T(8,128)(2,1)}, u32[]{:S(2)}) copy-start(bf16[128,1024]{1,0:T(8,128)(2,1)} %get-tuple-element.1317) | copy-start | bytes 786436
  458.9 32.0 %copy-start.95 = (f32[128]{0:T(128)S(1)}, f32[128]{0:T(128)}, u32[]{:S(2)}) copy-start(f32[128]{0:T(128)} %copy-done.94) | copy-start | bytes 1540
  458.9 32.0 %copy-start.97 = (f32[128]{0:T(128)S(1)}, f32[128]{0:T(128)}, u32[]{:S(2)}) copy-start(f32[128]{0:T(128)} %copy-done.96) | copy-start | bytes 1540
  461.0 32.1 %copy-start.119 = (f32[128]{0:T(128)S(1)}, f32[128]{0:T(128)}, u32[]{:S(2)}) copy-start(f32[128]{0:T(128)} %copy-done.118) | copy-start | bytes 1540
  461.0 32.1 %copy-start.117 = (f32[128]{0:T(128)S(1)}, f32[128]{0:T(128)}, u32[]{:S(2)}) copy-start(f32[128]{0:T(128)} %copy-done.116) | copy-start | bytes 1540
  462.1 31.1 %copy-start.34 = (bf16[2,128,1024]{2,1,0:T(8,128)(2,1)S(1)}, bf16[2,128,1024]{2,1,0:T(8,128)(2,1)}, u32[]{:S(2)}) copy-start(bf16[2,128,1024]{2,1,0:T(8,128)(2,1)} %param.41) | copy-start | bytes 1572868
  497.7 30.9 %copy-start.16 = (f32[2,1,64,128]{3,2,1,0:T(8,128)S(1)}, f32[2,1,64,128]{3,2,1,0:T(8,128)}, u32[]{:S(2)}) copy-start(f32[2,1,64,128]{3,2,1,0:T(8,128)} %copy-done.15) | copy-start | bytes 196612
  497.7 30.9 %copy-start.20 = (f32[2,1,64,128]{3,2,1,0:T(8,128)S(1)}, f32[2,1,64,128]{3,2,1,0:T(8,128)}, u32[]{:S(2)}) copy-start(f32[2,1,64,128]{3,2,1,0:T(8,128)} %copy-done.19) | copy-start | bytes 196612
  497.7 30.9 %copy-start.27 = (f32[1,128,256]{1,2,0:T(8,128)S(1)}, f32[1,128,256]{1,2,0:T(8,128)}, u32[]{:S(2)}) copy-start(f32[1,128,256]{1,2,0:T(8,128)} %custom-call.2) | copy-start | bytes 393220
  497.7 30.9 %copy-start.38 = (f32[2,1,64,128]{3,2,1,0:T(8,128)S(1)}, f32[2,1,64,128]{3,2,1,0:T(8,128)}, u32[]{:S(2)}) copy-start(f32[2,1,64,128]{3,2,1,0:T(8,128)} %copy-done.37) | copy-start | bytes 196612
  528.6 7.7 copy-start.68
  528.7 7.7 copy-start.72
  557.2 170.7 %all-reduce.19.cloned.1.call-start = ((), (), s32[]{:S(2)}) async-start(), calls=%async_computation.23 | async-start | bytes 2097152 | tf_op jit(solution)/shard_map/psum | solution.py:205
  557.8 278.2 %reduce-scatter.21.cloned.1.call-start = ((), (), s32[]{:S(2)}) async-start(), calls=%async_computation.17 | async-start | bytes 270336 | tf_op jit(solution)/shard_map/reduce_scatter | solution.py:296
  558.9 366.3 %reduce-scatter.13.cloned.1.call-start = ((), (), s32[]{:S(2)}) async-start(), calls=%async_computation.13 | async-start | bytes 589824 | tf_op jit(solution)/shard_map/reduce_scatter | solution.py:276
  560.2 429.8 %reduce-scatter.15.cloned.1.call-start = ((), (), s32[]{:S(2)}) async-start(), calls=%async_computation.14 | async-start | bytes 589824 | tf_op jit(solution)/shard_map/reduce_scatter | solution.py:277
  561.7 495.1 %reduce-scatter.17.cloned.1.call-start = ((), (), s32[]{:S(2)}) async-start(), calls=%async_computation.15 | async-start | bytes 1179648 | tf_op jit(solution)/shard_map/reduce_scatter | solution.py:278
  563.6 559.8 %reduce-scatter.19.cloned.1.call-start = ((), (), s32[]{:S(2)}) async-start(), calls=%async_computation.16 | async-start | bytes 1179648 | tf_op jit(solution)/shard_map/reduce_scatter | solution.py:279
  565.4 624.6 %reduce-scatter.23.cloned.1.call-start = ((), (), s32[]{:S(2)}) async-start(), calls=%async_computation.18 | async-start | bytes 1179648 | tf_op jit(solution)/shard_map/reduce_scatter | solution.py:280
  567.6 699.0 %reduce-scatter.25.cloned.1.call-start = ((), (), s32[]{:S(2)}) async-start(), calls=%async_computation.19 | async-start | bytes 3244032 | tf_op jit(solution)/shard_map/reduce_scatter | solution.py:281
  570.7 771.4 %reduce-scatter.27.cloned.1.call-start = ((), (), s32[]{:S(2)}) async-start(), calls=%async_computation.20 | async-start | bytes 3244032 | tf_op jit(solution)/shard_map/reduce_scatter | solution.py:282
  574.3 843.4 %reduce-scatter.29.cloned.1.call-start = ((), (), s32[]{:S(2)}) async-start(), calls=%async_computation.21 | async-start | bytes 3244032 | tf_op jit(solution)/shard_map/reduce_scatter | solution.py:283
  578.1 194.0 %copy-start.107 = (f32[128]{0:T(128)S(1)}, f32[128]{0:T(128)}, u32[]{:S(2)}) copy-start(f32[128]{0:T(128)} %copy-done.106) | copy-start | bytes 1540
  578.1 194.0 %copy-start.105 = (f32[128]{0:T(128)S(1)}, f32[128]{0:T(128)}, u32[]{:S(2)}) copy-start(f32[128]{0:T(128)} %copy-done.104) | copy-start | bytes 1540
  (83 other events, 163.0 us)
Sparse Core Ops, SparseCore 0:
  308.1 44.0 all-reduce.22
  458.8 32.0 all-reduce.20
  557.4 106.5 reduce-scatter.30
  667.1 60.7 all-reduce.18
  730.6 105.3 reduce-scatter.20
  840.2 84.9 reduce-scatter.12
  929.1 60.8 reduce-scatter.14
  994.4 62.3 reduce-scatter.16
  1060.7 62.5 reduce-scatter.18
  1127.5 62.4 reduce-scatter.22
  1194.2 72.4 reduce-scatter.24
  1270.7 71.3 reduce-scatter.26
  1346.2 71.4 reduce-scatter.28
Sparse Core Ops, SparseCore 1:
  310.4 53.1 all-gather.4
  365.5 41.4 all-gather.6
  408.9 41.3 all-gather.8
where the time goes:
time: 1430 us
  waiting for transfers between devices  947 us (66%)
  blocking collectives  300 us (21%)
  matrix products  69.9 us (5%)
  local copies, waits for them, and re-layouts  49.6 us (3%)
  other arithmetic  29.5 us (2%)
  between operations  17 us (1%)
    reduce_scatter x1, waiting for transfers between devices, on_device(): lax.psum_scatter(grad_mats[0], 'dp', scatter_dimension=0, tiled=True)  89.2 us
    unnamed x2, blocking collectives  87.9 us
    unnamed x17, waiting for transfers between devices  87.2 us
    reduce_scatter x1, waiting for transfers between devices, on_device(): lax.psum_scatter(grad_mats[5], 'dp', scatter_dimension=0, tiled=True)  76.6 us
    reduce_scatter x1, waiting for transfers between devices, on_device(): lax.psum_scatter(grad_mats[7], 'dp', scatter_dimension=0, tiled=True)  75.6 us
    reduce_scatter x1, waiting for transfers between devices, on_device(): lax.psum_scatter(grad_mats[6], 'dp', scatter_dimension=0, tiled=True)  75.4 us
    reduce_scatter x1, waiting for transfers between devices, on_device(): lax.psum_scatter(grad_mats[2], 'dp', scatter_dimension=0, tiled=True)  66.8 us
    reduce_scatter x1, waiting for transfers between devices, on_device(): lax.psum_scatter(grad_mats[4], 'dp', scatter_dimension=0, tiled=True)  66.7 us
  transfers between devices with their start and end apart: 16, of which 16 were waited for; matrix products, arithmetic and copies ran while one was open for 3% of the time, Pallas kernels for 0%

commit v1 on v0

v1 whole, which is shorter than its diff:
```python
import jax
import jax.numpy as jnp
from jax import lax
from jax.sharding import PartitionSpec as P

H = 4
norm_eps = 1e-06
head_eps = 0.1
gate_divisor = 16.0
BF = jnp.bfloat16
F32 = jnp.float32


def dot(left, right):
    return jnp.dot(left, right, preferred_element_type=F32)


def dot_t(left, right):
    return lax.dot_general(left, right, (((0,), (0,)), ((), ())), preferred_element_type=F32)


def dot_rt(left, right):
    return lax.dot_general(left, right, (((1,), (1,)), ((), ())), preferred_element_type=F32)


def exact(spec, left, right):
    return jnp.einsum(
        spec, left, right, precision=lax.Precision.HIGHEST, preferred_element_type=F32
    )


def rms_gain(values, gain):
    return values * lax.rsqrt(jnp.mean(values * values, axis=-1, keepdims=True) + norm_eps) * gain


def gla_core(queries, keys, values, decays, mask, lower):
    length, width = queries.shape[1], queries.shape[3]
    total = exact("ts,nshd->nthd", lower, decays)
    middle = lax.stop_gradient(total[:, length // 2 - 1 : length // 2])
    query_up = queries * jnp.exp(total - middle)
    key_down = keys * jnp.exp(middle - total)
    scores = jnp.where(mask, exact("nthd,nshd->nhts", query_up, key_down), 0.0)
    return width ** (-0.5) * exact("nhts,nshd->nthd", scores, values)


def head_gate(core_out, gate_lin, head_gain):
    normed = (
        core_out
        * lax.rsqrt(jnp.mean(core_out * core_out, axis=-1, keepdims=True) + head_eps)
        * head_gain
    )
    gate_three = gate_lin.reshape(core_out.shape)
    return normed * gate_three * jax.nn.sigmoid(gate_three)


class Rows:
    def __init__(self):
        self.count = lax.axis_size("dp")
        self.direct = self.count <= 8
        self.outer = self.count // 2
        index = lax.axis_index("dp")
        self.z, self.x = index // 2, index % 2

    def slots(self):
        if not self.direct:
            return list(range(self.count))
        return [
            lax.rem(self.z - s + self.outer, self.outer) * 2 + (1 - self.x if b else self.x)
            for s in range(self.outer)
            for b in range(2)
        ]

    def relative(self, array, axis):
        if not self.direct:
            return array
        size = array.shape[axis] // self.count
        return jnp.concatenate(
            [lax.dynamic_slice_in_dim(array, slot * size, size, axis) for slot in self.slots()],
            axis=axis,
        )

    def pair(self, array):
        return lax.ppermute(array, "dp", [(i, i ^ 1) for i in range(self.count)])

    def shift(self, array, step):
        n = self.outer
        perm = [(i, (i // 2 + step) % n * 2 + i % 2) for i in range(self.count)]
        return lax.ppermute(array, "dp", perm)

    def gather(self, block, axis):
        if not self.direct:
            return lax.all_gather(block, "dp", axis=axis, tiled=True)
        line = [block] + [self.shift(block, s) for s in range(1, self.outer)]
        pieces = []
        for item in line:
            pieces += [item, self.pair(item)]
        return jnp.concatenate(pieces, axis=axis)

    def scatter(self, blocks):
        if not self.direct:
            stacked = jnp.stack([blocks(i).astype(F32) for i in range(self.count)])
            return lax.psum_scatter(stacked, "dp", scatter_dimension=0, tiled=False)
        sums = []
        for s in range(self.outer):
            got = self.pair(blocks(2 * s + 1).astype(BF))
            sums.append(blocks(2 * s).astype(F32) + got.astype(F32))
        total = sums[0]
        for s in range(1, self.outer):
            total = total + self.shift(sums[s].astype(BF), -s).astype(F32)
        return total


class Lanes:
    def __init__(self):
        self.count = lax.axis_size("mp")
        self.index = lax.axis_index("mp")

    def at(self, step):
        return lax.rem(self.index + step, self.count)

    def send(self, array, step):
        return lax.ppermute(
            array, "mp", [(i, (i + step) % self.count) for i in range(self.count)]
        )

    def own(self, array, step=0):
        size = array.shape[0] // self.count
        return lax.dynamic_slice_in_dim(array, self.at(step) * size, size, 0)

    def scatter(self, array):
        total = self.own(array).astype(F32)
        low = array.astype(BF)
        for step in range(1, self.count):
            total = total + self.send(self.own(low, step), step).astype(F32)
        return total

    def gather(self, chunk):
        pieces = [chunk] + [self.send(chunk, step) for step in range(1, self.count)]
        size = chunk.shape[0]
        result = jnp.zeros((size * self.count,) + chunk.shape[1:], chunk.dtype)
        for step, piece in enumerate(pieces):
            place = lax.rem(self.index - step + self.count, self.count) * size
            result = lax.dynamic_update_slice_in_dim(result, piece, place, 0)
        return result


def on_device(
    inputs,
    segment,
    norm_gain,
    w_query,
    w_key,
    w_value,
    w_gate_out,
    w_rank_in,
    w_rank_out,
    rank_bias,
    head_gain,
    w_output,
    ffn_gain,
    w_ffn_gate,
    w_ffn_up,
    w_ffn_down,
    cotangent,
):
    rows, lanes = Rows(), Lanes()
    micro, length, model = inputs.shape
    n_tok = micro * length
    heads_local = H // lanes.count
    key_cols, value_cols = w_query.shape[1], w_value.shape[1]

    small_parts = (norm_gain, ffn_gain, head_gain, rank_bias, w_rank_in, w_rank_out)
    small_sizes = [part.size for part in small_parts]
    small_total = sum(small_sizes)
    small_width = -(-small_total // 2048) * 2048
    flat = jnp.concatenate([part.reshape(-1) for part in small_parts])
    flat = jnp.pad(flat, (0, small_width - small_total)).reshape(1, 16, small_width // 16)
    small_rel = rows.gather(lanes.gather(flat)[None], 0)
    small_rel = small_rel.reshape(rows.count, lanes.count, small_width)
    small_abs = rows.relative(small_rel, 0)

    def small(source, which):
        start = sum(small_sizes[:which])
        return source[:, :, start : start + small_sizes[which]]

    gain_in = small(small_rel, 0).reshape(-1).astype(F32)
    gain_mid = small(small_rel, 1).reshape(-1).astype(F32)
    gain_head = small(small_abs, 2).reshape(-1).astype(F32)
    bias_all = small(small_abs, 3).reshape(-1)
    rank_in = small(small_rel, 4).reshape(model, -1)
    rank_out_all = small(small_abs, 5).reshape(-1, rank_in.shape[1])
    head_start = lanes.index * key_cols
    rank_out = lax.dynamic_slice_in_dim(rank_out_all, head_start, key_cols, 0)
    bias_local = lax.dynamic_slice_in_dim(bias_all, head_start, key_cols, 0).astype(F32)

    attn_mat = rows.gather(
        jnp.concatenate([w_query, w_key, w_value, w_gate_out, w_output], axis=1), 0
    )
    in_cols = 2 * key_cols + 2 * value_cols
    in_mat, out_mat = attn_mat[:, :in_cols], attn_mat[:, in_cols:]
    ffn_mat = rows.gather(jnp.stack([w_ffn_gate, w_ffn_up, w_ffn_down]), 1)
    full_gate, full_up, full_down = ffn_mat[0], ffn_mat[1], ffn_mat[2]

    tokens_low = rows.relative(inputs.reshape(n_tok, model), 1)
    dy_low = rows.relative(cotangent.reshape(n_tok, model), 1)
    tokens = tokens_low.astype(F32)
    own_tokens = lanes.own(tokens_low).astype(F32)
    own_dy = lanes.own(dy_low).astype(F32)
    normed_low = rms_gain(tokens, gain_in).astype(BF)
    projected = dot(normed_low, in_mat)
    qkv_low = projected[:, : in_cols - value_cols].astype(BF).astype(F32)
    gate_lin = projected[:, in_cols - value_cols :]
    rank_low = dot(normed_low, rank_in).astype(BF)
    logits = dot_rt(rank_low, rank_out) + bias_local
    decays = jax.nn.log_sigmoid(logits) / gate_divisor

    def heads(array):
        return array.reshape(micro, length, heads_local, -1)

    position = jnp.arange(length)
    lower_mask = position[:, None] >= position[None, :]
    same = segment[:, :, None] == segment[:, None, :]
    mask = (lower_mask[None] & same)[:, None]
    lower = lower_mask.astype(F32)

    def core(queries, keys, values, decay):
        return gla_core(queries, keys, values, decay, mask, lower)

    core_out, core_back = jax.vjp(
        core,
        heads(qkv_low[:, :key_cols]),
        heads(qkv_low[:, key_cols : 2 * key_cols]),
        heads(qkv_low[:, 2 * key_cols :]),
        heads(decays),
    )
    gated, gate_back = jax.vjp(head_gate, core_out, gate_lin, gain_head)
    gated_low = gated.reshape(n_tok, -1).astype(BF)
    own_attended = lanes.scatter(dot_rt(gated_low, out_mat))
    own_middle = own_tokens + own_attended
    own_mid, norm_mid_back = jax.vjp(rms_gain, own_middle, gain_mid)
    mid_low = lanes.gather(own_mid.astype(BF))
    d_hidden = dot(dy_low, full_down)
    gate_act = dot(mid_low, full_gate)
    up_act = dot(mid_low, full_up)
    sigma = jax.nn.sigmoid(gate_act)
    hidden_low = (gate_act * sigma * up_act).astype(BF)

    d_gate_low = (d_hidden * up_act * sigma * (1.0 + gate_act * (1.0 - sigma))).astype(BF)
    d_up_low = (d_hidden * gate_act * sigma).astype(BF)
    own_d_mid = lanes.scatter(dot_rt(d_gate_low, full_gate) + dot_rt(d_up_low, full_up))
    own_output = own_middle + lanes.scatter(dot_rt(hidden_low, full_down))
    grad_down = dot_t(dy_low, hidden_low).astype(BF)
    grad_gate = dot_t(mid_low, d_gate_low).astype(BF)
    grad_up = dot_t(mid_low, d_up_low).astype(BF)
    block = model // rows.count

    def ffn_block(slot):
        part = slice(slot * block, (slot + 1) * block)
        return jnp.stack([grad_gate[part], grad_up[part], grad_down[part]])

    ffn_grads = rows.scatter(ffn_block)
    own_d_middle, grad_gain_mid = norm_mid_back(own_d_mid)
    own_d_middle = own_dy + own_d_middle

    d_att_low = lanes.gather(own_d_middle.astype(BF))
    d_gated = dot(d_att_low, out_mat)
    d_core, d_gate_lin, grad_head = gate_back(heads(d_gated))
    d_queries, d_keys, d_values, d_decays = core_back(d_core)
    d_in_low = jnp.concatenate(
        [
            d_queries.reshape(n_tok, -1).astype(BF),
            d_keys.reshape(n_tok, -1).astype(BF),
            d_values.reshape(n_tok, -1).astype(BF),
            d_gate_lin.astype(BF),
        ],
        axis=1,
    )
    d_logit_low = (d_decays.reshape(n_tok, -1) * jax.nn.sigmoid(-logits) / gate_divisor).astype(BF)
    d_rank_low = dot(d_logit_low, rank_out).astype(BF)
    own_d_in = lanes.scatter(dot_rt(d_in_low, in_mat) + dot_rt(d_rank_low, rank_in))
    grad_in = dot_t(normed_low, d_in_low).astype(BF)
    grad_out = dot_t(d_att_low, gated_low).astype(BF)

    def attn_block(slot):
        part = slice(slot * block, (slot + 1) * block)
        return jnp.concatenate([grad_in[part], grad_out[part]], axis=1)

    attn_grads = rows.scatter(attn_block)
    _, norm_in_back = jax.vjp(rms_gain, own_tokens, gain_in)
    own_d_tokens, grad_gain_in = norm_in_back(own_d_in)
    own_input_grad = own_d_middle + own_d_tokens

    grad_rank_out = dot_t(d_logit_low, rank_low)
    grad_bias = jnp.sum(d_logit_low.astype(F32), axis=0)
    grad_rank_in = dot_t(normed_low, d_rank_low)
    rank_out_full = lax.dynamic_update_slice_in_dim(
        jnp.zeros(rank_out_all.shape, F32), grad_rank_out, head_start, 0
    )
    bias_full = lax.dynamic_update_slice_in_dim(
        jnp.zeros(bias_all.shape, F32), grad_bias, head_start, 0
    )

    def owners(array):
        return array.reshape(rows.count, lanes.count, -1)

    small_grads = jnp.concatenate(
        [
            owners(grad_gain_in),
            owners(grad_gain_mid),
            rows.relative(
                jnp.concatenate([owners(grad_head), owners(bias_full)], axis=2), 0
            ),
            owners(grad_rank_in),
            rows.relative(owners(rank_out_full), 0),
        ],
        axis=2,
    )
    small_grads = jnp.pad(small_grads, ((0, 0), (0, 0), (0, small_width - small_total)))
    small_sum = rows.scatter(lambda slot: small_grads[slot])
    small_own = lanes.scatter(small_sum).reshape(-1)

    def small_out(which, like):
        start = sum(small_sizes[:which])
        return small_own[start : start + small_sizes[which]].reshape(like.shape)

    output = rows.relative(lanes.gather(own_output.astype(BF)), 1)
    input_grad = rows.relative(lanes.gather(own_input_grad.astype(BF)), 1).astype(F32)
    kk, kv = key_cols, value_cols
    return (
        output.reshape(inputs.shape),
        input_grad.reshape(inputs.shape),
        small_out(0, norm_gain),
        attn_grads[:, :kk],
        attn_grads[:, kk : 2 * kk],
        attn_grads[:, 2 * kk : 2 * kk + kv],
        attn_grads[:, 2 * kk + kv : in_cols],
        small_out(4, w_rank_in),
        small_out(5, w_rank_out),
        small_out(3, rank_bias),
        small_out(2, head_gain),
        attn_grads[:, in_cols:],
        small_out(1, ffn_gain),
        ffn_grads[0],
        ffn_grads[1],
        ffn_grads[2],
    )


def solution(mesh):
    in_specs = (
        P(None, "dp", None),
        P(None, "dp"),
        P(("dp", "mp")),
        P("dp", "mp"),
        P("dp", "mp"),
        P("dp", "mp"),
        P("dp", "mp"),
        P(("dp", "mp"), None),
        P(("dp", "mp"), None),
        P(("dp", "mp")),
        P(("dp", "mp")),
        P("dp", "mp"),
        P(("dp", "mp")),
        P("dp", "mp"),
        P("dp", "mp"),
        P("dp", "mp"),
        P(None, "dp", None),
    )
    out_specs = (
        P(None, "dp", None),
        P(None, "dp", None),
        P(("dp", "mp")),
        P("dp", "mp"),
        P("dp", "mp"),
        P("dp", "mp"),
        P("dp", "mp"),
        P(("dp", "mp"), None),
        P(("dp", "mp"), None),
        P(("dp", "mp")),
        P(("dp", "mp")),
        P("dp", "mp"),
        P(("dp", "mp")),
        P("dp", "mp"),
        P("dp", "mp"),
        P("dp", "mp"),
    )
    return jax.shard_map(
        on_device, mesh=mesh, in_specs=in_specs, out_specs=out_specs, check_vma=False
    )
```

time: 1430 us -> 323 us (0.23)
  waiting for transfers between devices: 947 us -> 118 us
  blocking collectives: 300 us -> 0 us
  starting transfers between devices: 1.06 us -> 97.4 us
  matrix products: 69.9 us -> 20.6 us
  between operations: 17 us -> 2.33 us
    reduce_scatter x9 -> x0, waiting for transfers between devices: 642 us -> none  [the longest x1 89.2 us: on_device(): lax.psum_scatter(grad_mats[0], 'dp', scatter_dimension=0, tiled=True)]
    all_gather x7 -> x0, blocking collectives: 212 us -> none  [the longest x1 53 us: on_device(): lax.all_gather(w_rank_out, ('dp', 'mp'), axis=0, tiled=True)]
    psum x3 -> x0, waiting for transfers between devices: 131 us -> none  [the longest x1 62.6 us: on_device(): ffn_out = lax.psum(ffn_part.astype(jnp.bfloat16), 'mp').astype(jnp.float32)]
    ppermute x0 -> x72, waiting for transfers between devices: none -> 118 us  [the longest x18 57.6 us: shift(): return lax.ppermute(array, 'dp', perm)]
    ppermute x0 -> x72, starting transfers between devices: none -> 97.4 us  [the longest x30 41.1 us: send(): lax.ppermute(array, 'mp', [(i, (i + step) % self.count) for i in range(se...]
    unnamed x2 -> x0, blocking collectives: 87.9 us -> none
    unnamed x17 -> x0, waiting for transfers between devices: 87.2 us -> none
    all_gather x3 -> x0, waiting for transfers between devices: 86.4 us -> none  [the longest x1 40.7 us: on_device(): lax.all_gather(w_ffn_up, 'dp', axis=0, tiled=True)]
  transfers between devices with their start and end apart: 16 -> 72, of which waited for: 16 -> 29; matrix products, arithmetic and copies ran while one was open for 3% -> 27% of each run, Pallas kernels for 0% -> 0%
where the time goes in v1:
time: 323 us; the launch traced here: 322 us
  waiting for transfers between devices  118 us (37%)
  starting transfers between devices  97.4 us (30%)
  local copies, waits for them, and re-layouts  54.9 us (17%)
  other arithmetic  28.7 us (9%)
  matrix products  20.6 us (6%)
    ppermute x18, waiting for transfers between devices, shift(): return lax.ppermute(array, 'dp', perm)  57.6 us
    ppermute x24, waiting for transfers between devices, pair(): return lax.ppermute(array, 'dp', [(i, i ^ 1) for i in range(self.count)])  44.4 us
    ppermute x30, starting transfers between devices, send(): lax.ppermute(array, 'mp', [(i, (i + step) % self.count) for i in range(se...  41.1 us
    ppermute x18, starting transfers between devices, shift(): return lax.ppermute(array, 'dp', perm)  39.6 us
    unnamed x203, local copies, waits for them, and re-layouts  26.9 us
    ppermute x24, starting transfers between devices, pair(): return lax.ppermute(array, 'dp', [(i, i ^ 1) for i in range(self.count)])  16.7 us
    ppermute x30, waiting for transfers between devices, send(): lax.ppermute(array, 'mp', [(i, (i + step) % self.count) for i in range(se...  15.5 us
    dot_general x7, matrix products, dot_rt(): lax.dot_general(left, right, (((1,), (1,)), ((), ())), preferred_element_...  7.47 us
  transfers between devices with their start and end apart: 72, of which 29 were waited for; matrix products, arithmetic and copies ran while one was open for 27% of the time, Pallas kernels for 0%

profile of v1, /device:TPU:13, one launch (start us, length us, event | category | flops | bytes accessed | tf_op | source)
XLA Modules:
  0.0 321.5 jit_solution(9288338853497999641)
XLA Ops:
  0.7 1.5 constant_dynamic-update-slice_fusion.20
  2.2 1.4 constant_dynamic-update-slice_fusion.19
  3.6 1.5 constant_dynamic-update-slice_fusion.18
  5.1 1.5 constant_dynamic-update-slice_fusion.17
  6.6 1.5 constant_dynamic-update-slice_fusion.16
  8.1 1.2 collective-permute-start.10
  9.3 1.3 collective-permute-start.11
  13.3 2.8 concatenate.87
  16.0 1.6 collective-permute-start
  17.6 1.2 collective-permute-start.1
  28.0 3.0 collective-permute-done.2
  31.6 1.9 collective-permute-done.3
  33.6 1.6 collective-permute-start.6
  37.1 1.5 collective-permute-start.8
  39.7 1.6 collective-permute-start.15
  42.0 2.1 collective-permute-done.9
  52.9 5.8 %collective-permute-start.26 = (bf16[3,128,704]{1,2,0:T(8,128)(2,1)}, bf16[3,128,704]{1,2,0:T(8,128)(2,1)S(1)}, u32[]{:S(2)}, u32[]{:S(2)}) collective-permute-start(bf16[3,128,704]{1,2,0:T(8,128)(2,1)} %get-tuple-element.110), channel_id=1, source_target_pairs={{0,16},{4,20},{8,24},{12,28},{16,0},{20,4},{24,8},{28,12},{1,17},{... | collective-permute-start | bytes 1622024 | tf_op jit(solution)/shard_map/ppermute | solution.py:88
  58.7 1.7 collective-permute-done.12
  62.4 3.5 %collective-permute-done.14 = bf16[128,1024]{1,0:T(8,128)(2,1)S(1)} collective-permute-done((bf16[128,1024]{1,0:T(8,128)(2,1)S(1)}, bf16[128,1024]{1,0:T(8,128)(2,1)S(1)}, u32[]{:S(2)}, u32[]{:S(2)}) %collective-permute-start.14) | collective-permute-done | bytes 262176 | tf_op jit(solution)/shard_map/ppermute | solution.py:83
  65.9 4.1 %collective-permute-start.28 = (bf16[3,128,704]{1,2,0:T(8,128)(2,1)}, bf16[3,128,704]{1,2,0:T(8,128)(2,1)S(1)}, u32[]{:S(2)}, u32[]{:S(2)}) collective-permute-start(bf16[3,128,704]{1,2,0:T(8,128)(2,1)} %get-tuple-element.110), channel_id=1, source_target_pairs={{0,24},{4,28},{8,0},{12,4},{16,8},{20,12},{24,16},{28,20},{1,25},{... | collective-permute-start | bytes 1622024 | tf_op jit(solution)/shard_map/ppermute | solution.py:88
  72.3 2.1 fusion.121
  76.7 1.4 fusion.122
  78.2 6.9 %collective-permute-start.19 = (bf16[64,1024]{1,0:T(8,128)(2,1)S(1)}, bf16[64,1024]{1,0:T(8,128)(2,1)S(1)}, u32[]{:S(2)}, u32[]{:S(2)}) collective-permute-start(bf16[64,1024]{1,0:T(8,128)(2,1)S(1)} %get-tuple-element.144), channel_id=1, source_target_pairs={{0,3},{1,0},{2,1},{3,2},{4,7},{5,4},{6,5},{7,6},{8,11},{9,8},{10,9... | collective-permute-start | bytes 393224 | tf_op jit(solution)/shard_map/ppermute | solution.py:122
  85.1 7.5 %collective-permute-start.17 = (bf16[64,1024]{1,0:T(8,128)(2,1)S(1)}, bf16[64,1024]{1,0:T(8,128)(2,1)S(1)}, u32[]{:S(2)}, u32[]{:S(2)}) collective-permute-start(bf16[64,1024]{1,0:T(8,128)(2,1)S(1)} %get-tuple-element.143), channel_id=1, source_target_pairs={{0,1},{1,2},{2,3},{3,0},{4,5},{5,6},{6,7},{7,4},{8,9},{9,10},{10,1... | collective-permute-start | bytes 393224 | tf_op jit(solution)/shard_map/ppermute | solution.py:122
  92.7 1.2 constant_dynamic-update-slice_fusion.47
  95.2 9.2 %collective-permute-done.28 = bf16[3,128,704]{1,2,0:T(8,128)(2,1)S(1)} collective-permute-done((bf16[3,128,704]{1,2,0:T(8,128)(2,1)}, bf16[3,128,704]{1,2,0:T(8,128)(2,1)S(1)}, u32[]{:S(2)}, u32[]{:S(2)}) %collective-permute-start.28) | collective-permute-done | bytes 540704 | tf_op jit(solution)/shard_map/ppermute | solution.py:88
  106.4 2.3 collective-permute-start.21
  109.2 3.3 %collective-permute-start.22 = (bf16[64,1024]{1,0:T(8,128)(2,1)S(1)}, bf16[64,1024]{1,0:T(8,128)(2,1)S(1)}, u32[]{:S(2)}, u32[]{:S(2)}) collective-permute-start(bf16[64,1024]{1,0:T(8,128)(2,1)S(1)} %get-tuple-element.68), channel_id=1, source_target_pairs={{0,3},{1,0},{2,1},{3,2},{4,7},{5,4},{6,5},{7,6},{8,11},{9,8},{10,9... | collective-permute-start | bytes 393224 | tf_op jit(solution)/shard_map/ppermute | solution.py:122
  112.6 2.4 collective-permute-done.21
  116.0 2.7 collective-permute-done.27
  119.1 11.2 %collective-permute-done.29 = bf16[3,128,704]{1,2,0:T(8,128)(2,1)S(1)} collective-permute-done((bf16[3,128,704]{1,2,0:T(8,128)(2,1)S(1)}, bf16[3,128,704]{1,2,0:T(8,128)(2,1)S(1)}, u32[]{:S(2)}, u32[]{:S(2)}) %collective-permute-start.29) | collective-permute-done | bytes 540704 | tf_op jit(solution)/shard_map/ppermute | solution.py:83
  134.9 2.0 collective-permute-start.32
  138.3 1.6 collective-permute-start.37
  139.9 1.7 collective-permute-start.36
  150.8 1.6 collective-permute-start.39
  155.0 1.4 reshape.449
  157.0 2.5 collective-permute-done.40
  159.5 3.5 %collective-permute-done.41 = bf16[64,1024]{1,0:T(8,128)(2,1)S(1)} collective-permute-done((bf16[64,1024]{1,0:T(8,128)(2,1)}, bf16[64,1024]{1,0:T(8,128)(2,1)S(1)}, u32[]{:S(2)}, u32[]{:S(2)}) %collective-permute-start.41) | collective-permute-done | bytes 131104 | tf_op jit(solution)/shard_map/ppermute | solution.py:122
  163.0 1.3 fusion.15
  164.4 1.8 fusion.31
  172.7 1.8 convolution_convert_fusion
  174.5 3.0 fusion.125
  179.3 2.0 collective-permute-start.42
  188.1 2.4 fusion.116
  194.4 1.4 fusion.30
  201.2 2.9 collective-permute-start.52
  204.2 1.4 collective-permute-start.50
  206.9 2.2 collective-permute-start.57
  218.0 1.7 collective-permute-done.46
  220.5 1.8 collective-permute-done.47
  224.7 10.4 %collective-permute-done.63 = bf16[128,1024]{0,1:T(8,128)(2,1)S(1)} collective-permute-done((bf16[128,1024]{0,1:T(8,128)(2,1)}, bf16[128,1024]{0,1:T(8,128)(2,1)S(1)}, u32[]{:S(2)}, u32[]{:S(2)}) %collective-permute-start.63) | collective-permute-done | bytes 262176 | tf_op jit(solution)/shard_map/ppermute | solution.py:83
  235.7 5.0 %collective-permute-done.61 = bf16[128,1024]{0,1:T(8,128)(2,1)S(1)} collective-permute-done((bf16[128,1024]{0,1:T(8,128)(2,1)}, bf16[128,1024]{0,1:T(8,128)(2,1)S(1)}, u32[]{:S(2)}, u32[]{:S(2)}) %collective-permute-start.61) | collective-permute-done | bytes 262176 | tf_op jit(solution)/shard_map/ppermute | solution.py:83
  241.3 5.0 %collective-permute-done.59 = bf16[128,1024]{0,1:T(8,128)(2,1)S(1)} collective-permute-done((bf16[128,1024]{0,1:T(8,128)(2,1)S(1)}, bf16[128,1024]{0,1:T(8,128)(2,1)S(1)}, u32[]{:S(2)}, u32[]{:S(2)}) %collective-permute-start.59) | collective-permute-done | bytes 262176 | tf_op jit(solution)/shard_map/ppermute | solution.py:83
  246.8 2.1 collective-permute-start.62
  248.9 2.0 add_convert_fusion
  253.6 1.5 collective-permute-start.71
  255.1 2.2 collective-permute-start.69
  257.3 3.7 %collective-permute-done.62 = bf16[128,1024]{0,1:T(8,128)(2,1)S(1)} collective-permute-done((bf16[128,1024]{0,1:T(8,128)(2,1)S(1)}, bf16[128,1024]{0,1:T(8,128)(2,1)S(1)}, u32[]{:S(2)}, u32[]{:S(2)}) %collective-permute-start.62) | collective-permute-done | bytes 262176 | tf_op jit(solution)/shard_map/ppermute | solution.py:88
  261.0 11.6 %collective-permute-start.67 = (bf16[3,128,704]{1,2,0:T(8,128)(2,1)S(1)}, bf16[3,128,704]{1,2,0:T(8,128)(2,1)}, u32[]{:S(2)}, u32[]{:S(2)}) collective-permute-start(bf16[3,128,704]{1,2,0:T(8,128)(2,1)S(1)} %add_convert_fusion.2), channel_id=1, source_target_pairs={{0,24},{4,28},{8,0},{12,4},{16,8},{20,12},{24,16},{28,20},{1,25},{... | collective-permute-start | bytes 1622024 | tf_op jit(solution)/shard_map/ppermute | solution.py:88
  272.6 22.9 %collective-permute-done.60 = bf16[128,1024]{0,1:T(8,128)(2,1)S(1)} collective-permute-done((bf16[128,1024]{0,1:T(8,128)(2,1)S(1)}, bf16[128,1024]{0,1:T(8,128)(2,1)S(1)}, u32[]{:S(2)}, u32[]{:S(2)}) %collective-permute-start.60) | collective-permute-done | bytes 262176 | tf_op jit(solution)/shard_map/ppermute | solution.py:88
  299.5 1.3 collective-permute-done.71
  300.8 11.6 %collective-permute-done.69 = bf16[3,128,704]{1,2,0:T(8,128)(2,1)} collective-permute-done((bf16[3,128,704]{1,2,0:T(8,128)(2,1)}, bf16[3,128,704]{1,2,0:T(8,128)(2,1)}, u32[]{:S(2)}, u32[]{:S(2)}) %collective-permute-start.69) | collective-permute-done | bytes 540704 | tf_op jit(solution)/shard_map/ppermute | solution.py:88
  312.3 6.5 %collective-permute-done.67 = bf16[3,128,704]{1,2,0:T(8,128)(2,1)} collective-permute-done((bf16[3,128,704]{1,2,0:T(8,128)(2,1)S(1)}, bf16[3,128,704]{1,2,0:T(8,128)(2,1)}, u32[]{:S(2)}, u32[]{:S(2)}) %collective-permute-start.67) | collective-permute-done | bytes 540704 | tf_op jit(solution)/shard_map/ppermute | solution.py:88
  318.8 1.7 convert_add_fusion
  (448 shorter events, 100.9 us)
Async XLA Ops:
  8.1 42.8 %collective-permute-start.10 = (bf16[128,1024]{1,0:T(8,128)(2,1)}, bf16[128,1024]{1,0:T(8,128)(2,1)S(1)}, u32[]{:S(2)}, u32[]{:S(2)}) collective-permute-start(bf16[128,1024]{1,0:T(8,128)(2,1)} %get-tuple-element.159), channel_id=1, source_target_pairs={{0,4},{4,0},{8,12},{12,8},{16,20},{20,16},{24,28},{28,24},{1,5},{5... | collective-permute-start | bytes 786440 | tf_op jit(solution)/shard_map/ppermute | solution.py:83
  9.3 38.4 %collective-permute-start.11 = (bf16[128,1024]{1,0:T(8,128)(2,1)}, bf16[128,1024]{1,0:T(8,128)(2,1)S(1)}, u32[]{:S(2)}, u32[]{:S(2)}) collective-permute-start(bf16[128,1024]{1,0:T(8,128)(2,1)} %get-tuple-element.159), channel_id=1, source_target_pairs={{0,8},{4,12},{8,16},{12,20},{16,24},{20,28},{24,0},{28,4},{1,9},{5... | collective-permute-start | bytes 786440 | tf_op jit(solution)/shard_map/ppermute | solution.py:88
  10.6 40.3 %collective-permute-start.13 = (bf16[128,1024]{1,0:T(8,128)(2,1)}, bf16[128,1024]{1,0:T(8,128)(2,1)S(1)}, u32[]{:S(2)}, u32[]{:S(2)}) collective-permute-start(bf16[128,1024]{1,0:T(8,128)(2,1)} %get-tuple-element.159), channel_id=1, source_target_pairs={{0,16},{4,20},{8,24},{12,28},{16,0},{20,4},{24,8},{28,12},{1,17},{... | collective-permute-start | bytes 786440 | tf_op jit(solution)/shard_map/ppermute | solution.py:88
  16.0 11.8 %collective-permute-start = (bf16[1,16,128]{2,1,0:T(8,128)(2,1)S(1)}, bf16[1,16,128]{2,1,0:T(8,128)(2,1)S(1)}, u32[]{:S(2)}, u32[]{:S(2)}) collective-permute-start(bf16[1,16,128]{2,1,0:T(8,128)(2,1)S(1)} %pad_bitcast_fusion), channel_id=1, source_target_pairs={{0,1},{1,2},{2,3},{3,0},{4,5},{5,6},{6,7},{7,4},{8,9},{9,10},{10,1... | collective-permute-start | bytes 12296 | tf_op jit(solution)/shard_map/ppermute | solution.py:122
  17.6 10.3 %collective-permute-start.1 = (bf16[1,16,128]{2,1,0:T(8,128)(2,1)S(1)}, bf16[1,16,128]{2,1,0:T(8,128)(2,1)S(1)}, u32[]{:S(2)}, u32[]{:S(2)}) collective-permute-start(bf16[1,16,128]{2,1,0:T(8,128)(2,1)S(1)} %pad_bitcast_fusion), channel_id=1, source_target_pairs={{0,2},{1,3},{2,0},{3,1},{4,6},{5,7},{6,4},{7,5},{8,10},{9,11},{10,... | collective-permute-start | bytes 12296 | tf_op jit(solution)/shard_map/ppermute | solution.py:122
  27.9 3.1 collective-permute-start.2
  31.2 4.0 %collective-permute-start.4 = (bf16[1,4,16,128]{3,2,1,0:T(8,128)(2,1)S(1)}, bf16[1,4,16,128]{3,2,1,0:T(8,128)(2,1)S(1)}, u32[]{:S(2)}, u32[]{:S(2)}) collective-permute-start(bf16[1,4,16,128]{3,2,1,0:T(8,128)(2,1)S(1)} %constant_dynamic-update-slice_fusion.105), channel_id=1, source_target_pairs={{0,8},{4,12},{8,16},{12,20},{16,24},{20,28},{24,0},{28,4},{1,9},{5... | collective-permute-start | bytes 49160 | tf_op jit(solution)/shard_map/ppermute | solution.py:88
  33.6 3.5 %collective-permute-start.6 = (bf16[1,4,16,128]{3,2,1,0:T(8,128)(2,1)S(1)}, bf16[1,4,16,128]{3,2,1,0:T(8,128)(2,1)S(1)}, u32[]{:S(2)}, u32[]{:S(2)}) collective-permute-start(bf16[1,4,16,128]{3,2,1,0:T(8,128)(2,1)S(1)} %constant_dynamic-update-slice_fusion.105), channel_id=1, source_target_pairs={{0,16},{4,20},{8,24},{12,28},{16,0},{20,4},{24,8},{28,12},{1,17},{... | collective-permute-start | bytes 49160 | tf_op jit(solution)/shard_map/ppermute | solution.py:88
  35.2 3.4 %collective-permute-start.5 = (bf16[1,4,16,128]{3,2,1,0:T(8,128)(2,1)S(1)}, bf16[1,4,16,128]{3,2,1,0:T(8,128)(2,1)S(1)}, u32[]{:S(2)}, u32[]{:S(2)}) collective-permute-start(bf16[1,4,16,128]{3,2,1,0:T(8,128)(2,1)S(1)} %collective-permute-done.4), channel_id=1, source_target_pairs={{0,4},{4,0},{8,12},{12,8},{16,20},{20,16},{24,28},{28,24},{1,5},{5... | collective-permute-start | bytes 49160 | tf_op jit(solution)/shard_map/ppermute | solution.py:83
  39.7 13.3 %collective-permute-start.15 = (bf16[128,1024]{1,0:T(8,128)(2,1)}, bf16[128,1024]{1,0:T(8,128)(2,1)S(1)}, u32[]{:S(2)}, u32[]{:S(2)}) collective-permute-start(bf16[128,1024]{1,0:T(8,128)(2,1)} %get-tuple-element.159), channel_id=1, source_target_pairs={{0,24},{4,28},{8,0},{12,4},{16,8},{20,12},{24,16},{28,20},{1,25},{... | collective-permute-start | bytes 786440 | tf_op jit(solution)/shard_map/ppermute | solution.py:88
  44.0 41.1 %collective-permute-start.23 = (bf16[3,128,704]{1,2,0:T(8,128)(2,1)}, bf16[3,128,704]{1,2,0:T(8,128)(2,1)}, u32[]{:S(2)}, u32[]{:S(2)}) collective-permute-start(bf16[3,128,704]{1,2,0:T(8,128)(2,1)} %get-tuple-element.110), channel_id=1, source_target_pairs={{0,4},{4,0},{8,12},{12,8},{16,20},{20,16},{24,28},{28,24},{1,5},{5... | collective-permute-start | bytes 1622024 | tf_op jit(solution)/shard_map/ppermute | solution.py:83
  47.7 12.7 %collective-permute-start.12 = (bf16[128,1024]{1,0:T(8,128)(2,1)S(1)}, bf16[128,1024]{1,0:T(8,128)(2,1)S(1)}, u32[]{:S(2)}, u32[]{:S(2)}) collective-permute-start(bf16[128,1024]{1,0:T(8,128)(2,1)S(1)} %collective-permute-done.11), channel_id=1, source_target_pairs={{0,4},{4,0},{8,12},{12,8},{16,20},{20,16},{24,28},{28,24},{1,5},{5... | collective-permute-start | bytes 786440 | tf_op jit(solution)/shard_map/ppermute | solution.py:83
  50.9 34.2 %collective-permute-start.24 = (bf16[3,128,704]{1,2,0:T(8,128)(2,1)}, bf16[3,128,704]{1,2,0:T(8,128)(2,1)S(1)}, u32[]{:S(2)}, u32[]{:S(2)}) collective-permute-start(bf16[3,128,704]{1,2,0:T(8,128)(2,1)} %get-tuple-element.110), channel_id=1, source_target_pairs={{0,8},{4,12},{8,16},{12,20},{16,24},{20,28},{24,0},{28,4},{1,9},{5... | collective-permute-start | bytes 1622024 | tf_op jit(solution)/shard_map/ppermute | solution.py:88
  50.9 15.0 %collective-permute-start.14 = (bf16[128,1024]{1,0:T(8,128)(2,1)S(1)}, bf16[128,1024]{1,0:T(8,128)(2,1)S(1)}, u32[]{:S(2)}, u32[]{:S(2)}) collective-permute-start(bf16[128,1024]{1,0:T(8,128)(2,1)S(1)} %collective-permute-done.13), channel_id=1, source_target_pairs={{0,4},{4,0},{8,12},{12,8},{16,20},{20,16},{24,28},{28,24},{1,5},{5... | collective-permute-start | bytes 786440 | tf_op jit(solution)/shard_map/ppermute | solution.py:83
  52.9 41.4 %collective-permute-start.26 = (bf16[3,128,704]{1,2,0:T(8,128)(2,1)}, bf16[3,128,704]{1,2,0:T(8,128)(2,1)S(1)}, u32[]{:S(2)}, u32[]{:S(2)}) collective-permute-start(bf16[3,128,704]{1,2,0:T(8,128)(2,1)} %get-tuple-element.110), channel_id=1, source_target_pairs={{0,16},{4,20},{8,24},{12,28},{16,0},{20,4},{24,8},{28,12},{1,17},{... | collective-permute-start | bytes 1622024 | tf_op jit(solution)/shard_map/ppermute | solution.py:88
  60.4 11.1 %collective-permute-start.16 = (bf16[128,1024]{1,0:T(8,128)(2,1)S(1)}, bf16[128,1024]{1,0:T(8,128)(2,1)S(1)}, u32[]{:S(2)}, u32[]{:S(2)}) collective-permute-start(bf16[128,1024]{1,0:T(8,128)(2,1)S(1)} %collective-permute-done.15), channel_id=1, source_target_pairs={{0,4},{4,0},{8,12},{12,8},{16,20},{20,16},{24,28},{28,24},{1,5},{5... | collective-permute-start | bytes 786440 | tf_op jit(solution)/shard_map/ppermute | solution.py:83
  65.9 38.4 %collective-permute-start.28 = (bf16[3,128,704]{1,2,0:T(8,128)(2,1)}, bf16[3,128,704]{1,2,0:T(8,128)(2,1)S(1)}, u32[]{:S(2)}, u32[]{:S(2)}) collective-permute-start(bf16[3,128,704]{1,2,0:T(8,128)(2,1)} %get-tuple-element.110), channel_id=1, source_target_pairs={{0,24},{4,28},{8,0},{12,4},{16,8},{20,12},{24,16},{28,20},{1,25},{... | collective-permute-start | bytes 1622024 | tf_op jit(solution)/shard_map/ppermute | solution.py:88
  78.2 26.8 %collective-permute-start.19 = (bf16[64,1024]{1,0:T(8,128)(2,1)S(1)}, bf16[64,1024]{1,0:T(8,128)(2,1)S(1)}, u32[]{:S(2)}, u32[]{:S(2)}) collective-permute-start(bf16[64,1024]{1,0:T(8,128)(2,1)S(1)} %get-tuple-element.144), channel_id=1, source_target_pairs={{0,3},{1,0},{2,1},{3,2},{4,7},{5,4},{6,5},{7,6},{8,11},{9,8},{10,9... | collective-permute-start | bytes 393224 | tf_op jit(solution)/shard_map/ppermute | solution.py:122
  85.1 20.7 %collective-permute-start.18 = (bf16[64,1024]{1,0:T(8,128)(2,1)S(1)}, bf16[64,1024]{1,0:T(8,128)(2,1)S(1)}, u32[]{:S(2)}, u32[]{:S(2)}) collective-permute-start(bf16[64,1024]{1,0:T(8,128)(2,1)S(1)} %get-tuple-element.145), channel_id=1, source_target_pairs={{0,2},{1,3},{2,0},{3,1},{4,6},{5,7},{6,4},{7,5},{8,10},{9,11},{10,... | collective-permute-start | bytes 393224 | tf_op jit(solution)/shard_map/ppermute | solution.py:122
  85.1 20.7 %collective-permute-start.17 = (bf16[64,1024]{1,0:T(8,128)(2,1)S(1)}, bf16[64,1024]{1,0:T(8,128)(2,1)S(1)}, u32[]{:S(2)}, u32[]{:S(2)}) collective-permute-start(bf16[64,1024]{1,0:T(8,128)(2,1)S(1)} %get-tuple-element.143), channel_id=1, source_target_pairs={{0,1},{1,2},{2,3},{3,0},{4,5},{5,6},{6,7},{7,4},{8,9},{9,10},{10,1... | collective-permute-start | bytes 393224 | tf_op jit(solution)/shard_map/ppermute | solution.py:122
  94.4 21.2 %collective-permute-start.25 = (bf16[3,128,704]{1,2,0:T(8,128)(2,1)S(1)}, bf16[3,128,704]{1,2,0:T(8,128)(2,1)S(1)}, u32[]{:S(2)}, u32[]{:S(2)}) collective-permute-start(bf16[3,128,704]{1,2,0:T(8,128)(2,1)S(1)} %collective-permute-done.24), channel_id=1, source_target_pairs={{0,4},{4,0},{8,12},{12,8},{16,20},{20,16},{24,28},{28,24},{1,5},{5... | collective-permute-start | bytes 1622024 | tf_op jit(solution)/shard_map/ppermute | solution.py:83
  104.4 14.4 %collective-permute-start.27 = (bf16[3,128,704]{1,2,0:T(8,128)(2,1)S(1)}, bf16[3,128,704]{1,2,0:T(8,128)(2,1)S(1)}, u32[]{:S(2)}, u32[]{:S(2)}) collective-permute-start(bf16[3,128,704]{1,2,0:T(8,128)(2,1)S(1)} %collective-permute-done.26), channel_id=1, source_target_pairs={{0,4},{4,0},{8,12},{12,8},{16,20},{20,16},{24,28},{28,24},{1,5},{5... | collective-permute-start | bytes 1622024 | tf_op jit(solution)/shard_map/ppermute | solution.py:83
  105.0 25.3 %collective-permute-start.29 = (bf16[3,128,704]{1,2,0:T(8,128)(2,1)S(1)}, bf16[3,128,704]{1,2,0:T(8,128)(2,1)S(1)}, u32[]{:S(2)}, u32[]{:S(2)}) collective-permute-start(bf16[3,128,704]{1,2,0:T(8,128)(2,1)S(1)} %collective-permute-done.28), channel_id=1, source_target_pairs={{0,4},{4,0},{8,12},{12,8},{16,20},{20,16},{24,28},{28,24},{1,5},{5... | collective-permute-start | bytes 1622024 | tf_op jit(solution)/shard_map/ppermute | solution.py:83
  106.4 8.5 %collective-permute-start.21 = (bf16[64,1024]{1,0:T(8,128)(2,1)S(1)}, bf16[64,1024]{1,0:T(8,128)(2,1)S(1)}, u32[]{:S(2)}, u32[]{:S(2)}) collective-permute-start(bf16[64,1024]{1,0:T(8,128)(2,1)S(1)} %get-tuple-element.68), channel_id=1, source_target_pairs={{0,2},{1,3},{2,0},{3,1},{4,6},{5,7},{6,4},{7,5},{8,10},{9,11},{10,... | collective-permute-start | bytes 393224 | tf_op jit(solution)/shard_map/ppermute | solution.py:122
  109.2 6.3 %collective-permute-start.22 = (bf16[64,1024]{1,0:T(8,128)(2,1)S(1)}, bf16[64,1024]{1,0:T(8,128)(2,1)S(1)}, u32[]{:S(2)}, u32[]{:S(2)}) collective-permute-start(bf16[64,1024]{1,0:T(8,128)(2,1)S(1)} %get-tuple-element.68), channel_id=1, source_target_pairs={{0,3},{1,0},{2,1},{3,2},{4,7},{5,4},{6,5},{7,6},{8,11},{9,8},{10,9... | collective-permute-start | bytes 393224 | tf_op jit(solution)/shard_map/ppermute | solution.py:122
  134.9 17.5 %collective-permute-start.32 = (bf16[64,1024]{1,0:T(8,128)(2,1)S(1)}, bf16[64,1024]{1,0:T(8,128)(2,1)S(1)}, u32[]{:S(2)}, u32[]{:S(2)}) collective-permute-start(bf16[64,1024]{1,0:T(8,128)(2,1)S(1)} %get-tuple-element.141), channel_id=1, source_target_pairs={{0,3},{1,0},{2,1},{3,2},{4,7},{5,4},{6,5},{7,6},{8,11},{9,8},{10,9... | collective-permute-start | bytes 393224 | tf_op jit(solution)/shard_map/ppermute | solution.py:122
  136.8 16.0 %collective-permute-start.31 = (bf16[64,1024]{1,0:T(8,128)(2,1)S(1)}, bf16[64,1024]{1,0:T(8,128)(2,1)S(1)}, u32[]{:S(2)}, u32[]{:S(2)}) collective-permute-start(bf16[64,1024]{1,0:T(8,128)(2,1)S(1)} %get-tuple-element.142), channel_id=1, source_target_pairs={{0,2},{1,3},{2,0},{3,1},{4,6},{5,7},{6,4},{7,5},{8,10},{9,11},{10,... | collective-permute-start | bytes 393224 | tf_op jit(solution)/shard_map/ppermute | solution.py:122
  138.0 10.3 %collective-permute-start.38 = (bf16[64,1024]{1,0:T(8,128)(2,1)S(1)}, bf16[64,1024]{1,0:T(8,128)(2,1)S(1)}, u32[]{:S(2)}, u32[]{:S(2)}) collective-permute-start(bf16[64,1024]{1,0:T(8,128)(2,1)S(1)} %get-tuple-element.137), channel_id=1, source_target_pairs={{0,3},{1,0},{2,1},{3,2},{4,7},{5,4},{6,5},{7,6},{8,11},{9,8},{10,9... | collective-permute-start | bytes 393224 | tf_op jit(solution)/shard_map/ppermute | solution.py:122
  138.3 10.0 %collective-permute-start.37 = (bf16[64,1024]{1,0:T(8,128)(2,1)S(1)}, bf16[64,1024]{1,0:T(8,128)(2,1)S(1)}, u32[]{:S(2)}, u32[]{:S(2)}) collective-permute-start(bf16[64,1024]{1,0:T(8,128)(2,1)S(1)} %get-tuple-element.138), channel_id=1, source_target_pairs={{0,2},{1,3},{2,0},{3,1},{4,6},{5,7},{6,4},{7,5},{8,10},{9,11},{10,... | collective-permute-start | bytes 393224 | tf_op jit(solution)/shard_map/ppermute | solution.py:122
  139.9 9.3 %collective-permute-start.36 = (bf16[64,1024]{1,0:T(8,128)(2,1)S(1)}, bf16[64,1024]{1,0:T(8,128)(2,1)S(1)}, u32[]{:S(2)}, u32[]{:S(2)}) collective-permute-start(bf16[64,1024]{1,0:T(8,128)(2,1)S(1)} %get-tuple-element.136), channel_id=1, source_target_pairs={{0,1},{1,2},{2,3},{3,0},{4,5},{5,6},{6,7},{7,4},{8,9},{9,10},{10,1... | collective-permute-start | bytes 393224 | tf_op jit(solution)/shard_map/ppermute | solution.py:122
  148.3 4.6 %collective-permute-start.30 = (bf16[64,1024]{1,0:T(8,128)(2,1)S(1)}, bf16[64,1024]{1,0:T(8,128)(2,1)S(1)}, u32[]{:S(2)}, u32[]{:S(2)}) collective-permute-start(bf16[64,1024]{1,0:T(8,128)(2,1)S(1)} %get-tuple-element.140), channel_id=1, source_target_pairs={{0,1},{1,2},{2,3},{3,0},{4,5},{5,6},{6,7},{7,4},{8,9},{9,10},{10,1... | collective-permute-start | bytes 393224 | tf_op jit(solution)/shard_map/ppermute | solution.py:122
  148.3 98.5 %collective-permute-start.70 = (bf16[3,128,704]{1,2,0:T(8,128)(2,1)}, bf16[3,128,704]{1,2,0:T(8,128)(2,1)}, u32[]{:S(2)}, u32[]{:S(2)}) collective-permute-start(bf16[3,128,704]{1,2,0:T(8,128)(2,1)} %pad_maximum_fusion.4), channel_id=1, source_target_pairs={{0,4},{4,0},{8,12},{12,8},{16,20},{20,16},{24,28},{28,24},{1,5},{5... | collective-permute-start | bytes 1622024 | tf_op jit(solution)/shard_map/ppermute | solution.py:83
  150.8 5.6 %collective-permute-start.39 = (bf16[64,1024]{1,0:T(8,128)(2,1)}, bf16[64,1024]{1,0:T(8,128)(2,1)S(1)}, u32[]{:S(2)}, u32[]{:S(2)}) collective-permute-start(bf16[64,1024]{1,0:T(8,128)(2,1)} %get-tuple-element.63), channel_id=1, source_target_pairs={{0,1},{1,2},{2,3},{3,0},{4,5},{5,6},{6,7},{7,4},{8,9},{9,10},{10,1... | collective-permute-start | bytes 393224 | tf_op jit(solution)/shard_map/ppermute | solution.py:122
  152.4 7.1 %collective-permute-start.40 = (bf16[64,1024]{1,0:T(8,128)(2,1)}, bf16[64,1024]{1,0:T(8,128)(2,1)S(1)}, u32[]{:S(2)}, u32[]{:S(2)}) collective-permute-start(bf16[64,1024]{1,0:T(8,128)(2,1)} %get-tuple-element.63), channel_id=1, source_target_pairs={{0,2},{1,3},{2,0},{3,1},{4,6},{5,7},{6,4},{7,5},{8,10},{9,11},{10,... | collective-permute-start | bytes 393224 | tf_op jit(solution)/shard_map/ppermute | solution.py:122
  153.7 16.0 %collective-permute-start.33 = (bf16[64,1024]{1,0:T(8,128)(2,1)}, bf16[64,1024]{1,0:T(8,128)(2,1)}, u32[]{:S(2)}, u32[]{:S(2)}) collective-permute-start(bf16[64,1024]{1,0:T(8,128)(2,1)} %get-tuple-element.66), channel_id=1, source_target_pairs={{0,1},{1,2},{2,3},{3,0},{4,5},{5,6},{6,7},{7,4},{8,9},{9,10},{10,1... | collective-permute-start | bytes 393224 | tf_op jit(solution)/shard_map/ppermute | solution.py:122
  154.0 16.6 %collective-permute-start.34 = (bf16[64,1024]{1,0:T(8,128)(2,1)}, bf16[64,1024]{1,0:T(8,128)(2,1)}, u32[]{:S(2)}, u32[]{:S(2)}) collective-permute-start(bf16[64,1024]{1,0:T(8,128)(2,1)} %get-tuple-element.66), channel_id=1, source_target_pairs={{0,2},{1,3},{2,0},{3,1},{4,6},{5,7},{6,4},{7,5},{8,10},{9,11},{10,... | collective-permute-start | bytes 393224 | tf_op jit(solution)/shard_map/ppermute | solution.py:122
  156.4 6.6 %collective-permute-start.41 = (bf16[64,1024]{1,0:T(8,128)(2,1)}, bf16[64,1024]{1,0:T(8,128)(2,1)S(1)}, u32[]{:S(2)}, u32[]{:S(2)}) collective-permute-start(bf16[64,1024]{1,0:T(8,128)(2,1)} %get-tuple-element.63), channel_id=1, source_target_pairs={{0,3},{1,0},{2,1},{3,2},{4,7},{5,4},{6,5},{7,6},{8,11},{9,8},{10,9... | collective-permute-start | bytes 393224 | tf_op jit(solution)/shard_map/ppermute | solution.py:122
  159.5 12.1 %collective-permute-start.35 = (bf16[64,1024]{1,0:T(8,128)(2,1)}, bf16[64,1024]{1,0:T(8,128)(2,1)S(1)}, u32[]{:S(2)}, u32[]{:S(2)}) collective-permute-start(bf16[64,1024]{1,0:T(8,128)(2,1)} %get-tuple-element.66), channel_id=1, source_target_pairs={{0,3},{1,0},{2,1},{3,2},{4,7},{5,4},{6,5},{7,6},{8,11},{9,8},{10,9... | collective-permute-start | bytes 393224 | tf_op jit(solution)/shard_map/ppermute | solution.py:122
  178.3 16.1 %collective-permute-start.44 = (bf16[64,1024]{1,0:T(8,128)(2,1)}, bf16[64,1024]{1,0:T(8,128)(2,1)}, u32[]{:S(2)}, u32[]{:S(2)}) collective-permute-start(bf16[64,1024]{1,0:T(8,128)(2,1)} %get-tuple-element.134), channel_id=1, source_target_pairs={{0,3},{1,0},{2,1},{3,2},{4,7},{5,4},{6,5},{7,6},{8,11},{9,8},{10,9... | collective-permute-start | bytes 393224 | tf_op jit(solution)/shard_map/ppermute | solution.py:122
  178.3 16.1 %collective-permute-start.43 = (bf16[64,1024]{1,0:T(8,128)(2,1)}, bf16[64,1024]{1,0:T(8,128)(2,1)}, u32[]{:S(2)}, u32[]{:S(2)}) collective-permute-start(bf16[64,1024]{1,0:T(8,128)(2,1)} %get-tuple-element.135), channel_id=1, source_target_pairs={{0,2},{1,3},{2,0},{3,1},{4,6},{5,7},{6,4},{7,5},{8,10},{9,11},{10,... | collective-permute-start | bytes 393224 | tf_op jit(solution)/shard_map/ppermute | solution.py:122
  179.3 15.1 %collective-permute-start.42 = (bf16[64,1024]{1,0:T(8,128)(2,1)}, bf16[64,1024]{1,0:T(8,128)(2,1)}, u32[]{:S(2)}, u32[]{:S(2)}) collective-permute-start(bf16[64,1024]{1,0:T(8,128)(2,1)} %get-tuple-element.133), channel_id=1, source_target_pairs={{0,1},{1,2},{2,3},{3,0},{4,5},{5,6},{6,7},{7,4},{8,9},{9,10},{10,1... | collective-permute-start | bytes 393224 | tf_op jit(solution)/shard_map/ppermute | solution.py:122
  196.9 3.6 %collective-permute-start.49 = (bf16[4,2048]{1,0:T(4,128)(2,1)S(1)}, bf16[4,2048]{1,0:T(4,128)(2,1)S(1)}, u32[]{:S(2)}, u32[]{:S(2)}) collective-permute-start(bf16[4,2048]{1,0:T(4,128)(2,1)S(1)} %get-tuple-element.153), channel_id=1, source_target_pairs={{0,4},{4,0},{8,12},{12,8},{16,20},{20,16},{24,28},{28,24},{1,5},{5... | collective-permute-start | bytes 49160 | tf_op jit(solution)/shard_map/ppermute | solution.py:83
  199.7 5.9 %collective-permute-start.48 = (bf16[4,2048]{1,0:T(4,128)(2,1)S(1)}, bf16[4,2048]{1,0:T(4,128)(2,1)S(1)}, u32[]{:S(2)}, u32[]{:S(2)}) collective-permute-start(bf16[4,2048]{1,0:T(4,128)(2,1)S(1)} %get-tuple-element.150), channel_id=1, source_target_pairs={{0,4},{4,0},{8,12},{12,8},{16,20},{20,16},{24,28},{28,24},{1,5},{5... | collective-permute-start | bytes 49160 | tf_op jit(solution)/shard_map/ppermute | solution.py:83
  201.0 5.3 %collective-permute-start.54 = (bf16[4,2048]{1,0:T(4,128)(2,1)S(1)}, bf16[4,2048]{1,0:T(4,128)(2,1)S(1)}, u32[]{:S(2)}, u32[]{:S(2)}) collective-permute-start(bf16[4,2048]{1,0:T(4,128)(2,1)S(1)} %get-tuple-element.158), channel_id=1, source_target_pairs={{0,8},{4,12},{8,16},{12,20},{16,24},{20,28},{24,0},{28,4},{1,9},{5... | collective-permute-start | bytes 49160 | tf_op jit(solution)/shard_map/ppermute | solution.py:88
  201.2 5.1 %collective-permute-start.52 = (bf16[4,2048]{1,0:T(4,128)(2,1)S(1)}, bf16[4,2048]{1,0:T(4,128)(2,1)S(1)}, u32[]{:S(2)}, u32[]{:S(2)}) collective-permute-start(bf16[4,2048]{1,0:T(4,128)(2,1)S(1)} %get-tuple-element.157), channel_id=1, source_target_pairs={{0,16},{4,20},{8,24},{12,28},{16,0},{20,4},{24,8},{28,12},{1,17},{... | collective-permute-start | bytes 49160 | tf_op jit(solution)/shard_map/ppermute | solution.py:88
  205.6 45.3 %collective-permute-start.68 = (bf16[3,128,704]{1,2,0:T(8,128)(2,1)}, bf16[3,128,704]{1,2,0:T(8,128)(2,1)S(1)}, u32[]{:S(2)}, u32[]{:S(2)}) collective-permute-start(bf16[3,128,704]{1,2,0:T(8,128)(2,1)} %pad_maximum_fusion.3), channel_id=1, source_target_pairs={{0,4},{4,0},{8,12},{12,8},{16,20},{20,16},{24,28},{28,24},{1,5},{5... | collective-permute-start | bytes 1622024 | tf_op jit(solution)/shard_map/ppermute | solution.py:83
  206.9 5.2 %collective-permute-start.57 = (bf16[1,2048]{1,0:T(2,128)(2,1)S(1)}, bf16[1,2048]{1,0:T(2,128)(2,1)S(1)}, u32[]{:S(2)}, u32[]{:S(2)}) collective-permute-start(bf16[1,2048]{1,0:T(2,128)(2,1)S(1)} %get-tuple-element.170), channel_id=1, source_target_pairs={{0,3},{1,0},{2,1},{3,2},{4,7},{5,4},{6,5},{7,6},{8,11},{9,8},{10,9... | collective-permute-start | bytes 12296 | tf_op jit(solution)/shard_map/ppermute | solution.py:122
  209.2 3.8 %collective-permute-start.56 = (bf16[1,2048]{1,0:T(2,128)(2,1)S(1)}, bf16[1,2048]{1,0:T(2,128)(2,1)S(1)}, u32[]{:S(2)}, u32[]{:S(2)}) collective-permute-start(bf16[1,2048]{1,0:T(2,128)(2,1)S(1)} %get-tuple-element.171), channel_id=1, source_target_pairs={{0,2},{1,3},{2,0},{3,1},{4,6},{5,7},{6,4},{7,5},{8,10},{9,11},{10,... | collective-permute-start | bytes 12296 | tf_op jit(solution)/shard_map/ppermute | solution.py:122
  210.1 3.6 %collective-permute-start.55 = (bf16[1,2048]{1,0:T(2,128)(2,1)S(1)}, bf16[1,2048]{1,0:T(2,128)(2,1)S(1)}, u32[]{:S(2)}, u32[]{:S(2)}) collective-permute-start(bf16[1,2048]{1,0:T(2,128)(2,1)S(1)} %get-tuple-element.169), channel_id=1, source_target_pairs={{0,1},{1,2},{2,3},{3,0},{4,5},{5,6},{6,7},{7,4},{8,9},{9,10},{10,1... | collective-permute-start | bytes 12296 | tf_op jit(solution)/shard_map/ppermute | solution.py:122
  212.1 39.8 %collective-permute-start.66 = (bf16[3,128,704]{1,2,0:T(8,128)(2,1)}, bf16[3,128,704]{1,2,0:T(8,128)(2,1)}, u32[]{:S(2)}, u32[]{:S(2)}) collective-permute-start(bf16[3,128,704]{1,2,0:T(8,128)(2,1)} %pad_maximum_fusion.2), channel_id=1, source_target_pairs={{0,4},{4,0},{8,12},{12,8},{16,20},{20,16},{24,28},{28,24},{1,5},{5... | collective-permute-start | bytes 1622024 | tf_op jit(solution)/shard_map/ppermute | solution.py:83
  213.0 4.7 %collective-permute-start.45 = (bf16[64,1024]{1,0:T(8,128)(2,1)S(1)}, bf16[64,1024]{1,0:T(8,128)(2,1)S(1)}, u32[]{:S(2)}, u32[]{:S(2)}) collective-permute-start(bf16[64,1024]{1,0:T(8,128)(2,1)S(1)} %get-tuple-element.59), channel_id=1, source_target_pairs={{0,1},{1,2},{2,3},{3,0},{4,5},{5,6},{6,7},{7,4},{8,9},{9,10},{10,1... | collective-permute-start | bytes 393224 | tf_op jit(solution)/shard_map/ppermute | solution.py:122
  213.8 6.0 %collective-permute-start.46 = (bf16[64,1024]{1,0:T(8,128)(2,1)S(1)}, bf16[64,1024]{1,0:T(8,128)(2,1)S(1)}, u32[]{:S(2)}, u32[]{:S(2)}) collective-permute-start(bf16[64,1024]{1,0:T(8,128)(2,1)S(1)} %get-tuple-element.59), channel_id=1, source_target_pairs={{0,2},{1,3},{2,0},{3,1},{4,6},{5,7},{6,4},{7,5},{8,10},{9,11},{10,... | collective-permute-start | bytes 393224 | tf_op jit(solution)/shard_map/ppermute | solution.py:122
  217.6 4.7 %collective-permute-start.47 = (bf16[64,1024]{1,0:T(8,128)(2,1)S(1)}, bf16[64,1024]{1,0:T(8,128)(2,1)S(1)}, u32[]{:S(2)}, u32[]{:S(2)}) collective-permute-start(bf16[64,1024]{1,0:T(8,128)(2,1)S(1)} %get-tuple-element.59), channel_id=1, source_target_pairs={{0,3},{1,0},{2,1},{3,2},{4,7},{5,4},{6,5},{7,6},{8,11},{9,8},{10,9... | collective-permute-start | bytes 393224 | tf_op jit(solution)/shard_map/ppermute | solution.py:122
  219.7 15.4 %collective-permute-start.63 = (bf16[128,1024]{0,1:T(8,128)(2,1)}, bf16[128,1024]{0,1:T(8,128)(2,1)S(1)}, u32[]{:S(2)}, u32[]{:S(2)}) collective-permute-start(bf16[128,1024]{0,1:T(8,128)(2,1)} %pad_maximum_fusion.9), channel_id=1, source_target_pairs={{0,4},{4,0},{8,12},{12,8},{16,20},{20,16},{24,28},{28,24},{1,5},{5... | collective-permute-start | bytes 786440 | tf_op jit(solution)/shard_map/ppermute | solution.py:83
  222.3 18.4 %collective-permute-start.61 = (bf16[128,1024]{0,1:T(8,128)(2,1)}, bf16[128,1024]{0,1:T(8,128)(2,1)S(1)}, u32[]{:S(2)}, u32[]{:S(2)}) collective-permute-start(bf16[128,1024]{0,1:T(8,128)(2,1)} %pad_maximum_fusion.8), channel_id=1, source_target_pairs={{0,4},{4,0},{8,12},{12,8},{16,20},{20,16},{24,28},{28,24},{1,5},{5... | collective-permute-start | bytes 786440 | tf_op jit(solution)/shard_map/ppermute | solution.py:83
  235.1 11.2 %collective-permute-start.59 = (bf16[128,1024]{0,1:T(8,128)(2,1)S(1)}, bf16[128,1024]{0,1:T(8,128)(2,1)S(1)}, u32[]{:S(2)}, u32[]{:S(2)}) collective-permute-start(bf16[128,1024]{0,1:T(8,128)(2,1)S(1)} %copy-done.27), channel_id=1, source_target_pairs={{0,4},{4,0},{8,12},{12,8},{16,20},{20,16},{24,28},{28,24},{1,5},{5... | collective-permute-start | bytes 786440 | tf_op jit(solution)/shard_map/ppermute | solution.py:83
  240.7 12.9 %collective-permute-start.58 = (bf16[128,1024]{0,1:T(8,128)(2,1)S(1)}, bf16[128,1024]{0,1:T(8,128)(2,1)S(1)}, u32[]{:S(2)}, u32[]{:S(2)}) collective-permute-start(bf16[128,1024]{0,1:T(8,128)(2,1)S(1)} %copy-done.26), channel_id=1, source_target_pairs={{0,4},{4,0},{8,12},{12,8},{16,20},{20,16},{24,28},{28,24},{1,5},{5... | collective-permute-start | bytes 786440 | tf_op jit(solution)/shard_map/ppermute | solution.py:83
  246.4 8.8 %collective-permute-start.64 = (bf16[128,1024]{0,1:T(8,128)(2,1)S(1)}, bf16[128,1024]{0,1:T(8,128)(2,1)S(1)}, u32[]{:S(2)}, u32[]{:S(2)}) collective-permute-start(bf16[128,1024]{0,1:T(8,128)(2,1)S(1)} %add_convert_fusion.3), channel_id=1, source_target_pairs={{0,8},{4,12},{8,16},{12,20},{16,24},{20,28},{24,0},{28,4},{1,9},{5... | collective-permute-start | bytes 786440 | tf_op jit(solution)/shard_map/ppermute | solution.py:88
  246.8 14.2 %collective-permute-start.62 = (bf16[128,1024]{0,1:T(8,128)(2,1)S(1)}, bf16[128,1024]{0,1:T(8,128)(2,1)S(1)}, u32[]{:S(2)}, u32[]{:S(2)}) collective-permute-start(bf16[128,1024]{0,1:T(8,128)(2,1)S(1)} %add_convert_fusion.4), channel_id=1, source_target_pairs={{0,16},{4,20},{8,24},{12,28},{16,0},{20,4},{24,8},{28,12},{1,17},{... | collective-permute-start | bytes 786440 | tf_op jit(solution)/shard_map/ppermute | solution.py:88
  250.9 44.6 %collective-permute-start.60 = (bf16[128,1024]{0,1:T(8,128)(2,1)S(1)}, bf16[128,1024]{0,1:T(8,128)(2,1)S(1)}, u32[]{:S(2)}, u32[]{:S(2)}) collective-permute-start(bf16[128,1024]{0,1:T(8,128)(2,1)S(1)} %add_convert_fusion.5), channel_id=1, source_target_pairs={{0,24},{4,28},{8,0},{12,4},{16,8},{20,12},{24,16},{28,20},{1,25},{... | collective-permute-start | bytes 786440 | tf_op jit(solution)/shard_map/ppermute | solution.py:88
  251.9 47.6 %collective-permute-start.65 = (bf16[3,128,704]{1,2,0:T(8,128)(2,1)}, bf16[3,128,704]{1,2,0:T(8,128)(2,1)S(1)}, u32[]{:S(2)}, u32[]{:S(2)}) collective-permute-start(bf16[3,128,704]{1,2,0:T(8,128)(2,1)} %pad_maximum_fusion.1), channel_id=1, source_target_pairs={{0,4},{4,0},{8,12},{12,8},{16,20},{20,16},{24,28},{28,24},{1,5},{5... | collective-permute-start | bytes 1622024 | tf_op jit(solution)/shard_map/ppermute | solution.py:83
  253.6 47.1 %collective-permute-start.71 = (bf16[3,128,704]{1,2,0:T(8,128)(2,1)}, bf16[3,128,704]{1,2,0:T(8,128)(2,1)}, u32[]{:S(2)}, u32[]{:S(2)}) collective-permute-start(bf16[3,128,704]{1,2,0:T(8,128)(2,1)} %add_convert_fusion), channel_id=1, source_target_pairs={{0,8},{4,12},{8,16},{12,20},{16,24},{20,28},{24,0},{28,4},{1,9},{5... | collective-permute-start | bytes 1622024 | tf_op jit(solution)/shard_map/ppermute | solution.py:88
  255.1 57.2 %collective-permute-start.69 = (bf16[3,128,704]{1,2,0:T(8,128)(2,1)}, bf16[3,128,704]{1,2,0:T(8,128)(2,1)}, u32[]{:S(2)}, u32[]{:S(2)}) collective-permute-start(bf16[3,128,704]{1,2,0:T(8,128)(2,1)} %add_convert_fusion.1), channel_id=1, source_target_pairs={{0,16},{4,20},{8,24},{12,28},{16,0},{20,4},{24,8},{28,12},{1,17},{... | collective-permute-start | bytes 1622024 | tf_op jit(solution)/shard_map/ppermute | solution.py:88
  261.0 57.8 %collective-permute-start.67 = (bf16[3,128,704]{1,2,0:T(8,128)(2,1)S(1)}, bf16[3,128,704]{1,2,0:T(8,128)(2,1)}, u32[]{:S(2)}, u32[]{:S(2)}) collective-permute-start(bf16[3,128,704]{1,2,0:T(8,128)(2,1)S(1)} %add_convert_fusion.2), channel_id=1, source_target_pairs={{0,24},{4,28},{8,0},{12,4},{16,8},{20,12},{24,16},{28,20},{1,25},{... | collective-permute-start | bytes 1622024 | tf_op jit(solution)/shard_map/ppermute | solution.py:88
  (74 other events, 1243.2 us)

commit v2 on v1

--- a/solution.py
+++ b/solution.py
@@ -53,6 +53,10 @@
     return normed * gate_three * jax.nn.sigmoid(gate_three)
 
 
+def after(value, *earlier):
+    return lax.optimization_barrier((value,) + earlier)[0]
+
+
 class Rows:
     def __init__(self):
         self.count = lax.axis_size("dp")
@@ -87,27 +91,41 @@
         perm = [(i, (i // 2 + step) % n * 2 + i % 2) for i in range(self.count)]
         return lax.ppermute(array, "dp", perm)
 
-    def gather(self, block, axis):
+    def gather(self, block, earlier=()):
         if not self.direct:
-            return lax.all_gather(block, "dp", axis=axis, tiled=True)
-        line = [block] + [self.shift(block, s) for s in range(1, self.outer)]
-        pieces = []
+            every = lax.all_gather(block, "dp", axis=0, tiled=False)
+            return [every[i] for i in range(self.count)], [every]
+        line = [block]
+        for s in range(1, self.outer):
+            gate = earlier[s - 1 : s] if len(earlier) >= s else ()
+            line.append(self.shift(after(block, *gate), s))
+        pieces, order = [], line[1:]
         for item in line:
-            pieces += [item, self.pair(item)]
-        return jnp.concatenate(pieces, axis=axis)
-
-    def scatter(self, blocks):
+            other = self.pair(item)
+            pieces += [item, other]
+            order.append(other)
+        return pieces, order
+
+    def pair_sums(self, blocks):
         if not self.direct:
-            stacked = jnp.stack([blocks(i).astype(F32) for i in range(self.count)])
-            return lax.psum_scatter(stacked, "dp", scatter_dimension=0, tiled=False)
-        sums = []
-        for s in range(self.outer):
+            return [blocks(i).astype(F32) for i in range(self.count)], []
+        sums, arrived = {}, []
+        for s in list(range(1, self.outer)) + [0]:
             got = self.pair(blocks(2 * s + 1).astype(BF))
-            sums.append(blocks(2 * s).astype(F32) + got.astype(F32))
+            sums[s] = blocks(2 * s).astype(F32) + got.astype(F32)
+            if s:
+                sums[s] = sums[s].astype(BF)
+            arrived.append(sums[s])
+        return [sums[s] for s in range(self.outer)], arrived
+
+    def line_sum(self, sums):
+        if not self.direct:
+            return lax.psum_scatter(jnp.stack(sums), "dp", scatter_dimension=0), []
+        arrived = [self.shift(sums[s], -s) for s in range(1, self.outer)]
         total = sums[0]
-        for s in range(1, self.outer):
-            total = total + self.shift(sums[s].astype(BF), -s).astype(F32)
-        return total
+        for part in arrived:
+            total = total + part.astype(F32)
+        return total, arrived
 
 
 class Lanes:
@@ -175,7 +193,18 @@
     small_width = -(-small_total // 2048) * 2048
     flat = jnp.concatenate([part.reshape(-1) for part in small_parts])
     flat = jnp.pad(flat, (0, small_width - small_total)).reshape(1, 16, small_width // 16)
-    small_rel = rows.gather(lanes.gather(flat)[None], 0)
+    model_rows = w_query.shape[0]
+    pack_cols = 2 * key_cols + 3 * value_cols
+    small_rows = lanes.gather(flat).reshape(-1, pack_cols)
+    attn_pieces, attn_order = rows.gather(
+        jnp.concatenate(
+            [
+                jnp.concatenate([w_query, w_key, w_value, w_gate_out, w_output], axis=1),
+                small_rows,
+            ]
+        )
+    )
+    small_rel = jnp.stack([piece[model_rows:] for piece in attn_pieces])
     small_rel = small_rel.reshape(rows.count, lanes.count, small_width)
     small_abs = rows.relative(small_rel, 0)
 
@@ -193,21 +222,22 @@
     rank_out = lax.dynamic_slice_in_dim(rank_out_all, head_start, key_cols, 0)
     bias_local = lax.dynamic_slice_in_dim(bias_all, head_start, key_cols, 0).astype(F32)
 
-    attn_mat = rows.gather(
-        jnp.concatenate([w_query, w_key, w_value, w_gate_out, w_output], axis=1), 0
-    )
+    attn_mat = jnp.concatenate([piece[:model_rows] for piece in attn_pieces])
     in_cols = 2 * key_cols + 2 * value_cols
     in_mat, out_mat = attn_mat[:, :in_cols], attn_mat[:, in_cols:]
-    ffn_mat = rows.gather(jnp.stack([w_ffn_gate, w_ffn_up, w_ffn_down]), 1)
+    ffn_pieces, ffn_order = rows.gather(
+        jnp.stack([w_ffn_gate, w_ffn_up, w_ffn_down]), attn_order
+    )
+    ffn_mat = jnp.concatenate(ffn_pieces, axis=1)
     full_gate, full_up, full_down = ffn_mat[0], ffn_mat[1], ffn_mat[2]
 
     tokens_low = rows.relative(inputs.reshape(n_tok, model), 1)
-    dy_low = rows.relative(cotangent.reshape(n_tok, model), 1)
+    dy_low = rows.relative(after(cotangent, attn_order[-1]).reshape(n_tok, model), 1)
     tokens = tokens_low.astype(F32)
     own_tokens = lanes.own(tokens_low).astype(F32)
     own_dy = lanes.own(dy_low).astype(F32)
     normed_low = rms_gain(tokens, gain_in).astype(BF)
-    projected = dot(normed_low, in_mat)
+    projected = after(dot(normed_low, in_mat), *ffn_order[:1])
     qkv_low = projected[:, : in_cols - value_cols].astype(BF).astype(F32)
     gate_lin = projected[:, in_cols - value_cols :]
     rank_low = dot(normed_low, rank_in).astype(BF)
@@ -234,11 +264,11 @@
         heads(decays),
     )
     gated, gate_back = jax.vjp(head_gate, core_out, gate_lin, gain_head)
-    gated_low = gated.reshape(n_tok, -1).astype(BF)
+    gated_low = after(gated.reshape(n_tok, -1).astype(BF), *ffn_order[1:2])
     own_attended = lanes.scatter(dot_rt(gated_low, out_mat))
     own_middle = own_tokens + own_attended
     own_mid, norm_mid_back = jax.vjp(rms_gain, own_middle, gain_mid)
-    mid_low = lanes.gather(own_mid.astype(BF))
+    mid_low = lanes.gather(after(own_mid.astype(BF), *ffn_order[2:4]))
     d_hidden = dot(dy_low, full_down)
     gate_act = dot(mid_low, full_gate)
     up_act = dot(mid_low, full_up)
@@ -248,7 +278,6 @@
     d_gate_low = (d_hidden * up_act * sigma * (1.0 + gate_act * (1.0 - sigma))).astype(BF)
     d_up_low = (d_hidden * gate_act * sigma).astype(BF)
     own_d_mid = lanes.scatter(dot_rt(d_gate_low, full_gate) + dot_rt(d_up_low, full_up))
-    own_output = own_middle + lanes.scatter(dot_rt(hidden_low, full_down))
     grad_down = dot_t(dy_low, hidden_low).astype(BF)
     grad_gate = dot_t(mid_low, d_gate_low).astype(BF)
     grad_up = dot_t(mid_low, d_up_low).astype(BF)
@@ -258,13 +287,14 @@
         part = slice(slot * block, (slot + 1) * block)
         return jnp.stack([grad_gate[part], grad_up[part], grad_down[part]])
 
-    ffn_grads = rows.scatter(ffn_block)
+    ffn_sums, ffn_pairs = rows.pair_sums(ffn_block)
     own_d_middle, grad_gain_mid = norm_mid_back(own_d_mid)
     own_d_middle = own_dy + own_d_middle
 
-    d_att_low = lanes.gather(own_d_middle.astype(BF))
+    d_att_low = after(lanes.gather(own_d_middle.astype(BF)), *ffn_pairs[:1])
     d_gated = dot(d_att_low, out_mat)
     d_core, d_gate_lin, grad_head = gate_back(heads(d_gated))
+    d_core = after(d_core, *ffn_pairs[1:2])
     d_queries, d_keys, d_values, d_decays = core_back(d_core)
     d_in_low = jnp.concatenate(
         [
@@ -278,14 +308,10 @@
     d_logit_low = (d_decays.reshape(n_tok, -1) * jax.nn.sigmoid(-logits) / gate_divisor).astype(BF)
     d_rank_low = dot(d_logit_low, rank_out).astype(BF)
     own_d_in = lanes.scatter(dot_rt(d_in_low, in_mat) + dot_rt(d_rank_low, rank_in))
-    grad_in = dot_t(normed_low, d_in_low).astype(BF)
+    ffn_grads, ffn_shifts = rows.line_sum(ffn_sums)
+    grad_in = dot_t(normed_low, after(d_in_low, *ffn_pairs[2:], *ffn_shifts[:1])).astype(BF)
     grad_out = dot_t(d_att_low, gated_low).astype(BF)
 
-    def attn_block(slot):
-        part = slice(slot * block, (slot + 1) * block)
-        return jnp.concatenate([grad_in[part], grad_out[part]], axis=1)
-
-    attn_grads = rows.scatter(attn_block)
     _, norm_in_back = jax.vjp(rms_gain, own_tokens, gain_in)
     own_d_tokens, grad_gain_in = norm_in_back(own_d_in)
     own_input_grad = own_d_middle + own_d_tokens
@@ -316,8 +342,20 @@
         axis=2,
     )
     small_grads = jnp.pad(small_grads, ((0, 0), (0, 0), (0, small_width - small_total)))
-    small_sum = rows.scatter(lambda slot: small_grads[slot])
-    small_own = lanes.scatter(small_sum).reshape(-1)
+    small_part = lanes.scatter(jnp.swapaxes(small_grads, 0, 1).astype(BF))[0]
+    small_part = small_part.astype(BF).reshape(rows.count, -1, pack_cols)
+
+    def attn_block(slot):
+        part = slice(slot * block, (slot + 1) * block)
+        mats = jnp.concatenate([grad_in[part], grad_out[part]], axis=1)
+        return jnp.concatenate([mats, small_part[slot]])
+
+    attn_sums, _ = rows.pair_sums(attn_block)
+    attn_grads, _ = rows.line_sum(attn_sums)
+    small_own = attn_grads[block:].reshape(-1)
+    attn_grads = attn_grads[:block]
+    late_hidden = after(hidden_low, own_d_in)
+    own_output = own_middle + lanes.scatter(dot_rt(late_hidden, full_down))
 
     def small_out(which, like):
         start = sum(small_sizes[:which])

time: 323 us -> 349 us (1.080)
  waiting for transfers between devices: 118 us -> 168 us
  starting transfers between devices: 97.4 us -> 58 us
  matrix products: 20.6 us -> 28.1 us
  local copies, waits for them, and re-layouts: 54.9 us -> 59.8 us
    ppermute x24 -> x16, waiting for transfers between devices: 44.4 us -> 82 us  [pair(): return lax.ppermute(array, 'dp', [(i, i ^ 1) for i in range(self.count)])]
    ppermute x18 -> x12, starting transfers between devices: 39.6 us -> 16.7 us  [shift(): return lax.ppermute(array, 'dp', perm)]
    ppermute x30, starting transfers between devices: 41.1 us -> 27.3 us  [send(): lax.ppermute(array, 'mp', [(i, (i + step) % self.count) for i in range(se...]
    ppermute x18 -> x12, waiting for transfers between devices: 57.6 us -> 65.2 us  [shift(): return lax.ppermute(array, 'dp', perm)]
    ppermute x30, waiting for transfers between devices: 15.5 us -> 20.4 us  [send(): lax.ppermute(array, 'mp', [(i, (i + step) % self.count) for i in range(se...]
    squeeze x0 -> x16, local copies, waits for them, and re-layouts: none -> 4.45 us  [attn_block(): return jnp.concatenate([mats, small_part[slot]])]
    dot_general x7, matrix products: 5.92 us -> 9.55 us  [dot(): return jnp.dot(left, right, preferred_element_type=F32)]
    unnamed x203 -> x234, local copies, waits for them, and re-layouts: 26.9 us -> 30.5 us
  transfers between devices with their start and end apart: 72 -> 58, of which waited for: 29 -> 34; matrix products, arithmetic and copies ran while one was open for 27% -> 27% of each run, Pallas kernels for 0% -> 0%
where the time goes in v2:
time: 349 us; the launch traced here: 347 us
  waiting for transfers between devices  168 us (48%)
  local copies, waits for them, and re-layouts  59.8 us (17%)
  starting transfers between devices  58 us (17%)
  other arithmetic  30.6 us (9%)
  matrix products  28.1 us (8%)
    ppermute x16, waiting for transfers between devices, pair(): return lax.ppermute(array, 'dp', [(i, i ^ 1) for i in range(self.count)])  82 us
    ppermute x12, waiting for transfers between devices, shift(): return lax.ppermute(array, 'dp', perm)  65.2 us
    unnamed x234, local copies, waits for them, and re-layouts  30.5 us
    ppermute x30, starting transfers between devices, send(): lax.ppermute(array, 'mp', [(i, (i + step) % self.count) for i in range(se...  27.3 us
    ppermute x30, waiting for transfers between devices, send(): lax.ppermute(array, 'mp', [(i, (i + step) % self.count) for i in range(se...  20.4 us
    ppermute x12, starting transfers between devices, shift(): return lax.ppermute(array, 'dp', perm)  16.7 us
    ppermute x16, starting transfers between devices, pair(): return lax.ppermute(array, 'dp', [(i, i ^ 1) for i in range(self.count)])  14 us
    dot_general x7, matrix products, dot_rt(): lax.dot_general(left, right, (((1,), (1,)), ((), ())), preferred_element_...  10.8 us
  transfers between devices with their start and end apart: 58, of which 34 were waited for; matrix products, arithmetic and copies ran while one was open for 27% of the time, Pallas kernels for 0%

profile of v2, /device:TPU:13, one launch (start us, length us, event | category | flops | bytes accessed | tf_op | source)
XLA Modules:
  0.0 346.6 jit_solution(9668375560496108896)
XLA Ops:
  2.3 2.8 concatenate.115
  5.9 1.2 collective-permute-start.1
  7.2 2.2 constant_dynamic-update-slice_fusion.41
  10.6 1.4 constant_dynamic-update-slice_fusion.12
  12.0 1.4 constant_dynamic-update-slice_fusion.11
  13.4 1.5 constant_dynamic-update-slice_fusion.10
  16.7 1.3 collective-permute-start.4
  19.0 1.5 collective-permute-start.8
  20.9 7.9 %collective-permute-done.3 = bf16[136,1024]{1,0:T(8,128)(2,1)S(1)} collective-permute-done((bf16[136,1024]{1,0:T(8,128)(2,1)S(1)}, bf16[136,1024]{1,0:T(8,128)(2,1)S(1)}, u32[]{:S(2)}, u32[]{:S(2)}) %collective-permute-start.3) | collective-permute-done | bytes 278560 | tf_op jit(solution)/shard_map/ppermute | solution.py:87
  28.9 11.8 %collective-permute-done.6 = bf16[136,1024]{1,0:T(8,128)(2,1)S(1)} collective-permute-done((bf16[136,1024]{1,0:T(8,128)(2,1)S(1)}, bf16[136,1024]{1,0:T(8,128)(2,1)S(1)}, u32[]{:S(2)}, u32[]{:S(2)}) %collective-permute-start.6) | collective-permute-done | bytes 278560 | tf_op jit(solution)/shard_map/ppermute | solution.py:92
  40.7 3.4 collective-permute-done.8
  44.2 1.3 collective-permute-start.5
  49.4 2.6 collective-permute-done.5
  53.1 4.9 %collective-permute-done.7 = bf16[136,1024]{1,0:T(8,128)(2,1)} collective-permute-done((bf16[136,1024]{1,0:T(8,128)(2,1)S(1)}, bf16[136,1024]{1,0:T(8,128)(2,1)}, u32[]{:S(2)}, u32[]{:S(2)}) %collective-permute-start.7) | collective-permute-done | bytes 278560 | tf_op jit(solution)/shard_map/ppermute | solution.py:87
  58.8 5.2 %collective-permute-done.9 = bf16[136,1024]{1,0:T(8,128)(2,1)S(1)} collective-permute-done((bf16[136,1024]{1,0:T(8,128)(2,1)S(1)}, bf16[136,1024]{1,0:T(8,128)(2,1)S(1)}, u32[]{:S(2)}, u32[]{:S(2)}) %collective-permute-start.9) | collective-permute-done | bytes 278560 | tf_op jit(solution)/shard_map/ppermute | solution.py:87
  69.1 1.7 slice_dynamic-update-slice_fusion.4
  70.8 1.7 slice_dynamic-update-slice_fusion.3
  72.5 1.7 slice_dynamic-update-slice_fusion.2
  75.8 2.0 fusion.2
  80.4 10.3 %collective-permute-done.11 = bf16[3,128,704]{1,2,0:T(8,128)(2,1)} collective-permute-done((bf16[3,128,704]{1,2,0:T(8,128)(2,1)}, bf16[3,128,704]{1,2,0:T(8,128)(2,1)}, u32[]{:S(2)}, u32[]{:S(2)}) %collective-permute-start.11) | collective-permute-done | bytes 540704 | tf_op jit(solution)/shard_map/ppermute | solution.py:92
  90.7 2.3 fusion.124
  93.7 1.4 collective-permute-start.12
  99.0 2.0 constant_dynamic-update-slice_fusion.39
  104.4 2.0 collective-permute-start.17
  107.5 1.6 collective-permute-done.17
  109.2 1.6 collective-permute-start.19
  110.8 1.6 collective-permute-done.18
  112.4 2.2 collective-permute-done.19
  115.5 1.9 constant_dynamic-update-slice_fusion.37
  117.4 5.1 %collective-permute-done.21 = bf16[3,128,704]{1,2,0:T(8,128)(2,1)S(1)} collective-permute-done((bf16[3,128,704]{1,2,0:T(8,128)(2,1)}, bf16[3,128,704]{1,2,0:T(8,128)(2,1)S(1)}, u32[]{:S(2)}, u32[]{:S(2)}) %collective-permute-start.21) | collective-permute-done | bytes 540704 | tf_op jit(solution)/shard_map/ppermute | solution.py:87
  123.4 1.9 constant_dynamic-update-slice_fusion.35
  125.3 8.8 %collective-permute-done.22 = bf16[3,128,704]{1,2,0:T(8,128)(2,1)S(1)} collective-permute-done((bf16[3,128,704]{1,2,0:T(8,128)(2,1)}, bf16[3,128,704]{1,2,0:T(8,128)(2,1)S(1)}, u32[]{:S(2)}, u32[]{:S(2)}) %collective-permute-start.22) | collective-permute-done | bytes 540704 | tf_op jit(solution)/shard_map/ppermute | solution.py:87
  135.0 2.1 fusion.9
  137.1 1.9 fusion.11
  146.0 2.2 collective-permute-start.23
  152.3 3.2 collective-permute-done.24
  164.2 1.5 collective-permute-done.28
  165.7 9.1 %collective-permute-done.30 = bf16[3,128,704]{1,2,0:T(8,128)(2,1)} collective-permute-done((bf16[3,128,704]{1,2,0:T(8,128)(2,1)}, bf16[3,128,704]{1,2,0:T(8,128)(2,1)}, u32[]{:S(2)}, u32[]{:S(2)}) %collective-permute-start.30) | collective-permute-done | bytes 540704 | tf_op jit(solution)/shard_map/ppermute | solution.py:87
  174.9 2.2 add_convert_fusion.1
  177.1 3.1 collective-permute-start.56
  180.2 6.2 %collective-permute-done.29 = bf16[3,128,704]{1,2,0:T(8,128)(2,1)} collective-permute-done((bf16[3,128,704]{1,2,0:T(8,128)(2,1)}, bf16[3,128,704]{1,2,0:T(8,128)(2,1)}, u32[]{:S(2)}, u32[]{:S(2)}) %collective-permute-start.29) | collective-permute-done | bytes 540704 | tf_op jit(solution)/shard_map/ppermute | solution.py:87
  186.4 2.0 add_convert_fusion.2
  188.4 1.4 fusion.15
  201.7 3.1 fusion.126
  206.2 4.0 %collective-permute-start.31 = (bf16[64,1024]{1,0:T(8,128)(2,1)}, bf16[64,1024]{1,0:T(8,128)(2,1)}, u32[]{:S(2)}, u32[]{:S(2)}) collective-permute-start(bf16[64,1024]{1,0:T(8,128)(2,1)} %get-tuple-element.161), channel_id=1, source_target_pairs={{0,1},{1,2},{2,3},{3,0},{4,5},{5,6},{6,7},{7,4},{8,9},{9,10},{10,1... | collective-permute-start | bytes 393224 | tf_op jit(solution)/shard_map/ppermute | solution.py:140
  212.1 2.0 add_convert_fusion
  217.4 1.3 fusion.28
  221.8 2.9 fusion.127
  226.0 1.5 collective-permute-start.34
  237.0 2.4 collective-permute-start.42
  239.4 2.1 collective-permute-done.41
  245.3 2.7 collective-permute-done.38
  248.0 1.4 collective-permute-start.57
  252.5 1.3 collective-permute-start.50
  254.4 11.1 %collective-permute-done.50 = bf16[130,1024]{0,1:T(8,128)(2,1)S(1)} collective-permute-done((bf16[130,1024]{0,1:T(8,128)(2,1)S(1)}, bf16[130,1024]{0,1:T(8,128)(2,1)S(1)}, u32[]{:S(2)}, u32[]{:S(2)}) %collective-permute-start.50) | collective-permute-done | bytes 266272 | tf_op jit(solution)/shard_map/ppermute | solution.py:87
  266.9 9.8 %collective-permute-done.52 = bf16[130,1024]{0,1:T(8,128)(2,1)S(1)} collective-permute-done((bf16[130,1024]{0,1:T(8,128)(2,1)S(1)}, bf16[130,1024]{0,1:T(8,128)(2,1)S(1)}, u32[]{:S(2)}, u32[]{:S(2)}) %collective-permute-start.52) | collective-permute-done | bytes 266272 | tf_op jit(solution)/shard_map/ppermute | solution.py:87
  278.1 9.8 %collective-permute-done.54 = bf16[130,1024]{0,1:T(8,128)(2,1)S(1)} collective-permute-done((bf16[130,1024]{0,1:T(8,128)(2,1)S(1)}, bf16[130,1024]{0,1:T(8,128)(2,1)S(1)}, u32[]{:S(2)}, u32[]{:S(2)}) %collective-permute-start.54) | collective-permute-done | bytes 266272 | tf_op jit(solution)/shard_map/ppermute | solution.py:87
  288.0 5.6 %collective-permute-start.51 = (bf16[130,1024]{0,1:T(8,128)(2,1)S(1)}, bf16[130,1024]{0,1:T(8,128)(2,1)S(1)}, u32[]{:S(2)}, u32[]{:S(2)}) collective-permute-start(bf16[130,1024]{0,1:T(8,128)(2,1)S(1)} %add_convert_fusion.5), channel_id=1, source_target_pairs={{0,24},{4,28},{8,0},{12,4},{16,8},{20,12},{24,16},{28,20},{1,25},{... | collective-permute-start | bytes 798728 | tf_op jit(solution)/shard_map/ppermute | solution.py:92
  293.8 1.4 collective-permute-start.55
  295.2 1.6 convert_add_fusion
  297.8 1.4 collective-permute-done.49
  299.2 9.1 %collective-permute-done.51 = bf16[130,1024]{0,1:T(8,128)(2,1)S(1)} collective-permute-done((bf16[130,1024]{0,1:T(8,128)(2,1)S(1)}, bf16[130,1024]{0,1:T(8,128)(2,1)S(1)}, u32[]{:S(2)}, u32[]{:S(2)}) %collective-permute-start.51) | collective-permute-done | bytes 266272 | tf_op jit(solution)/shard_map/ppermute | solution.py:92
  308.3 19.3 %collective-permute-done.53 = bf16[130,1024]{0,1:T(8,128)(2,1)S(1)} collective-permute-done((bf16[130,1024]{0,1:T(8,128)(2,1)S(1)}, bf16[130,1024]{0,1:T(8,128)(2,1)S(1)}, u32[]{:S(2)}, u32[]{:S(2)}) %collective-permute-start.53) | collective-permute-done | bytes 266272 | tf_op jit(solution)/shard_map/ppermute | solution.py:92
  327.7 11.2 %collective-permute-done.55 = bf16[130,1024]{0,1:T(8,128)(2,1)S(1)} collective-permute-done((bf16[130,1024]{0,1:T(8,128)(2,1)S(1)}, bf16[130,1024]{0,1:T(8,128)(2,1)S(1)}, u32[]{:S(2)}, u32[]{:S(2)}) %collective-permute-start.55) | collective-permute-done | bytes 266272 | tf_op jit(solution)/shard_map/ppermute | solution.py:92
  (487 shorter events, 103.6 us)
Async XLA Ops:
  5.1 11.1 %collective-permute-start = (bf16[1,16,128]{2,1,0:T(8,128)(2,1)S(1)}, bf16[1,16,128]{2,1,0:T(8,128)(2,1)S(1)}, u32[]{:S(2)}, u32[]{:S(2)}) collective-permute-start(bf16[1,16,128]{2,1,0:T(8,128)(2,1)S(1)} %pad_bitcast_fusion), channel_id=1, source_target_pairs={{0,1},{1,2},{2,3},{3,0},{4,5},{5,6},{6,7},{7,4},{8,9},{9,10},{10,1... | collective-permute-start | bytes 12296 | tf_op jit(solution)/shard_map/ppermute | solution.py:140
  5.9 10.3 %collective-permute-start.1 = (bf16[1,16,128]{2,1,0:T(8,128)(2,1)S(1)}, bf16[1,16,128]{2,1,0:T(8,128)(2,1)S(1)}, u32[]{:S(2)}, u32[]{:S(2)}) collective-permute-start(bf16[1,16,128]{2,1,0:T(8,128)(2,1)S(1)} %pad_bitcast_fusion), channel_id=1, source_target_pairs={{0,2},{1,3},{2,0},{3,1},{4,6},{5,7},{6,4},{7,5},{8,10},{9,11},{10,... | collective-permute-start | bytes 12296 | tf_op jit(solution)/shard_map/ppermute | solution.py:140
  7.2 9.1 %collective-permute-start.2 = (bf16[1,16,128]{2,1,0:T(8,128)(2,1)S(1)}, bf16[1,16,128]{2,1,0:T(8,128)(2,1)S(1)}, u32[]{:S(2)}, u32[]{:S(2)}) collective-permute-start(bf16[1,16,128]{2,1,0:T(8,128)(2,1)S(1)} %pad_bitcast_fusion), channel_id=1, source_target_pairs={{0,3},{1,0},{2,1},{3,2},{4,7},{5,4},{6,5},{7,6},{8,11},{9,8},{10,9... | collective-permute-start | bytes 12296 | tf_op jit(solution)/shard_map/ppermute | solution.py:140
  9.4 39.0 %collective-permute-start.16 = (bf16[3,128,704]{1,2,0:T(8,128)(2,1)}, bf16[3,128,704]{1,2,0:T(8,128)(2,1)S(1)}, u32[]{:S(2)}, u32[]{:S(2)}) collective-permute-start(bf16[3,128,704]{1,2,0:T(8,128)(2,1)} %get-tuple-element.31), channel_id=1, source_target_pairs={{0,4},{4,0},{8,12},{12,8},{16,20},{20,16},{24,28},{28,24},{1,5},{5... | collective-permute-start | bytes 1622024 | tf_op jit(solution)/shard_map/ppermute | solution.py:87
  16.3 49.4 %copy-start.32 = (bf16[2,128,1024]{2,1,0:T(8,128)(2,1)S(1)}, bf16[2,128,1024]{2,1,0:T(8,128)(2,1)}, u32[]{:S(2)}) copy-start(bf16[2,128,1024]{2,1,0:T(8,128)(2,1)} %param.17) | copy-start | bytes 1572868
  16.3 12.5 %collective-permute-start.3 = (bf16[136,1024]{1,0:T(8,128)(2,1)S(1)}, bf16[136,1024]{1,0:T(8,128)(2,1)S(1)}, u32[]{:S(2)}, u32[]{:S(2)}) collective-permute-start(bf16[136,1024]{1,0:T(8,128)(2,1)S(1)} %pad_maximum_fusion.10), channel_id=1, source_target_pairs={{0,4},{4,0},{8,12},{12,8},{16,20},{20,16},{24,28},{28,24},{1,5},{5... | collective-permute-start | bytes 835592 | tf_op jit(solution)/shard_map/ppermute | solution.py:87
  16.7 12.2 %collective-permute-start.4 = (bf16[136,1024]{1,0:T(8,128)(2,1)S(1)}, bf16[136,1024]{1,0:T(8,128)(2,1)S(1)}, u32[]{:S(2)}, u32[]{:S(2)}) collective-permute-start(bf16[136,1024]{1,0:T(8,128)(2,1)S(1)} %pad_maximum_fusion.10), channel_id=1, source_target_pairs={{0,8},{4,12},{8,16},{12,20},{16,24},{20,28},{24,0},{28,4},{1,9},{5... | collective-permute-start | bytes 835592 | tf_op jit(solution)/shard_map/ppermute | solution.py:92
  18.0 22.7 %collective-permute-start.6 = (bf16[136,1024]{1,0:T(8,128)(2,1)S(1)}, bf16[136,1024]{1,0:T(8,128)(2,1)S(1)}, u32[]{:S(2)}, u32[]{:S(2)}) collective-permute-start(bf16[136,1024]{1,0:T(8,128)(2,1)S(1)} %pad_maximum_fusion.10), channel_id=1, source_target_pairs={{0,16},{4,20},{8,24},{12,28},{16,0},{20,4},{24,8},{28,12},{1,17},{... | collective-permute-start | bytes 835592 | tf_op jit(solution)/shard_map/ppermute | solution.py:92
  19.0 25.1 %collective-permute-start.8 = (bf16[136,1024]{1,0:T(8,128)(2,1)S(1)}, bf16[136,1024]{1,0:T(8,128)(2,1)S(1)}, u32[]{:S(2)}, u32[]{:S(2)}) collective-permute-start(bf16[136,1024]{1,0:T(8,128)(2,1)S(1)} %pad_maximum_fusion.10), channel_id=1, source_target_pairs={{0,24},{4,28},{8,0},{12,4},{16,8},{20,12},{24,16},{28,20},{1,25},{... | collective-permute-start | bytes 835592 | tf_op jit(solution)/shard_map/ppermute | solution.py:92
  44.1 33.8 %collective-permute-start.10 = (bf16[3,128,704]{1,2,0:T(8,128)(2,1)}, bf16[3,128,704]{1,2,0:T(8,128)(2,1)S(1)}, u32[]{:S(2)}, u32[]{:S(2)}) collective-permute-start(bf16[3,128,704]{1,2,0:T(8,128)(2,1)} %get-tuple-element.31), channel_id=1, source_target_pairs={{0,8},{4,12},{8,16},{12,20},{16,24},{20,28},{24,0},{28,4},{1,9},{5... | collective-permute-start | bytes 1622024 | tf_op jit(solution)/shard_map/ppermute | solution.py:92
  44.2 7.8 %collective-permute-start.5 = (bf16[136,1024]{1,0:T(8,128)(2,1)S(1)}, bf16[136,1024]{1,0:T(8,128)(2,1)S(1)}, u32[]{:S(2)}, u32[]{:S(2)}) collective-permute-start(bf16[136,1024]{1,0:T(8,128)(2,1)S(1)} %collective-permute-done.4), channel_id=1, source_target_pairs={{0,4},{4,0},{8,12},{12,8},{16,20},{20,16},{24,28},{28,24},{1,5},{5... | collective-permute-start | bytes 835592 | tf_op jit(solution)/shard_map/ppermute | solution.py:87
  45.4 12.6 %collective-permute-start.7 = (bf16[136,1024]{1,0:T(8,128)(2,1)S(1)}, bf16[136,1024]{1,0:T(8,128)(2,1)}, u32[]{:S(2)}, u32[]{:S(2)}) collective-permute-start(bf16[136,1024]{1,0:T(8,128)(2,1)S(1)} %collective-permute-done.6), channel_id=1, source_target_pairs={{0,4},{4,0},{8,12},{12,8},{16,20},{20,16},{24,28},{28,24},{1,5},{5... | collective-permute-start | bytes 835592 | tf_op jit(solution)/shard_map/ppermute | solution.py:87
  45.7 18.3 %collective-permute-start.9 = (bf16[136,1024]{1,0:T(8,128)(2,1)S(1)}, bf16[136,1024]{1,0:T(8,128)(2,1)S(1)}, u32[]{:S(2)}, u32[]{:S(2)}) collective-permute-start(bf16[136,1024]{1,0:T(8,128)(2,1)S(1)} %collective-permute-done.8), channel_id=1, source_target_pairs={{0,4},{4,0},{8,12},{12,8},{16,20},{20,16},{24,28},{28,24},{1,5},{5... | collective-permute-start | bytes 835592 | tf_op jit(solution)/shard_map/ppermute | solution.py:87
  48.4 42.3 %collective-permute-start.11 = (bf16[3,128,704]{1,2,0:T(8,128)(2,1)}, bf16[3,128,704]{1,2,0:T(8,128)(2,1)}, u32[]{:S(2)}, u32[]{:S(2)}) collective-permute-start(bf16[3,128,704]{1,2,0:T(8,128)(2,1)} %get-tuple-element.31), channel_id=1, source_target_pairs={{0,16},{4,20},{8,24},{12,28},{16,0},{20,4},{24,8},{28,12},{1,17},{... | collective-permute-start | bytes 1622024 | tf_op jit(solution)/shard_map/ppermute | solution.py:92
  52.0 49.1 %collective-permute-start.15 = (bf16[3,128,704]{1,2,0:T(8,128)(2,1)}, bf16[3,128,704]{1,2,0:T(8,128)(2,1)}, u32[]{:S(2)}, u32[]{:S(2)}) collective-permute-start(bf16[3,128,704]{1,2,0:T(8,128)(2,1)} %get-tuple-element.31), channel_id=1, source_target_pairs={{0,24},{4,28},{8,0},{12,4},{16,8},{20,12},{24,16},{28,20},{1,25},{... | collective-permute-start | bytes 1622024 | tf_op jit(solution)/shard_map/ppermute | solution.py:92
  93.7 7.6 %collective-permute-start.12 = (bf16[64,1024]{1,0:T(8,128)(2,1)}, bf16[64,1024]{1,0:T(8,128)(2,1)S(1)}, u32[]{:S(2)}, u32[]{:S(2)}) collective-permute-start(bf16[64,1024]{1,0:T(8,128)(2,1)} %get-tuple-element.168), channel_id=1, source_target_pairs={{0,1},{1,2},{2,3},{3,0},{4,5},{5,6},{6,7},{7,4},{8,9},{9,10},{10,1... | collective-permute-start | bytes 393224 | tf_op jit(solution)/shard_map/ppermute | solution.py:140
  95.1 7.7 %collective-permute-start.13 = (bf16[64,1024]{1,0:T(8,128)(2,1)S(1)}, bf16[64,1024]{1,0:T(8,128)(2,1)S(1)}, u32[]{:S(2)}, u32[]{:S(2)}) collective-permute-start(bf16[64,1024]{1,0:T(8,128)(2,1)S(1)} %get-tuple-element.170), channel_id=1, source_target_pairs={{0,2},{1,3},{2,0},{3,1},{4,6},{5,7},{6,4},{7,5},{8,10},{9,11},{10,... | collective-permute-start | bytes 393224 | tf_op jit(solution)/shard_map/ppermute | solution.py:140
  96.1 7.1 %collective-permute-start.14 = (bf16[64,1024]{1,0:T(8,128)(2,1)S(1)}, bf16[64,1024]{1,0:T(8,128)(2,1)S(1)}, u32[]{:S(2)}, u32[]{:S(2)}) collective-permute-start(bf16[64,1024]{1,0:T(8,128)(2,1)S(1)} %get-tuple-element.169), channel_id=1, source_target_pairs={{0,3},{1,0},{2,1},{3,2},{4,7},{5,4},{6,5},{7,6},{8,11},{9,8},{10,9... | collective-permute-start | bytes 393224 | tf_op jit(solution)/shard_map/ppermute | solution.py:140
  96.9 40.2 %copy-start.3 = (bf16[256,1024]{1,0:T(8,128)(2,1)}, bf16[256,1024]{1,0:T(8,128)(2,1)S(1)}, u32[]{:S(2)}) copy-start(bf16[256,1024]{1,0:T(8,128)(2,1)S(1)} %constant_dynamic-update-slice_fusion.42) | copy-start | bytes 1572868
  97.8 16.8 %collective-permute-start.20 = (bf16[3,128,704]{1,2,0:T(8,128)(2,1)}, bf16[3,128,704]{1,2,0:T(8,128)(2,1)S(1)}, u32[]{:S(2)}, u32[]{:S(2)}) collective-permute-start(bf16[3,128,704]{1,2,0:T(8,128)(2,1)} %copy-done.31), channel_id=1, source_target_pairs={{0,4},{4,0},{8,12},{12,8},{16,20},{20,16},{24,28},{28,24},{1,5},{5... | collective-permute-start | bytes 1622024 | tf_op jit(solution)/shard_map/ppermute | solution.py:87
  101.1 21.5 %collective-permute-start.21 = (bf16[3,128,704]{1,2,0:T(8,128)(2,1)}, bf16[3,128,704]{1,2,0:T(8,128)(2,1)S(1)}, u32[]{:S(2)}, u32[]{:S(2)}) collective-permute-start(bf16[3,128,704]{1,2,0:T(8,128)(2,1)} %collective-permute-done.11), channel_id=1, source_target_pairs={{0,4},{4,0},{8,12},{12,8},{16,20},{20,16},{24,28},{28,24},{1,5},{5... | collective-permute-start | bytes 1622024 | tf_op jit(solution)/shard_map/ppermute | solution.py:87
  101.3 32.8 %collective-permute-start.22 = (bf16[3,128,704]{1,2,0:T(8,128)(2,1)}, bf16[3,128,704]{1,2,0:T(8,128)(2,1)S(1)}, u32[]{:S(2)}, u32[]{:S(2)}) collective-permute-start(bf16[3,128,704]{1,2,0:T(8,128)(2,1)} %collective-permute-done.15), channel_id=1, source_target_pairs={{0,4},{4,0},{8,12},{12,8},{16,20},{20,16},{24,28},{28,24},{1,5},{5... | collective-permute-start | bytes 1622024 | tf_op jit(solution)/shard_map/ppermute | solution.py:87
  104.3 52.1 %copy-start.67 = (f32[64]{0:T(128)}, f32[64]{0:T(128)S(1)}, u32[]{:S(2)}) copy-start(f32[64]{0:T(128)S(1)} %fusion.106) | copy-start | bytes 772
  104.4 4.7 %collective-permute-start.17 = (bf16[64,1024]{1,0:T(8,128)(2,1)S(1)}, bf16[64,1024]{1,0:T(8,128)(2,1)S(1)}, u32[]{:S(2)}, u32[]{:S(2)}) collective-permute-start(bf16[64,1024]{1,0:T(8,128)(2,1)S(1)} %multiply_convert_fusion.3), channel_id=1, source_target_pairs={{0,1},{1,2},{2,3},{3,0},{4,5},{5,6},{6,7},{7,4},{8,9},{9,10},{10,1... | collective-permute-start | bytes 393224 | tf_op jit(solution)/shard_map/ppermute | solution.py:140
  106.5 5.9 %collective-permute-start.18 = (bf16[64,1024]{1,0:T(8,128)(2,1)S(1)}, bf16[64,1024]{1,0:T(8,128)(2,1)S(1)}, u32[]{:S(2)}, u32[]{:S(2)}) collective-permute-start(bf16[64,1024]{1,0:T(8,128)(2,1)S(1)} %multiply_convert_fusion.3), channel_id=1, source_target_pairs={{0,2},{1,3},{2,0},{3,1},{4,6},{5,7},{6,4},{7,5},{8,10},{9,11},{10,... | collective-permute-start | bytes 393224 | tf_op jit(solution)/shard_map/ppermute | solution.py:140
  109.2 5.4 %collective-permute-start.19 = (bf16[64,1024]{1,0:T(8,128)(2,1)S(1)}, bf16[64,1024]{1,0:T(8,128)(2,1)S(1)}, u32[]{:S(2)}, u32[]{:S(2)}) collective-permute-start(bf16[64,1024]{1,0:T(8,128)(2,1)S(1)} %multiply_convert_fusion.3), channel_id=1, source_target_pairs={{0,3},{1,0},{2,1},{3,2},{4,7},{5,4},{6,5},{7,6},{8,11},{9,8},{10,9... | collective-permute-start | bytes 393224 | tf_op jit(solution)/shard_map/ppermute | solution.py:140
  146.0 6.4 %collective-permute-start.23 = (bf16[64,1024]{1,0:T(8,128)(2,1)S(1)}, bf16[64,1024]{1,0:T(8,128)(2,1)S(1)}, u32[]{:S(2)}, u32[]{:S(2)}) collective-permute-start(bf16[64,1024]{1,0:T(8,128)(2,1)S(1)} %get-tuple-element.164), channel_id=1, source_target_pairs={{0,1},{1,2},{2,3},{3,0},{4,5},{5,6},{6,7},{7,4},{8,9},{9,10},{10,1... | collective-permute-start | bytes 393224 | tf_op jit(solution)/shard_map/ppermute | solution.py:140
  148.2 7.4 %collective-permute-start.24 = (bf16[64,1024]{1,0:T(8,128)(2,1)S(1)}, bf16[64,1024]{1,0:T(8,128)(2,1)S(1)}, u32[]{:S(2)}, u32[]{:S(2)}) collective-permute-start(bf16[64,1024]{1,0:T(8,128)(2,1)S(1)} %get-tuple-element.166), channel_id=1, source_target_pairs={{0,2},{1,3},{2,0},{3,1},{4,6},{5,7},{6,4},{7,5},{8,10},{9,11},{10,... | collective-permute-start | bytes 393224 | tf_op jit(solution)/shard_map/ppermute | solution.py:140
  149.1 7.0 %collective-permute-start.25 = (bf16[64,1024]{1,0:T(8,128)(2,1)S(1)}, bf16[64,1024]{1,0:T(8,128)(2,1)S(1)}, u32[]{:S(2)}, u32[]{:S(2)}) collective-permute-start(bf16[64,1024]{1,0:T(8,128)(2,1)S(1)} %get-tuple-element.165), channel_id=1, source_target_pairs={{0,3},{1,0},{2,1},{3,2},{4,7},{5,4},{6,5},{7,6},{8,11},{9,8},{10,9... | collective-permute-start | bytes 393224 | tf_op jit(solution)/shard_map/ppermute | solution.py:140
  150.0 143.7 %collective-permute-start.44 = (bf16[3,128,704]{1,2,0:T(8,128)(2,1)}, bf16[3,128,704]{1,2,0:T(8,128)(2,1)}, u32[]{:S(2)}, u32[]{:S(2)}) collective-permute-start(bf16[3,128,704]{1,2,0:T(8,128)(2,1)} %pad_maximum_fusion.4), channel_id=1, source_target_pairs={{0,4},{4,0},{8,12},{12,8},{16,20},{20,16},{24,28},{28,24},{1,5},{5... | collective-permute-start | bytes 1622024 | tf_op jit(solution)/shard_map/ppermute | solution.py:87
  152.1 22.8 %collective-permute-start.30 = (bf16[3,128,704]{1,2,0:T(8,128)(2,1)}, bf16[3,128,704]{1,2,0:T(8,128)(2,1)}, u32[]{:S(2)}, u32[]{:S(2)}) collective-permute-start(bf16[3,128,704]{1,2,0:T(8,128)(2,1)} %pad_maximum_fusion.2), channel_id=1, source_target_pairs={{0,4},{4,0},{8,12},{12,8},{16,20},{20,16},{24,28},{28,24},{1,5},{5... | collective-permute-start | bytes 1622024 | tf_op jit(solution)/shard_map/ppermute | solution.py:87
  156.5 3.6 %collective-permute-start.26 = (bf16[64,1024]{1,0:T(8,128)(2,1)S(1)}, bf16[64,1024]{1,0:T(8,128)(2,1)}, u32[]{:S(2)}, u32[]{:S(2)}) collective-permute-start(bf16[64,1024]{1,0:T(8,128)(2,1)S(1)} %get-tuple-element.92), channel_id=1, source_target_pairs={{0,1},{1,2},{2,3},{3,0},{4,5},{5,6},{6,7},{7,4},{8,9},{9,10},{10,1... | collective-permute-start | bytes 393224 | tf_op jit(solution)/shard_map/ppermute | solution.py:140
  156.6 29.8 %copy-start.24 = (bf16[1,128,704]{1,2,0:T(8,128)(2,1)S(1)}, bf16[1,128,704]{1,2,0:T(8,128)(2,1)}, u32[]{:S(2)}) copy-start(bf16[1,128,704]{1,2,0:T(8,128)(2,1)} %get-tuple-element.127) | copy-start | bytes 540676
  157.5 28.9 %collective-permute-start.29 = (bf16[3,128,704]{1,2,0:T(8,128)(2,1)}, bf16[3,128,704]{1,2,0:T(8,128)(2,1)}, u32[]{:S(2)}, u32[]{:S(2)}) collective-permute-start(bf16[3,128,704]{1,2,0:T(8,128)(2,1)} %pad_maximum_fusion.1), channel_id=1, source_target_pairs={{0,4},{4,0},{8,12},{12,8},{16,20},{20,16},{24,28},{28,24},{1,5},{5... | collective-permute-start | bytes 1622024 | tf_op jit(solution)/shard_map/ppermute | solution.py:87
  158.7 4.4 %collective-permute-start.27 = (bf16[64,1024]{1,0:T(8,128)(2,1)S(1)}, bf16[64,1024]{1,0:T(8,128)(2,1)}, u32[]{:S(2)}, u32[]{:S(2)}) collective-permute-start(bf16[64,1024]{1,0:T(8,128)(2,1)S(1)} %get-tuple-element.92), channel_id=1, source_target_pairs={{0,2},{1,3},{2,0},{3,1},{4,6},{5,7},{6,4},{7,5},{8,10},{9,11},{10,... | collective-permute-start | bytes 393224 | tf_op jit(solution)/shard_map/ppermute | solution.py:140
  160.1 5.6 %collective-permute-start.28 = (bf16[64,1024]{1,0:T(8,128)(2,1)S(1)}, bf16[64,1024]{1,0:T(8,128)(2,1)S(1)}, u32[]{:S(2)}, u32[]{:S(2)}) collective-permute-start(bf16[64,1024]{1,0:T(8,128)(2,1)S(1)} %get-tuple-element.92), channel_id=1, source_target_pairs={{0,3},{1,0},{2,1},{3,2},{4,7},{5,4},{6,5},{7,6},{8,11},{9,8},{10,9... | collective-permute-start | bytes 393224 | tf_op jit(solution)/shard_map/ppermute | solution.py:140
  163.1 48.8 %collective-permute-start.43 = (bf16[3,128,704]{1,2,0:T(8,128)(2,1)}, bf16[3,128,704]{1,2,0:T(8,128)(2,1)}, u32[]{:S(2)}, u32[]{:S(2)}) collective-permute-start(bf16[3,128,704]{1,2,0:T(8,128)(2,1)} %pad_maximum_fusion.3), channel_id=1, source_target_pairs={{0,4},{4,0},{8,12},{12,8},{16,20},{20,16},{24,28},{28,24},{1,5},{5... | collective-permute-start | bytes 1622024 | tf_op jit(solution)/shard_map/ppermute | solution.py:87
  177.1 118.1 %collective-permute-start.56 = (bf16[3,128,704]{1,2,0:T(8,128)(2,1)}, bf16[3,128,704]{1,2,0:T(8,128)(2,1)}, u32[]{:S(2)}, u32[]{:S(2)}) collective-permute-start(bf16[3,128,704]{1,2,0:T(8,128)(2,1)} %add_convert_fusion.1), channel_id=1, source_target_pairs={{0,16},{4,20},{8,24},{12,28},{16,0},{20,4},{24,8},{28,12},{1,17},{... | collective-permute-start | bytes 1622024 | tf_op jit(solution)/shard_map/ppermute | solution.py:92
  206.2 10.0 %collective-permute-start.31 = (bf16[64,1024]{1,0:T(8,128)(2,1)}, bf16[64,1024]{1,0:T(8,128)(2,1)}, u32[]{:S(2)}, u32[]{:S(2)}) collective-permute-start(bf16[64,1024]{1,0:T(8,128)(2,1)} %get-tuple-element.161), channel_id=1, source_target_pairs={{0,1},{1,2},{2,3},{3,0},{4,5},{5,6},{6,7},{7,4},{8,9},{9,10},{10,1... | collective-permute-start | bytes 393224 | tf_op jit(solution)/shard_map/ppermute | solution.py:140
  210.2 6.7 %collective-permute-start.32 = (bf16[64,1024]{1,0:T(8,128)(2,1)}, bf16[64,1024]{1,0:T(8,128)(2,1)}, u32[]{:S(2)}, u32[]{:S(2)}) collective-permute-start(bf16[64,1024]{1,0:T(8,128)(2,1)} %get-tuple-element.163), channel_id=1, source_target_pairs={{0,2},{1,3},{2,0},{3,1},{4,6},{5,7},{6,4},{7,5},{8,10},{9,11},{10,... | collective-permute-start | bytes 393224 | tf_op jit(solution)/shard_map/ppermute | solution.py:140
  211.8 5.6 %collective-permute-start.33 = (bf16[64,1024]{1,0:T(8,128)(2,1)}, bf16[64,1024]{1,0:T(8,128)(2,1)S(1)}, u32[]{:S(2)}, u32[]{:S(2)}) collective-permute-start(bf16[64,1024]{1,0:T(8,128)(2,1)} %get-tuple-element.162), channel_id=1, source_target_pairs={{0,3},{1,0},{2,1},{3,2},{4,7},{5,4},{6,5},{7,6},{8,11},{9,8},{10,9... | collective-permute-start | bytes 393224 | tf_op jit(solution)/shard_map/ppermute | solution.py:140
  220.0 6.1 %collective-permute-start.46 = (bf16[1,8,2048]{2,0,1:T(2,128)(2,1)S(1)}, bf16[1,8,2048]{2,0,1:T(2,128)(2,1)S(1)}, u32[]{:S(2)}, u32[]{:S(2)}) collective-permute-start(bf16[1,8,2048]{2,0,1:T(2,128)(2,1)S(1)} %get-tuple-element.183), channel_id=1, source_target_pairs={{0,1},{1,2},{2,3},{3,0},{4,5},{5,6},{6,7},{7,4},{8,9},{9,10},{10,1... | collective-permute-start | bytes 98312 | tf_op jit(solution)/shard_map/ppermute | solution.py:140
  220.5 7.0 %collective-permute-start.47 = (bf16[1,8,2048]{2,0,1:T(2,128)(2,1)S(1)}, bf16[1,8,2048]{2,0,1:T(2,128)(2,1)S(1)}, u32[]{:S(2)}, u32[]{:S(2)}) collective-permute-start(bf16[1,8,2048]{2,0,1:T(2,128)(2,1)S(1)} %get-tuple-element.184), channel_id=1, source_target_pairs={{0,2},{1,3},{2,0},{3,1},{4,6},{5,7},{6,4},{7,5},{8,10},{9,11},{10,... | collective-permute-start | bytes 98312 | tf_op jit(solution)/shard_map/ppermute | solution.py:140
  221.5 6.5 %collective-permute-start.48 = (bf16[1,8,2048]{2,0,1:T(2,128)(2,1)S(1)}, bf16[1,8,2048]{2,0,1:T(2,128)(2,1)S(1)}, u32[]{:S(2)}, u32[]{:S(2)}) collective-permute-start(bf16[1,8,2048]{2,0,1:T(2,128)(2,1)S(1)} %get-tuple-element.185), channel_id=1, source_target_pairs={{0,3},{1,0},{2,1},{3,2},{4,7},{5,4},{6,5},{7,6},{8,11},{9,8},{10,9... | collective-permute-start | bytes 98312 | tf_op jit(solution)/shard_map/ppermute | solution.py:140
  226.0 6.8 %collective-permute-start.34 = (bf16[64,1024]{1,0:T(8,128)(2,1)S(1)}, bf16[64,1024]{1,0:T(8,128)(2,1)}, u32[]{:S(2)}, u32[]{:S(2)}) collective-permute-start(bf16[64,1024]{1,0:T(8,128)(2,1)S(1)} %get-tuple-element.158), channel_id=1, source_target_pairs={{0,1},{1,2},{2,3},{3,0},{4,5},{5,6},{6,7},{7,4},{8,9},{9,10},{10,1... | collective-permute-start | bytes 393224 | tf_op jit(solution)/shard_map/ppermute | solution.py:140
  227.5 6.5 %collective-permute-start.35 = (bf16[64,1024]{1,0:T(8,128)(2,1)S(1)}, bf16[64,1024]{1,0:T(8,128)(2,1)}, u32[]{:S(2)}, u32[]{:S(2)}) collective-permute-start(bf16[64,1024]{1,0:T(8,128)(2,1)S(1)} %get-tuple-element.160), channel_id=1, source_target_pairs={{0,2},{1,3},{2,0},{3,1},{4,6},{5,7},{6,4},{7,5},{8,10},{9,11},{10,... | collective-permute-start | bytes 393224 | tf_op jit(solution)/shard_map/ppermute | solution.py:140
  228.0 6.7 %collective-permute-start.36 = (bf16[64,1024]{1,0:T(8,128)(2,1)S(1)}, bf16[64,1024]{1,0:T(8,128)(2,1)}, u32[]{:S(2)}, u32[]{:S(2)}) collective-permute-start(bf16[64,1024]{1,0:T(8,128)(2,1)S(1)} %get-tuple-element.159), channel_id=1, source_target_pairs={{0,3},{1,0},{2,1},{3,2},{4,7},{5,4},{6,5},{7,6},{8,11},{9,8},{10,9... | collective-permute-start | bytes 393224 | tf_op jit(solution)/shard_map/ppermute | solution.py:140
  232.8 17.1 %collective-permute-start.45 = (bf16[3,128,704]{1,2,0:T(8,128)(2,1)}, bf16[3,128,704]{1,2,0:T(8,128)(2,1)S(1)}, u32[]{:S(2)}, u32[]{:S(2)}) collective-permute-start(bf16[3,128,704]{1,2,0:T(8,128)(2,1)} %add_convert_fusion.2), channel_id=1, source_target_pairs={{0,24},{4,28},{8,0},{12,4},{16,8},{20,12},{24,16},{28,20},{1,25},{... | collective-permute-start | bytes 1622024 | tf_op jit(solution)/shard_map/ppermute | solution.py:92
  234.0 3.0 collective-permute-start.40
  234.7 6.8 %collective-permute-start.41 = (bf16[64,1024]{1,0:T(8,128)(2,1)S(1)}, bf16[64,1024]{1,0:T(8,128)(2,1)S(1)}, u32[]{:S(2)}, u32[]{:S(2)}) collective-permute-start(bf16[64,1024]{1,0:T(8,128)(2,1)S(1)} %get-tuple-element.87), channel_id=1, source_target_pairs={{0,2},{1,3},{2,0},{3,1},{4,6},{5,7},{6,4},{7,5},{8,10},{9,11},{10,... | collective-permute-start | bytes 393224 | tf_op jit(solution)/shard_map/ppermute | solution.py:140
  237.0 5.6 %collective-permute-start.42 = (bf16[64,1024]{1,0:T(8,128)(2,1)S(1)}, bf16[64,1024]{1,0:T(8,128)(2,1)S(1)}, u32[]{:S(2)}, u32[]{:S(2)}) collective-permute-start(bf16[64,1024]{1,0:T(8,128)(2,1)S(1)} %get-tuple-element.87), channel_id=1, source_target_pairs={{0,3},{1,0},{2,1},{3,2},{4,7},{5,4},{6,5},{7,6},{8,11},{9,8},{10,9... | collective-permute-start | bytes 393224 | tf_op jit(solution)/shard_map/ppermute | solution.py:140
  241.5 3.6 %collective-permute-start.37 = (bf16[64,1024]{1,0:T(8,128)(2,1)S(1)}, bf16[64,1024]{1,0:T(8,128)(2,1)S(1)}, u32[]{:S(2)}, u32[]{:S(2)}) collective-permute-start(bf16[64,1024]{1,0:T(8,128)(2,1)S(1)} %get-tuple-element.90), channel_id=1, source_target_pairs={{0,1},{1,2},{2,3},{3,0},{4,5},{5,6},{6,7},{7,4},{8,9},{9,10},{10,1... | collective-permute-start | bytes 393224 | tf_op jit(solution)/shard_map/ppermute | solution.py:140
  242.6 5.5 %collective-permute-start.38 = (bf16[64,1024]{1,0:T(8,128)(2,1)S(1)}, bf16[64,1024]{1,0:T(8,128)(2,1)S(1)}, u32[]{:S(2)}, u32[]{:S(2)}) collective-permute-start(bf16[64,1024]{1,0:T(8,128)(2,1)S(1)} %get-tuple-element.90), channel_id=1, source_target_pairs={{0,2},{1,3},{2,0},{3,1},{4,6},{5,7},{6,4},{7,5},{8,10},{9,11},{10,... | collective-permute-start | bytes 393224 | tf_op jit(solution)/shard_map/ppermute | solution.py:140
  245.2 4.4 %collective-permute-start.39 = (bf16[64,1024]{1,0:T(8,128)(2,1)S(1)}, bf16[64,1024]{1,0:T(8,128)(2,1)S(1)}, u32[]{:S(2)}, u32[]{:S(2)}) collective-permute-start(bf16[64,1024]{1,0:T(8,128)(2,1)S(1)} %get-tuple-element.90), channel_id=1, source_target_pairs={{0,3},{1,0},{2,1},{3,2},{4,7},{5,4},{6,5},{7,6},{8,11},{9,8},{10,9... | collective-permute-start | bytes 393224 | tf_op jit(solution)/shard_map/ppermute | solution.py:140
  248.0 45.8 %collective-permute-start.57 = (bf16[3,128,704]{1,2,0:T(8,128)(2,1)S(1)}, bf16[3,128,704]{1,2,0:T(8,128)(2,1)S(1)}, u32[]{:S(2)}, u32[]{:S(2)}) collective-permute-start(bf16[3,128,704]{1,2,0:T(8,128)(2,1)S(1)} %copy-done.30), channel_id=1, source_target_pairs={{0,8},{4,12},{8,16},{12,20},{16,24},{20,28},{24,0},{28,4},{1,9},{5... | collective-permute-start | bytes 1622024 | tf_op jit(solution)/shard_map/ppermute | solution.py:92
  252.5 13.0 %collective-permute-start.50 = (bf16[130,1024]{0,1:T(8,128)(2,1)S(1)}, bf16[130,1024]{0,1:T(8,128)(2,1)S(1)}, u32[]{:S(2)}, u32[]{:S(2)}) collective-permute-start(bf16[130,1024]{0,1:T(8,128)(2,1)S(1)} %pad_maximum_fusion.6), channel_id=1, source_target_pairs={{0,4},{4,0},{8,12},{12,8},{16,20},{20,16},{24,28},{28,24},{1,5},{5... | collective-permute-start | bytes 798728 | tf_op jit(solution)/shard_map/ppermute | solution.py:87
  253.9 22.8 %collective-permute-start.52 = (bf16[130,1024]{0,1:T(8,128)(2,1)S(1)}, bf16[130,1024]{0,1:T(8,128)(2,1)S(1)}, u32[]{:S(2)}, u32[]{:S(2)}) collective-permute-start(bf16[130,1024]{0,1:T(8,128)(2,1)S(1)} %pad_maximum_fusion.7), channel_id=1, source_target_pairs={{0,4},{4,0},{8,12},{12,8},{16,20},{20,16},{24,28},{28,24},{1,5},{5... | collective-permute-start | bytes 798728 | tf_op jit(solution)/shard_map/ppermute | solution.py:87
  265.5 22.5 %collective-permute-start.54 = (bf16[130,1024]{0,1:T(8,128)(2,1)S(1)}, bf16[130,1024]{0,1:T(8,128)(2,1)S(1)}, u32[]{:S(2)}, u32[]{:S(2)}) collective-permute-start(bf16[130,1024]{0,1:T(8,128)(2,1)S(1)} %pad_maximum_fusion.8), channel_id=1, source_target_pairs={{0,4},{4,0},{8,12},{12,8},{16,20},{20,16},{24,28},{28,24},{1,5},{5... | collective-permute-start | bytes 798728 | tf_op jit(solution)/shard_map/ppermute | solution.py:87
  266.7 28.5 %copy-start.27 = (bf16[1,128,704]{1,2,0:T(8,128)(2,1)S(1)}, bf16[1,128,704]{1,2,0:T(8,128)(2,1)}, u32[]{:S(2)}) copy-start(bf16[1,128,704]{1,2,0:T(8,128)(2,1)} %get-tuple-element.120) | copy-start | bytes 540676
  276.7 22.5 %collective-permute-start.49 = (bf16[130,1024]{0,1:T(8,128)(2,1)S(1)}, bf16[130,1024]{0,1:T(8,128)(2,1)S(1)}, u32[]{:S(2)}, u32[]{:S(2)}) collective-permute-start(bf16[130,1024]{0,1:T(8,128)(2,1)S(1)} %pad_maximum_fusion.5), channel_id=1, source_target_pairs={{0,4},{4,0},{8,12},{12,8},{16,20},{20,16},{24,28},{28,24},{1,5},{5... | collective-permute-start | bytes 798728 | tf_op jit(solution)/shard_map/ppermute | solution.py:87
  288.0 20.4 %collective-permute-start.51 = (bf16[130,1024]{0,1:T(8,128)(2,1)S(1)}, bf16[130,1024]{0,1:T(8,128)(2,1)S(1)}, u32[]{:S(2)}, u32[]{:S(2)}) collective-permute-start(bf16[130,1024]{0,1:T(8,128)(2,1)S(1)} %add_convert_fusion.5), channel_id=1, source_target_pairs={{0,24},{4,28},{8,0},{12,4},{16,8},{20,12},{24,16},{28,20},{1,25},{... | collective-permute-start | bytes 798728 | tf_op jit(solution)/shard_map/ppermute | solution.py:92
  293.7 34.0 %collective-permute-start.53 = (bf16[130,1024]{0,1:T(8,128)(2,1)S(1)}, bf16[130,1024]{0,1:T(8,128)(2,1)S(1)}, u32[]{:S(2)}, u32[]{:S(2)}) collective-permute-start(bf16[130,1024]{0,1:T(8,128)(2,1)S(1)} %add_convert_fusion.4), channel_id=1, source_target_pairs={{0,16},{4,20},{8,24},{12,28},{16,0},{20,4},{24,8},{28,12},{1,17},{... | collective-permute-start | bytes 798728 | tf_op jit(solution)/shard_map/ppermute | solution.py:92
  293.8 45.1 %collective-permute-start.55 = (bf16[130,1024]{0,1:T(8,128)(2,1)S(1)}, bf16[130,1024]{0,1:T(8,128)(2,1)S(1)}, u32[]{:S(2)}, u32[]{:S(2)}) collective-permute-start(bf16[130,1024]{0,1:T(8,128)(2,1)S(1)} %add_convert_fusion.3), channel_id=1, source_target_pairs={{0,8},{4,12},{8,16},{12,20},{16,24},{20,28},{24,0},{28,4},{1,9},{5... | collective-permute-start | bytes 798728 | tf_op jit(solution)/shard_map/ppermute | solution.py:92
  295.2 43.7 %copy-start.40 = (bf16[128,256]{0,1:T(8,128)(2,1)S(1)}, bf16[128,256]{0,1:T(8,128)(2,1)}, u32[]{:S(2)}) copy-start(bf16[128,256]{0,1:T(8,128)(2,1)} %get-tuple-element.142) | copy-start | bytes 196612
  (76 other events, 605.1 us)

commit v3 on v2

--- a/solution.py
+++ b/solution.py
@@ -226,18 +226,18 @@
     in_cols = 2 * key_cols + 2 * value_cols
     in_mat, out_mat = attn_mat[:, :in_cols], attn_mat[:, in_cols:]
     ffn_pieces, ffn_order = rows.gather(
-        jnp.stack([w_ffn_gate, w_ffn_up, w_ffn_down]), attn_order
+        jnp.stack([w_ffn_gate, w_ffn_up, w_ffn_down])
     )
     ffn_mat = jnp.concatenate(ffn_pieces, axis=1)
     full_gate, full_up, full_down = ffn_mat[0], ffn_mat[1], ffn_mat[2]
 
     tokens_low = rows.relative(inputs.reshape(n_tok, model), 1)
-    dy_low = rows.relative(after(cotangent, attn_order[-1]).reshape(n_tok, model), 1)
+    dy_low = rows.relative(cotangent.reshape(n_tok, model), 1)
     tokens = tokens_low.astype(F32)
     own_tokens = lanes.own(tokens_low).astype(F32)
     own_dy = lanes.own(dy_low).astype(F32)
     normed_low = rms_gain(tokens, gain_in).astype(BF)
-    projected = after(dot(normed_low, in_mat), *ffn_order[:1])
+    projected = dot(normed_low, in_mat)
     qkv_low = projected[:, : in_cols - value_cols].astype(BF).astype(F32)
     gate_lin = projected[:, in_cols - value_cols :]
     rank_low = dot(normed_low, rank_in).astype(BF)
@@ -264,11 +264,11 @@
         heads(decays),
     )
     gated, gate_back = jax.vjp(head_gate, core_out, gate_lin, gain_head)
-    gated_low = after(gated.reshape(n_tok, -1).astype(BF), *ffn_order[1:2])
+    gated_low = gated.reshape(n_tok, -1).astype(BF)
     own_attended = lanes.scatter(dot_rt(gated_low, out_mat))
     own_middle = own_tokens + own_attended
     own_mid, norm_mid_back = jax.vjp(rms_gain, own_middle, gain_mid)
-    mid_low = lanes.gather(after(own_mid.astype(BF), *ffn_order[2:4]))
+    mid_low = lanes.gather(own_mid.astype(BF))
     d_hidden = dot(dy_low, full_down)
     gate_act = dot(mid_low, full_gate)
     up_act = dot(mid_low, full_up)
@@ -291,10 +291,10 @@
     own_d_middle, grad_gain_mid = norm_mid_back(own_d_mid)
     own_d_middle = own_dy + own_d_middle
 
-    d_att_low = after(lanes.gather(own_d_middle.astype(BF)), *ffn_pairs[:1])
+    d_att_low = lanes.gather(own_d_middle.astype(BF))
     d_gated = dot(d_att_low, out_mat)
     d_core, d_gate_lin, grad_head = gate_back(heads(d_gated))
-    d_core = after(d_core, *ffn_pairs[1:2])
+    d_core = after(d_core, *ffn_pairs[:1])
     d_queries, d_keys, d_values, d_decays = core_back(d_core)
     d_in_low = jnp.concatenate(
         [
@@ -309,7 +309,7 @@
     d_rank_low = dot(d_logit_low, rank_out).astype(BF)
     own_d_in = lanes.scatter(dot_rt(d_in_low, in_mat) + dot_rt(d_rank_low, rank_in))
     ffn_grads, ffn_shifts = rows.line_sum(ffn_sums)
-    grad_in = dot_t(normed_low, after(d_in_low, *ffn_pairs[2:], *ffn_shifts[:1])).astype(BF)
+    grad_in = dot_t(normed_low, after(d_in_low, *ffn_pairs[1:3])).astype(BF)
     grad_out = dot_t(d_att_low, gated_low).astype(BF)
 
     _, norm_in_back = jax.vjp(rms_gain, own_tokens, gain_in)

time: 349 us -> 343 us (0.983)
  waiting for transfers between devices: 168 us -> 130 us
  local copies, waits for them, and re-layouts: 59.8 us -> 90.5 us
  other arithmetic: 30.6 us -> 38 us
  starting transfers between devices: 58 us -> 51.8 us
    ppermute x16, waiting for transfers between devices: 82 us -> 64.8 us  [pair(): return lax.ppermute(array, 'dp', [(i, i ^ 1) for i in range(self.count)])]
    ppermute x12, waiting for transfers between devices: 65.2 us -> 52.2 us  [shift(): return lax.ppermute(array, 'dp', perm)]
    another operation x9, local copies, waits for them, and re-layouts: 0.2 us -> 11.5 us  [on_device(): small_rel = jnp.stack([piece[model_rows:] for piece in attn_pieces])]
    unnamed x234 -> x220, local copies, waits for them, and re-layouts: 30.5 us -> 39.8 us
    ppermute x30, waiting for transfers between devices: 20.4 us -> 12.8 us  [send(): lax.ppermute(array, 'mp', [(i, (i + step) % self.count) for i in range(se...]
    slice x7, local copies, waits for them, and re-layouts: 0.73 us -> 7.83 us  [on_device(): small_rel = jnp.stack([piece[model_rows:] for piece in attn_pieces])]
    ppermute x12, starting transfers between devices: 16.7 us -> 10 us  [shift(): return lax.ppermute(array, 'dp', perm)]
    concatenate x4, other arithmetic: 0.39 us -> 6.42 us  [attn_block(): return jnp.concatenate([mats, small_part[slot]])]
  transfers between devices with their start and end apart: 58 -> 58, of which waited for: 34 -> 24; matrix products, arithmetic and copies ran while one was open for 27% -> 39% of each run, Pallas kernels for 0% -> 0%
where the time goes in v3:
time: 343 us; the launch traced here: 339 us
  waiting for transfers between devices  130 us (38%)
  local copies, waits for them, and re-layouts  90.5 us (26%)
  starting transfers between devices  51.8 us (15%)
  other arithmetic  38 us (11%)
  matrix products  26.1 us (8%)
    ppermute x16, waiting for transfers between devices, pair(): return lax.ppermute(array, 'dp', [(i, i ^ 1) for i in range(self.count)])  64.8 us
    ppermute x12, waiting for transfers between devices, shift(): return lax.ppermute(array, 'dp', perm)  52.2 us
    unnamed x220, local copies, waits for them, and re-layouts  39.8 us
    ppermute x30, starting transfers between devices, send(): lax.ppermute(array, 'mp', [(i, (i + step) % self.count) for i in range(se...  30.2 us
    ppermute x30, waiting for transfers between devices, send(): lax.ppermute(array, 'mp', [(i, (i + step) % self.count) for i in range(se...  12.8 us
    ppermute x16, starting transfers between devices, pair(): return lax.ppermute(array, 'dp', [(i, i ^ 1) for i in range(self.count)])  11.5 us
    another operation x9, local copies, waits for them, and re-layouts, on_device(): small_rel = jnp.stack([piece[model_rows:] for piece in attn_pieces])  11.5 us
    ppermute x12, starting transfers between devices, shift(): return lax.ppermute(array, 'dp', perm)  10 us
  transfers between devices with their start and end apart: 58, of which 24 were waited for; matrix products, arithmetic and copies ran while one was open for 39% of the time, Pallas kernels for 0%

profile of v3, /device:TPU:13, one launch (start us, length us, event | category | flops | bytes accessed | tf_op | source)
XLA Modules:
  0.0 338.5 jit_solution(11946795287302340065)
XLA Ops:
  2.3 2.8 concatenate.115
  7.1 2.3 pad_maximum_fusion
  33.7 1.3 stack.134
  35.8 1.9 collective-permute-done.3
  38.3 1.3 stack.135
  40.4 1.3 slice.401
  41.7 1.3 stack.136
  43.3 12.1 %collective-permute-done.6 = bf16[136,1024]{1,0:T(8,128)(2,1)} collective-permute-done((bf16[136,1024]{1,0:T(8,128)(2,1)}, bf16[136,1024]{1,0:T(8,128)(2,1)}, u32[]{:S(2)}, u32[]{:S(2)}) %collective-permute-start.6) | collective-permute-done | bytes 278560 | tf_op jit(solution)/shard_map/ppermute | solution.py:92
  56.7 2.4 collective-permute-done.8
  61.0 1.3 slice.403
  62.3 1.3 stack.138
  65.0 1.3 stack.140
  67.4 1.3 slice.402
  68.7 1.3 stack.137
  71.8 1.3 stack.139
  73.7 1.3 stack.141
  79.4 1.4 reshape.498
  84.8 1.6 fusion.124
  89.2 1.6 fusion.38
  91.1 1.4 reshape.499
  96.9 3.4 %collective-permute-start.12 = (bf16[64,1024]{1,0:T(8,128)(2,1)S(1)}, bf16[64,1024]{1,0:T(8,128)(2,1)S(1)}, u32[]{:S(2)}, u32[]{:S(2)}) collective-permute-start(bf16[64,1024]{1,0:T(8,128)(2,1)S(1)} %get-tuple-element.155), channel_id=1, source_target_pairs={{0,3},{1,0},{2,1},{3,2},{4,7},{5,4},{6,5},{7,6},{8,11},{9,8},{10,9... | collective-permute-start | bytes 393224 | tf_op jit(solution)/shard_map/ppermute | solution.py:140
  102.1 2.0 constant_dynamic-update-slice_fusion.40
  104.1 2.0 constant_dynamic-update-slice_fusion.39
  106.1 1.7 slice.425
  114.5 2.5 collective-permute-start.15
  117.1 1.6 collective-permute-done.14
  118.7 1.3 collective-permute-done.15
  120.1 1.8 collective-permute-done.18
  122.8 2.0 constant_dynamic-update-slice_fusion.37
  124.7 8.7 %collective-permute-done.20 = bf16[3,128,704]{1,2,0:T(8,128)(2,1)S(1)} collective-permute-done((bf16[3,128,704]{1,2,0:T(8,128)(2,1)}, bf16[3,128,704]{1,2,0:T(8,128)(2,1)S(1)}, u32[]{:S(2)}, u32[]{:S(2)}) %collective-permute-start.20) | collective-permute-done | bytes 540704 | tf_op jit(solution)/shard_map/ppermute | solution.py:87
  134.4 1.9 constant_dynamic-update-slice_fusion.35
  136.3 8.8 %collective-permute-done.22 = bf16[3,128,704]{1,2,0:T(8,128)(2,1)S(1)} collective-permute-done((bf16[3,128,704]{1,2,0:T(8,128)(2,1)}, bf16[3,128,704]{1,2,0:T(8,128)(2,1)S(1)}, u32[]{:S(2)}, u32[]{:S(2)}) %collective-permute-start.22) | collective-permute-done | bytes 540704 | tf_op jit(solution)/shard_map/ppermute | solution.py:87
  145.9 2.1 fusion.11
  148.0 1.9 fusion.9
  154.4 1.8 collective-permute-start.23
  168.4 2.2 collective-permute-done.27
  172.7 1.3 fusion.15
  174.4 1.3 fusion.31
  177.8 2.2 add_convert_fusion.2
  186.9 1.7 convolution_dynamic-update-slice_fusion
  192.5 1.6 convolution_convert_fusion.6
  194.1 4.6 %collective-permute-done.43 = bf16[3,128,704]{1,2,0:T(8,128)(2,1)} collective-permute-done((bf16[3,128,704]{1,2,0:T(8,128)(2,1)}, bf16[3,128,704]{1,2,0:T(8,128)(2,1)}, u32[]{:S(2)}, u32[]{:S(2)}) %collective-permute-start.43) | collective-permute-done | bytes 540704 | tf_op jit(solution)/shard_map/ppermute | solution.py:87
  199.5 2.0 add_convert_fusion
  202.2 2.0 add_convert_fusion.1
  208.7 2.0 fusion.128
  212.1 1.9 collective-permute-start.44
  214.1 1.8 constant_dynamic-update-slice_fusion.85
  217.5 2.0 collective-permute-start.33
  220.5 1.9 pad_maximum_fusion.8
  222.3 1.9 pad_maximum_fusion.7
  224.2 1.7 pad_maximum_fusion.6
  228.0 2.2 collective-permute-start.56
  232.8 1.7 collective-permute-start.41
  234.5 2.3 collective-permute-done.40
  240.6 1.8 collective-permute-start.38
  242.4 1.4 collective-permute-done.37
  246.7 10.7 %collective-permute-done.52 = bf16[130,1024]{0,1:T(8,128)(2,1)S(1)} collective-permute-done((bf16[130,1024]{0,1:T(8,128)(2,1)S(1)}, bf16[130,1024]{0,1:T(8,128)(2,1)S(1)}, u32[]{:S(2)}, u32[]{:S(2)}) %collective-permute-start.52) | collective-permute-done | bytes 266272 | tf_op jit(solution)/shard_map/ppermute | solution.py:87
  257.4 11.2 %collective-permute-done.50 = bf16[130,1024]{0,1:T(8,128)(2,1)S(1)} collective-permute-done((bf16[130,1024]{0,1:T(8,128)(2,1)S(1)}, bf16[130,1024]{0,1:T(8,128)(2,1)S(1)}, u32[]{:S(2)}, u32[]{:S(2)}) %collective-permute-start.50) | collective-permute-done | bytes 266272 | tf_op jit(solution)/shard_map/ppermute | solution.py:87
  269.6 11.7 %collective-permute-done.48 = bf16[130,1024]{0,1:T(8,128)(2,1)S(1)} collective-permute-done((bf16[130,1024]{0,1:T(8,128)(2,1)S(1)}, bf16[130,1024]{0,1:T(8,128)(2,1)S(1)}, u32[]{:S(2)}, u32[]{:S(2)}) %collective-permute-start.48) | collective-permute-done | bytes 266272 | tf_op jit(solution)/shard_map/ppermute | solution.py:87
  282.6 2.1 collective-permute-start.51
  285.3 1.6 convert_add_fusion
  287.8 5.3 %collective-permute-done.47 = bf16[130,1024]{0,1:T(8,128)(2,1)S(1)} collective-permute-done((bf16[130,1024]{0,1:T(8,128)(2,1)S(1)}, bf16[130,1024]{0,1:T(8,128)(2,1)S(1)}, u32[]{:S(2)}, u32[]{:S(2)}) %collective-permute-start.47) | collective-permute-done | bytes 266272 | tf_op jit(solution)/shard_map/ppermute | solution.py:87
  293.7 32.2 %collective-permute-done.51 = bf16[130,1024]{0,1:T(8,128)(2,1)S(1)} collective-permute-done((bf16[130,1024]{0,1:T(8,128)(2,1)S(1)}, bf16[130,1024]{0,1:T(8,128)(2,1)S(1)}, u32[]{:S(2)}, u32[]{:S(2)}) %collective-permute-start.51) | collective-permute-done | bytes 266272 | tf_op jit(solution)/shard_map/ppermute | solution.py:92
  325.9 4.9 %collective-permute-done.49 = bf16[130,1024]{0,1:T(8,128)(2,1)S(1)} collective-permute-done((bf16[130,1024]{0,1:T(8,128)(2,1)S(1)}, bf16[130,1024]{0,1:T(8,128)(2,1)S(1)}, u32[]{:S(2)}, u32[]{:S(2)}) %collective-permute-start.49) | collective-permute-done | bytes 266272 | tf_op jit(solution)/shard_map/ppermute | solution.py:92
  (470 shorter events, 129.3 us)
Async XLA Ops:
  5.0 23.3 %collective-permute-start = (bf16[1,16,128]{2,1,0:T(8,128)(2,1)S(1)}, bf16[1,16,128]{2,1,0:T(8,128)(2,1)}, u32[]{:S(2)}, u32[]{:S(2)}) collective-permute-start(bf16[1,16,128]{2,1,0:T(8,128)(2,1)S(1)} %pad_bitcast_fusion), channel_id=1, source_target_pairs={{0,1},{1,2},{2,3},{3,0},{4,5},{5,6},{6,7},{7,4},{8,9},{9,10},{10,1... | collective-permute-start | bytes 12296 | tf_op jit(solution)/shard_map/ppermute | solution.py:140
  5.9 23.1 %collective-permute-start.1 = (bf16[1,16,128]{2,1,0:T(8,128)(2,1)S(1)}, bf16[1,16,128]{2,1,0:T(8,128)(2,1)S(1)}, u32[]{:S(2)}, u32[]{:S(2)}) collective-permute-start(bf16[1,16,128]{2,1,0:T(8,128)(2,1)S(1)} %pad_bitcast_fusion), channel_id=1, source_target_pairs={{0,2},{1,3},{2,0},{3,1},{4,6},{5,7},{6,4},{7,5},{8,10},{9,11},{10,... | collective-permute-start | bytes 12296 | tf_op jit(solution)/shard_map/ppermute | solution.py:140
  7.1 21.9 %collective-permute-start.2 = (bf16[1,16,128]{2,1,0:T(8,128)(2,1)S(1)}, bf16[1,16,128]{2,1,0:T(8,128)(2,1)S(1)}, u32[]{:S(2)}, u32[]{:S(2)}) collective-permute-start(bf16[1,16,128]{2,1,0:T(8,128)(2,1)S(1)} %pad_bitcast_fusion), channel_id=1, source_target_pairs={{0,3},{1,0},{2,1},{3,2},{4,7},{5,4},{6,5},{7,6},{8,11},{9,8},{10,9... | collective-permute-start | bytes 12296 | tf_op jit(solution)/shard_map/ppermute | solution.py:140
  9.4 91.0 %collective-permute-start.16 = (bf16[3,128,704]{1,2,0:T(8,128)(2,1)}, bf16[3,128,704]{1,2,0:T(8,128)(2,1)}, u32[]{:S(2)}, u32[]{:S(2)}) collective-permute-start(bf16[3,128,704]{1,2,0:T(8,128)(2,1)} %get-tuple-element.126), channel_id=1, source_target_pairs={{0,4},{4,0},{8,12},{12,8},{16,20},{20,16},{24,28},{28,24},{1,5},{5... | collective-permute-start | bytes 1622024 | tf_op jit(solution)/shard_map/ppermute | solution.py:87
  10.6 91.0 %collective-permute-start.17 = (bf16[3,128,704]{1,2,0:T(8,128)(2,1)}, bf16[3,128,704]{1,2,0:T(8,128)(2,1)}, u32[]{:S(2)}, u32[]{:S(2)}) collective-permute-start(bf16[3,128,704]{1,2,0:T(8,128)(2,1)} %get-tuple-element.126), channel_id=1, source_target_pairs={{0,8},{4,12},{8,16},{12,20},{16,24},{20,28},{24,0},{28,4},{1,9},{5... | collective-permute-start | bytes 1622024 | tf_op jit(solution)/shard_map/ppermute | solution.py:92
  26.5 56.3 %copy-start.5 = (bf16[256,1024]{1,0:T(8,128)(2,1)}, bf16[256,1024]{1,0:T(8,128)(2,1)S(1)}, u32[]{:S(2)}) copy-start(bf16[256,1024]{1,0:T(8,128)(2,1)S(1)} %constant_dynamic-update-slice_fusion.42) | copy-start | bytes 1572868
  30.4 7.3 %collective-permute-start.3 = (bf16[136,1024]{1,0:T(8,128)(2,1)}, bf16[136,1024]{1,0:T(8,128)(2,1)S(1)}, u32[]{:S(2)}, u32[]{:S(2)}) collective-permute-start(bf16[136,1024]{1,0:T(8,128)(2,1)} %pad_maximum_fusion.10), channel_id=1, source_target_pairs={{0,4},{4,0},{8,12},{12,8},{16,20},{20,16},{24,28},{28,24},{1,5},{5... | collective-permute-start | bytes 835592 | tf_op jit(solution)/shard_map/ppermute | solution.py:87
  31.4 9.0 %collective-permute-start.4 = (bf16[136,1024]{1,0:T(8,128)(2,1)}, bf16[136,1024]{1,0:T(8,128)(2,1)}, u32[]{:S(2)}, u32[]{:S(2)}) collective-permute-start(bf16[136,1024]{1,0:T(8,128)(2,1)} %pad_maximum_fusion.10), channel_id=1, source_target_pairs={{0,8},{4,12},{8,16},{12,20},{16,24},{20,28},{24,0},{28,4},{1,9},{5... | collective-permute-start | bytes 835592 | tf_op jit(solution)/shard_map/ppermute | solution.py:92
  32.7 22.7 %collective-permute-start.6 = (bf16[136,1024]{1,0:T(8,128)(2,1)}, bf16[136,1024]{1,0:T(8,128)(2,1)}, u32[]{:S(2)}, u32[]{:S(2)}) collective-permute-start(bf16[136,1024]{1,0:T(8,128)(2,1)} %pad_maximum_fusion.10), channel_id=1, source_target_pairs={{0,16},{4,20},{8,24},{12,28},{16,0},{20,4},{24,8},{28,12},{1,17},{... | collective-permute-start | bytes 835592 | tf_op jit(solution)/shard_map/ppermute | solution.py:92
  37.7 21.4 %collective-permute-start.8 = (bf16[136,1024]{1,0:T(8,128)(2,1)}, bf16[136,1024]{1,0:T(8,128)(2,1)}, u32[]{:S(2)}, u32[]{:S(2)}) collective-permute-start(bf16[136,1024]{1,0:T(8,128)(2,1)} %pad_maximum_fusion.10), channel_id=1, source_target_pairs={{0,24},{4,28},{8,0},{12,4},{16,8},{20,12},{24,16},{28,20},{1,25},{... | collective-permute-start | bytes 835592 | tf_op jit(solution)/shard_map/ppermute | solution.py:92
  43.1 24.2 %collective-permute-start.5 = (bf16[136,1024]{1,0:T(8,128)(2,1)}, bf16[136,1024]{1,0:T(8,128)(2,1)}, u32[]{:S(2)}, u32[]{:S(2)}) collective-permute-start(bf16[136,1024]{1,0:T(8,128)(2,1)} %collective-permute-done.4), channel_id=1, source_target_pairs={{0,4},{4,0},{8,12},{12,8},{16,20},{20,16},{24,28},{28,24},{1,5},{5... | collective-permute-start | bytes 835592 | tf_op jit(solution)/shard_map/ppermute | solution.py:87
  55.5 14.6 %collective-permute-start.7 = (bf16[136,1024]{1,0:T(8,128)(2,1)}, bf16[136,1024]{1,0:T(8,128)(2,1)}, u32[]{:S(2)}, u32[]{:S(2)}) collective-permute-start(bf16[136,1024]{1,0:T(8,128)(2,1)} %collective-permute-done.6), channel_id=1, source_target_pairs={{0,4},{4,0},{8,12},{12,8},{16,20},{20,16},{24,28},{28,24},{1,5},{5... | collective-permute-start | bytes 835592 | tf_op jit(solution)/shard_map/ppermute | solution.py:87
  59.1 14.1 %collective-permute-start.9 = (bf16[136,1024]{1,0:T(8,128)(2,1)}, bf16[136,1024]{1,0:T(8,128)(2,1)S(1)}, u32[]{:S(2)}, u32[]{:S(2)}) collective-permute-start(bf16[136,1024]{1,0:T(8,128)(2,1)} %collective-permute-done.8), channel_id=1, source_target_pairs={{0,4},{4,0},{8,12},{12,8},{16,20},{20,16},{24,28},{28,24},{1,5},{5... | collective-permute-start | bytes 835592 | tf_op jit(solution)/shard_map/ppermute | solution.py:87
  67.3 40.5 %collective-permute-start.19 = (bf16[3,128,704]{1,2,0:T(8,128)(2,1)}, bf16[3,128,704]{1,2,0:T(8,128)(2,1)}, u32[]{:S(2)}, u32[]{:S(2)}) collective-permute-start(bf16[3,128,704]{1,2,0:T(8,128)(2,1)} %get-tuple-element.126), channel_id=1, source_target_pairs={{0,16},{4,20},{8,24},{12,28},{16,0},{20,4},{24,8},{28,12},{1,17},{... | collective-permute-start | bytes 1622024 | tf_op jit(solution)/shard_map/ppermute | solution.py:92
  70.0 38.3 %collective-permute-start.21 = (bf16[3,128,704]{1,2,0:T(8,128)(2,1)}, bf16[3,128,704]{1,2,0:T(8,128)(2,1)}, u32[]{:S(2)}, u32[]{:S(2)}) collective-permute-start(bf16[3,128,704]{1,2,0:T(8,128)(2,1)} %get-tuple-element.126), channel_id=1, source_target_pairs={{0,24},{4,28},{8,0},{12,4},{16,8},{20,12},{24,16},{28,20},{1,25},{... | collective-permute-start | bytes 1622024 | tf_op jit(solution)/shard_map/ppermute | solution.py:92
  96.9 12.4 %collective-permute-start.12 = (bf16[64,1024]{1,0:T(8,128)(2,1)S(1)}, bf16[64,1024]{1,0:T(8,128)(2,1)S(1)}, u32[]{:S(2)}, u32[]{:S(2)}) collective-permute-start(bf16[64,1024]{1,0:T(8,128)(2,1)S(1)} %get-tuple-element.155), channel_id=1, source_target_pairs={{0,3},{1,0},{2,1},{3,2},{4,7},{5,4},{6,5},{7,6},{8,11},{9,8},{10,9... | collective-permute-start | bytes 393224 | tf_op jit(solution)/shard_map/ppermute | solution.py:140
  100.4 9.4 %collective-permute-start.11 = (bf16[64,1024]{1,0:T(8,128)(2,1)S(1)}, bf16[64,1024]{1,0:T(8,128)(2,1)S(1)}, u32[]{:S(2)}, u32[]{:S(2)}) collective-permute-start(bf16[64,1024]{1,0:T(8,128)(2,1)S(1)} %get-tuple-element.156), channel_id=1, source_target_pairs={{0,2},{1,3},{2,0},{3,1},{4,6},{5,7},{6,4},{7,5},{8,10},{9,11},{10,... | collective-permute-start | bytes 393224 | tf_op jit(solution)/shard_map/ppermute | solution.py:140
  101.6 8.2 %collective-permute-start.10 = (bf16[64,1024]{1,0:T(8,128)(2,1)S(1)}, bf16[64,1024]{1,0:T(8,128)(2,1)S(1)}, u32[]{:S(2)}, u32[]{:S(2)}) collective-permute-start(bf16[64,1024]{1,0:T(8,128)(2,1)S(1)} %get-tuple-element.154), channel_id=1, source_target_pairs={{0,1},{1,2},{2,3},{3,0},{4,5},{5,6},{6,7},{7,4},{8,9},{9,10},{10,1... | collective-permute-start | bytes 393224 | tf_op jit(solution)/shard_map/ppermute | solution.py:140
  107.8 14.1 %collective-permute-start.18 = (bf16[3,128,704]{1,2,0:T(8,128)(2,1)}, bf16[3,128,704]{1,2,0:T(8,128)(2,1)S(1)}, u32[]{:S(2)}, u32[]{:S(2)}) collective-permute-start(bf16[3,128,704]{1,2,0:T(8,128)(2,1)} %collective-permute-done.17), channel_id=1, source_target_pairs={{0,4},{4,0},{8,12},{12,8},{16,20},{20,16},{24,28},{28,24},{1,5},{5... | collective-permute-start | bytes 1622024 | tf_op jit(solution)/shard_map/ppermute | solution.py:87
  108.3 25.2 %collective-permute-start.20 = (bf16[3,128,704]{1,2,0:T(8,128)(2,1)}, bf16[3,128,704]{1,2,0:T(8,128)(2,1)S(1)}, u32[]{:S(2)}, u32[]{:S(2)}) collective-permute-start(bf16[3,128,704]{1,2,0:T(8,128)(2,1)} %collective-permute-done.19), channel_id=1, source_target_pairs={{0,4},{4,0},{8,12},{12,8},{16,20},{20,16},{24,28},{28,24},{1,5},{5... | collective-permute-start | bytes 1622024 | tf_op jit(solution)/shard_map/ppermute | solution.py:87
  109.3 35.8 %collective-permute-start.22 = (bf16[3,128,704]{1,2,0:T(8,128)(2,1)}, bf16[3,128,704]{1,2,0:T(8,128)(2,1)S(1)}, u32[]{:S(2)}, u32[]{:S(2)}) collective-permute-start(bf16[3,128,704]{1,2,0:T(8,128)(2,1)} %collective-permute-done.21), channel_id=1, source_target_pairs={{0,4},{4,0},{8,12},{12,8},{16,20},{20,16},{24,28},{28,24},{1,5},{5... | collective-permute-start | bytes 1622024 | tf_op jit(solution)/shard_map/ppermute | solution.py:87
  111.2 3.4 collective-permute-start.13
  112.2 6.5 %collective-permute-start.14 = (bf16[64,1024]{1,0:T(8,128)(2,1)S(1)}, bf16[64,1024]{1,0:T(8,128)(2,1)S(1)}, u32[]{:S(2)}, u32[]{:S(2)}) collective-permute-start(bf16[64,1024]{1,0:T(8,128)(2,1)S(1)} %get-tuple-element.79), channel_id=1, source_target_pairs={{0,2},{1,3},{2,0},{3,1},{4,6},{5,7},{6,4},{7,5},{8,10},{9,11},{10,... | collective-permute-start | bytes 393224 | tf_op jit(solution)/shard_map/ppermute | solution.py:140
  114.5 5.5 %collective-permute-start.15 = (bf16[64,1024]{1,0:T(8,128)(2,1)S(1)}, bf16[64,1024]{1,0:T(8,128)(2,1)S(1)}, u32[]{:S(2)}, u32[]{:S(2)}) collective-permute-start(bf16[64,1024]{1,0:T(8,128)(2,1)S(1)} %get-tuple-element.79), channel_id=1, source_target_pairs={{0,3},{1,0},{2,1},{3,2},{4,7},{5,4},{6,5},{7,6},{8,11},{9,8},{10,9... | collective-permute-start | bytes 393224 | tf_op jit(solution)/shard_map/ppermute | solution.py:140
  153.2 10.0 %collective-permute-start.25 = (bf16[64,1024]{1,0:T(8,128)(2,1)S(1)}, bf16[64,1024]{1,0:T(8,128)(2,1)S(1)}, u32[]{:S(2)}, u32[]{:S(2)}) collective-permute-start(bf16[64,1024]{1,0:T(8,128)(2,1)S(1)} %get-tuple-element.151), channel_id=1, source_target_pairs={{0,3},{1,0},{2,1},{3,2},{4,7},{5,4},{6,5},{7,6},{8,11},{9,8},{10,9... | collective-permute-start | bytes 393224 | tf_op jit(solution)/shard_map/ppermute | solution.py:140
  154.1 9.1 %collective-permute-start.24 = (bf16[64,1024]{1,0:T(8,128)(2,1)S(1)}, bf16[64,1024]{1,0:T(8,128)(2,1)S(1)}, u32[]{:S(2)}, u32[]{:S(2)}) collective-permute-start(bf16[64,1024]{1,0:T(8,128)(2,1)S(1)} %get-tuple-element.152), channel_id=1, source_target_pairs={{0,2},{1,3},{2,0},{3,1},{4,6},{5,7},{6,4},{7,5},{8,10},{9,11},{10,... | collective-permute-start | bytes 393224 | tf_op jit(solution)/shard_map/ppermute | solution.py:140
  154.4 8.8 %collective-permute-start.23 = (bf16[64,1024]{1,0:T(8,128)(2,1)S(1)}, bf16[64,1024]{1,0:T(8,128)(2,1)S(1)}, u32[]{:S(2)}, u32[]{:S(2)}) collective-permute-start(bf16[64,1024]{1,0:T(8,128)(2,1)S(1)} %get-tuple-element.150), channel_id=1, source_target_pairs={{0,1},{1,2},{2,3},{3,0},{4,5},{5,6},{6,7},{7,4},{8,9},{9,10},{10,1... | collective-permute-start | bytes 393224 | tf_op jit(solution)/shard_map/ppermute | solution.py:140
  160.9 16.9 %collective-permute-start.29 = (bf16[3,128,704]{1,2,0:T(8,128)(2,1)}, bf16[3,128,704]{1,2,0:T(8,128)(2,1)}, u32[]{:S(2)}, u32[]{:S(2)}) collective-permute-start(bf16[3,128,704]{1,2,0:T(8,128)(2,1)} %pad_maximum_fusion.1), channel_id=1, source_target_pairs={{0,4},{4,0},{8,12},{12,8},{16,20},{20,16},{24,28},{28,24},{1,5},{5... | collective-permute-start | bytes 1622024 | tf_op jit(solution)/shard_map/ppermute | solution.py:87
  162.2 39.3 %collective-permute-start.42 = (bf16[3,128,704]{1,2,0:T(8,128)(2,1)}, bf16[3,128,704]{1,2,0:T(8,128)(2,1)}, u32[]{:S(2)}, u32[]{:S(2)}) collective-permute-start(bf16[3,128,704]{1,2,0:T(8,128)(2,1)} %pad_maximum_fusion.2), channel_id=1, source_target_pairs={{0,4},{4,0},{8,12},{12,8},{16,20},{20,16},{24,28},{28,24},{1,5},{5... | collective-permute-start | bytes 1622024 | tf_op jit(solution)/shard_map/ppermute | solution.py:87
  163.6 4.3 %collective-permute-start.26 = (bf16[64,1024]{1,0:T(8,128)(2,1)S(1)}, bf16[64,1024]{1,0:T(8,128)(2,1)S(1)}, u32[]{:S(2)}, u32[]{:S(2)}) collective-permute-start(bf16[64,1024]{1,0:T(8,128)(2,1)S(1)} %get-tuple-element.76), channel_id=1, source_target_pairs={{0,1},{1,2},{2,3},{3,0},{4,5},{5,6},{6,7},{7,4},{8,9},{9,10},{10,1... | collective-permute-start | bytes 393224 | tf_op jit(solution)/shard_map/ppermute | solution.py:140
  165.1 33.6 %collective-permute-start.43 = (bf16[3,128,704]{1,2,0:T(8,128)(2,1)}, bf16[3,128,704]{1,2,0:T(8,128)(2,1)}, u32[]{:S(2)}, u32[]{:S(2)}) collective-permute-start(bf16[3,128,704]{1,2,0:T(8,128)(2,1)} %pad_maximum_fusion.3), channel_id=1, source_target_pairs={{0,4},{4,0},{8,12},{12,8},{16,20},{20,16},{24,28},{28,24},{1,5},{5... | collective-permute-start | bytes 1622024 | tf_op jit(solution)/shard_map/ppermute | solution.py:87
  165.6 5.0 %collective-permute-start.27 = (bf16[64,1024]{1,0:T(8,128)(2,1)S(1)}, bf16[64,1024]{1,0:T(8,128)(2,1)S(1)}, u32[]{:S(2)}, u32[]{:S(2)}) collective-permute-start(bf16[64,1024]{1,0:T(8,128)(2,1)S(1)} %get-tuple-element.76), channel_id=1, source_target_pairs={{0,2},{1,3},{2,0},{3,1},{4,6},{5,7},{6,4},{7,5},{8,10},{9,11},{10,... | collective-permute-start | bytes 393224 | tf_op jit(solution)/shard_map/ppermute | solution.py:140
  167.9 4.8 %collective-permute-start.28 = (bf16[64,1024]{1,0:T(8,128)(2,1)S(1)}, bf16[64,1024]{1,0:T(8,128)(2,1)S(1)}, u32[]{:S(2)}, u32[]{:S(2)}) collective-permute-start(bf16[64,1024]{1,0:T(8,128)(2,1)S(1)} %get-tuple-element.76), channel_id=1, source_target_pairs={{0,3},{1,0},{2,1},{3,2},{4,7},{5,4},{6,5},{7,6},{8,11},{9,8},{10,9... | collective-permute-start | bytes 393224 | tf_op jit(solution)/shard_map/ppermute | solution.py:140
  170.6 111.6 %collective-permute-start.54 = (bf16[3,128,704]{1,2,0:T(8,128)(2,1)}, bf16[3,128,704]{1,2,0:T(8,128)(2,1)}, u32[]{:S(2)}, u32[]{:S(2)}) collective-permute-start(bf16[3,128,704]{1,2,0:T(8,128)(2,1)} %pad_maximum_fusion.4), channel_id=1, source_target_pairs={{0,4},{4,0},{8,12},{12,8},{16,20},{20,16},{24,28},{28,24},{1,5},{5... | collective-permute-start | bytes 1622024 | tf_op jit(solution)/shard_map/ppermute | solution.py:87
  184.7 22.7 %collective-permute-start.32 = (bf16[64,1024]{1,0:T(8,128)(2,1)}, bf16[64,1024]{1,0:T(8,128)(2,1)}, u32[]{:S(2)}, u32[]{:S(2)}) collective-permute-start(bf16[64,1024]{1,0:T(8,128)(2,1)} %get-tuple-element.148), channel_id=1, source_target_pairs={{0,3},{1,0},{2,1},{3,2},{4,7},{5,4},{6,5},{7,6},{8,11},{9,8},{10,9... | collective-permute-start | bytes 393224 | tf_op jit(solution)/shard_map/ppermute | solution.py:140
  184.8 22.6 %collective-permute-start.31 = (bf16[64,1024]{1,0:T(8,128)(2,1)}, bf16[64,1024]{1,0:T(8,128)(2,1)}, u32[]{:S(2)}, u32[]{:S(2)}) collective-permute-start(bf16[64,1024]{1,0:T(8,128)(2,1)} %get-tuple-element.149), channel_id=1, source_target_pairs={{0,2},{1,3},{2,0},{3,1},{4,6},{5,7},{6,4},{7,5},{8,10},{9,11},{10,... | collective-permute-start | bytes 393224 | tf_op jit(solution)/shard_map/ppermute | solution.py:140
  198.6 8.8 %collective-permute-start.30 = (bf16[64,1024]{1,0:T(8,128)(2,1)}, bf16[64,1024]{1,0:T(8,128)(2,1)}, u32[]{:S(2)}, u32[]{:S(2)}) collective-permute-start(bf16[64,1024]{1,0:T(8,128)(2,1)} %get-tuple-element.147), channel_id=1, source_target_pairs={{0,1},{1,2},{2,3},{3,0},{4,5},{5,6},{6,7},{7,4},{8,9},{9,10},{10,1... | collective-permute-start | bytes 393224 | tf_op jit(solution)/shard_map/ppermute | solution.py:140
  201.5 81.1 %collective-permute-start.57 = (bf16[3,128,704]{1,2,0:T(8,128)(2,1)}, bf16[3,128,704]{1,2,0:T(8,128)(2,1)}, u32[]{:S(2)}, u32[]{:S(2)}) collective-permute-start(bf16[3,128,704]{1,2,0:T(8,128)(2,1)} %add_convert_fusion), channel_id=1, source_target_pairs={{0,8},{4,12},{8,16},{12,20},{16,24},{20,28},{24,0},{28,4},{1,9},{5... | collective-permute-start | bytes 1622024 | tf_op jit(solution)/shard_map/ppermute | solution.py:92
  211.2 5.4 %collective-permute-start.46 = (bf16[1,8,2048]{2,0,1:T(2,128)(2,1)S(1)}, bf16[1,8,2048]{2,0,1:T(2,128)(2,1)S(1)}, u32[]{:S(2)}, u32[]{:S(2)}) collective-permute-start(bf16[1,8,2048]{2,0,1:T(2,128)(2,1)S(1)} %get-tuple-element.171), channel_id=1, source_target_pairs={{0,3},{1,0},{2,1},{3,2},{4,7},{5,4},{6,5},{7,6},{8,11},{9,8},{10,9... | collective-permute-start | bytes 98312 | tf_op jit(solution)/shard_map/ppermute | solution.py:140
  211.4 5.3 %collective-permute-start.45 = (bf16[1,8,2048]{2,0,1:T(2,128)(2,1)S(1)}, bf16[1,8,2048]{2,0,1:T(2,128)(2,1)S(1)}, u32[]{:S(2)}, u32[]{:S(2)}) collective-permute-start(bf16[1,8,2048]{2,0,1:T(2,128)(2,1)S(1)} %get-tuple-element.170), channel_id=1, source_target_pairs={{0,2},{1,3},{2,0},{3,1},{4,6},{5,7},{6,4},{7,5},{8,10},{9,11},{10,... | collective-permute-start | bytes 98312 | tf_op jit(solution)/shard_map/ppermute | solution.py:140
  212.1 5.4 %collective-permute-start.44 = (bf16[1,8,2048]{2,0,1:T(2,128)(2,1)S(1)}, bf16[1,8,2048]{2,0,1:T(2,128)(2,1)S(1)}, u32[]{:S(2)}, u32[]{:S(2)}) collective-permute-start(bf16[1,8,2048]{2,0,1:T(2,128)(2,1)S(1)} %get-tuple-element.169), channel_id=1, source_target_pairs={{0,1},{1,2},{2,3},{3,0},{4,5},{5,6},{6,7},{7,4},{8,9},{9,10},{10,1... | collective-permute-start | bytes 98312 | tf_op jit(solution)/shard_map/ppermute | solution.py:140
  216.6 11.4 %collective-permute-start.35 = (bf16[64,1024]{1,0:T(8,128)(2,1)}, bf16[64,1024]{1,0:T(8,128)(2,1)}, u32[]{:S(2)}, u32[]{:S(2)}) collective-permute-start(bf16[64,1024]{1,0:T(8,128)(2,1)} %get-tuple-element.145), channel_id=1, source_target_pairs={{0,3},{1,0},{2,1},{3,2},{4,7},{5,4},{6,5},{7,6},{8,11},{9,8},{10,9... | collective-permute-start | bytes 393224 | tf_op jit(solution)/shard_map/ppermute | solution.py:140
  216.6 13.6 %collective-permute-start.34 = (bf16[64,1024]{1,0:T(8,128)(2,1)}, bf16[64,1024]{1,0:T(8,128)(2,1)}, u32[]{:S(2)}, u32[]{:S(2)}) collective-permute-start(bf16[64,1024]{1,0:T(8,128)(2,1)} %get-tuple-element.146), channel_id=1, source_target_pairs={{0,2},{1,3},{2,0},{3,1},{4,6},{5,7},{6,4},{7,5},{8,10},{9,11},{10,... | collective-permute-start | bytes 393224 | tf_op jit(solution)/shard_map/ppermute | solution.py:140
  217.5 13.0 %collective-permute-start.33 = (bf16[64,1024]{1,0:T(8,128)(2,1)}, bf16[64,1024]{1,0:T(8,128)(2,1)}, u32[]{:S(2)}, u32[]{:S(2)}) collective-permute-start(bf16[64,1024]{1,0:T(8,128)(2,1)} %get-tuple-element.144), channel_id=1, source_target_pairs={{0,1},{1,2},{2,3},{3,0},{4,5},{5,6},{6,7},{7,4},{8,9},{9,10},{10,1... | collective-permute-start | bytes 393224 | tf_op jit(solution)/shard_map/ppermute | solution.py:140
  228.0 56.7 %collective-permute-start.56 = (bf16[3,128,704]{1,2,0:T(8,128)(2,1)}, bf16[3,128,704]{1,2,0:T(8,128)(2,1)S(1)}, u32[]{:S(2)}, u32[]{:S(2)}) collective-permute-start(bf16[3,128,704]{1,2,0:T(8,128)(2,1)} %add_convert_fusion.1), channel_id=1, source_target_pairs={{0,16},{4,20},{8,24},{12,28},{16,0},{20,4},{24,8},{28,12},{1,17},{... | collective-permute-start | bytes 1622024 | tf_op jit(solution)/shard_map/ppermute | solution.py:92
  230.2 2.6 collective-permute-start.39
  230.5 6.3 %collective-permute-start.40 = (bf16[64,1024]{1,0:T(8,128)(2,1)}, bf16[64,1024]{1,0:T(8,128)(2,1)S(1)}, u32[]{:S(2)}, u32[]{:S(2)}) collective-permute-start(bf16[64,1024]{1,0:T(8,128)(2,1)} %get-tuple-element.71), channel_id=1, source_target_pairs={{0,2},{1,3},{2,0},{3,1},{4,6},{5,7},{6,4},{7,5},{8,10},{9,11},{10,... | collective-permute-start | bytes 393224 | tf_op jit(solution)/shard_map/ppermute | solution.py:140
  232.8 5.5 %collective-permute-start.41 = (bf16[64,1024]{1,0:T(8,128)(2,1)S(1)}, bf16[64,1024]{1,0:T(8,128)(2,1)S(1)}, u32[]{:S(2)}, u32[]{:S(2)}) collective-permute-start(bf16[64,1024]{1,0:T(8,128)(2,1)S(1)} %copy-done.44), channel_id=1, source_target_pairs={{0,3},{1,0},{2,1},{3,2},{4,7},{5,4},{6,5},{7,6},{8,11},{9,8},{10,9... | collective-permute-start | bytes 393224 | tf_op jit(solution)/shard_map/ppermute | solution.py:140
  236.8 3.7 %collective-permute-start.36 = (bf16[64,1024]{1,0:T(8,128)(2,1)S(1)}, bf16[64,1024]{1,0:T(8,128)(2,1)S(1)}, u32[]{:S(2)}, u32[]{:S(2)}) collective-permute-start(bf16[64,1024]{1,0:T(8,128)(2,1)S(1)} %get-tuple-element.74), channel_id=1, source_target_pairs={{0,1},{1,2},{2,3},{3,0},{4,5},{5,6},{6,7},{7,4},{8,9},{9,10},{10,1... | collective-permute-start | bytes 393224 | tf_op jit(solution)/shard_map/ppermute | solution.py:140
  238.3 5.5 %collective-permute-start.37 = (bf16[64,1024]{1,0:T(8,128)(2,1)S(1)}, bf16[64,1024]{1,0:T(8,128)(2,1)S(1)}, u32[]{:S(2)}, u32[]{:S(2)}) collective-permute-start(bf16[64,1024]{1,0:T(8,128)(2,1)S(1)} %get-tuple-element.74), channel_id=1, source_target_pairs={{0,2},{1,3},{2,0},{3,1},{4,6},{5,7},{6,4},{7,5},{8,10},{9,11},{10,... | collective-permute-start | bytes 393224 | tf_op jit(solution)/shard_map/ppermute | solution.py:140
  240.6 5.1 %collective-permute-start.38 = (bf16[64,1024]{1,0:T(8,128)(2,1)S(1)}, bf16[64,1024]{1,0:T(8,128)(2,1)S(1)}, u32[]{:S(2)}, u32[]{:S(2)}) collective-permute-start(bf16[64,1024]{1,0:T(8,128)(2,1)S(1)} %get-tuple-element.74), channel_id=1, source_target_pairs={{0,3},{1,0},{2,1},{3,2},{4,7},{5,4},{6,5},{7,6},{8,11},{9,8},{10,9... | collective-permute-start | bytes 393224 | tf_op jit(solution)/shard_map/ppermute | solution.py:140
  243.8 13.6 %collective-permute-start.52 = (bf16[130,1024]{0,1:T(8,128)(2,1)S(1)}, bf16[130,1024]{0,1:T(8,128)(2,1)S(1)}, u32[]{:S(2)}, u32[]{:S(2)}) collective-permute-start(bf16[130,1024]{0,1:T(8,128)(2,1)S(1)} %copy-done.32), channel_id=1, source_target_pairs={{0,4},{4,0},{8,12},{12,8},{16,20},{20,16},{24,28},{28,24},{1,5},{5... | collective-permute-start | bytes 798728 | tf_op jit(solution)/shard_map/ppermute | solution.py:87
  245.7 23.0 %collective-permute-start.50 = (bf16[130,1024]{0,1:T(8,128)(2,1)S(1)}, bf16[130,1024]{0,1:T(8,128)(2,1)S(1)}, u32[]{:S(2)}, u32[]{:S(2)}) collective-permute-start(bf16[130,1024]{0,1:T(8,128)(2,1)S(1)} %copy-done.31), channel_id=1, source_target_pairs={{0,4},{4,0},{8,12},{12,8},{16,20},{20,16},{24,28},{28,24},{1,5},{5... | collective-permute-start | bytes 798728 | tf_op jit(solution)/shard_map/ppermute | solution.py:87
  246.3 35.6 %copy-start.12 = (bf16[128,768]{0,1:T(8,128)(2,1)S(1)}, bf16[128,768]{0,1:T(8,128)(2,1)}, u32[]{:S(2)}) copy-start(bf16[128,768]{0,1:T(8,128)(2,1)} %get-tuple-element.88) | copy-start | bytes 589828
  246.3 35.6 %copy-start.36 = (bf16[128,256]{0,1:T(8,128)(2,1)S(1)}, bf16[128,256]{0,1:T(8,128)(2,1)}, u32[]{:S(2)}) copy-start(bf16[128,256]{0,1:T(8,128)(2,1)} %get-tuple-element.134) | copy-start | bytes 196612
  246.7 35.5 %copy-start.64 = (bf16[256,1024]{1,0:T(8,128)(2,1)}, bf16[256,1024]{1,0:T(8,128)(2,1)S(1)}, u32[]{:S(2)}) copy-start(bf16[256,1024]{1,0:T(8,128)(2,1)S(1)} %constant_dynamic-update-slice_fusion.50) | copy-start | bytes 1572868
  257.4 27.8 %collective-permute-start.55 = (bf16[3,128,704]{1,2,0:T(8,128)(2,1)S(1)}, bf16[3,128,704]{1,2,0:T(8,128)(2,1)S(1)}, u32[]{:S(2)}, u32[]{:S(2)}) collective-permute-start(bf16[3,128,704]{1,2,0:T(8,128)(2,1)S(1)} %copy-done.29), channel_id=1, source_target_pairs={{0,24},{4,28},{8,0},{12,4},{16,8},{20,12},{24,16},{28,20},{1,25},{... | collective-permute-start | bytes 1622024 | tf_op jit(solution)/shard_map/ppermute | solution.py:92
  268.6 12.7 %collective-permute-start.48 = (bf16[130,1024]{0,1:T(8,128)(2,1)S(1)}, bf16[130,1024]{0,1:T(8,128)(2,1)S(1)}, u32[]{:S(2)}, u32[]{:S(2)}) collective-permute-start(bf16[130,1024]{0,1:T(8,128)(2,1)S(1)} %copy-done.30), channel_id=1, source_target_pairs={{0,4},{4,0},{8,12},{12,8},{16,20},{20,16},{24,28},{28,24},{1,5},{5... | collective-permute-start | bytes 798728 | tf_op jit(solution)/shard_map/ppermute | solution.py:87
  281.4 11.8 %collective-permute-start.47 = (bf16[130,1024]{0,1:T(8,128)(2,1)S(1)}, bf16[130,1024]{0,1:T(8,128)(2,1)S(1)}, u32[]{:S(2)}, u32[]{:S(2)}) collective-permute-start(bf16[130,1024]{0,1:T(8,128)(2,1)S(1)} %pad_maximum_fusion.5), channel_id=1, source_target_pairs={{0,4},{4,0},{8,12},{12,8},{16,20},{20,16},{24,28},{28,24},{1,5},{5... | collective-permute-start | bytes 798728 | tf_op jit(solution)/shard_map/ppermute | solution.py:87
  282.2 11.6 %collective-permute-start.53 = (bf16[130,1024]{0,1:T(8,128)(2,1)S(1)}, bf16[130,1024]{0,1:T(8,128)(2,1)S(1)}, u32[]{:S(2)}, u32[]{:S(2)}) collective-permute-start(bf16[130,1024]{0,1:T(8,128)(2,1)S(1)} %add_convert_fusion.3), channel_id=1, source_target_pairs={{0,8},{4,12},{8,16},{12,20},{16,24},{20,28},{24,0},{28,4},{1,9},{5... | collective-permute-start | bytes 798728 | tf_op jit(solution)/shard_map/ppermute | solution.py:92
  282.6 43.3 %collective-permute-start.51 = (bf16[130,1024]{0,1:T(8,128)(2,1)S(1)}, bf16[130,1024]{0,1:T(8,128)(2,1)S(1)}, u32[]{:S(2)}, u32[]{:S(2)}) collective-permute-start(bf16[130,1024]{0,1:T(8,128)(2,1)S(1)} %add_convert_fusion.4), channel_id=1, source_target_pairs={{0,16},{4,20},{8,24},{12,28},{16,0},{20,4},{24,8},{28,12},{1,17},{... | collective-permute-start | bytes 798728 | tf_op jit(solution)/shard_map/ppermute | solution.py:92
  284.7 46.1 %collective-permute-start.49 = (bf16[130,1024]{0,1:T(8,128)(2,1)S(1)}, bf16[130,1024]{0,1:T(8,128)(2,1)S(1)}, u32[]{:S(2)}, u32[]{:S(2)}) collective-permute-start(bf16[130,1024]{0,1:T(8,128)(2,1)S(1)} %add_convert_fusion.5), channel_id=1, source_target_pairs={{0,24},{4,28},{8,0},{12,4},{16,8},{20,12},{24,16},{28,20},{1,25},{... | collective-permute-start | bytes 798728 | tf_op jit(solution)/shard_map/ppermute | solution.py:92
  285.3 45.6 %copy-start.11 = (bf16[128,768]{0,1:T(8,128)(2,1)S(1)}, bf16[128,768]{0,1:T(8,128)(2,1)}, u32[]{:S(2)}) copy-start(bf16[128,768]{0,1:T(8,128)(2,1)} %get-tuple-element.82) | copy-start | bytes 589828
  285.3 45.6 %copy-start.35 = (bf16[128,256]{0,1:T(8,128)(2,1)S(1)}, bf16[128,256]{0,1:T(8,128)(2,1)}, u32[]{:S(2)}) copy-start(bf16[128,256]{0,1:T(8,128)(2,1)} %get-tuple-element.128) | copy-start | bytes 196612
  (68 other events, 611.7 us)
